TPU v7x, 256 devices: a whole 4x4x8 slice. The times are simulated.
256 devices in a mesh: ctx: 64 (over x, z, core), head: 4 (over y).
Axes of the slice: x: 4, y: 4, z: 8, core: 2. Of those that a mesh axis runs over, the one named last changes fastest.
Arguments:
- tokens: bfloat16 [65536, 1024], P('ctx'), may hold values from -90 to 90
- w_qkv: bfloat16 [3, 1024, 1024], P(None, None, 'head'), may hold values from -0.1875 to 0.1875
- w_out: bfloat16 [1024, 1024], replicated, may hold values from -0.1875 to 0.1875
- conv_weight: float32 [16, 33], P('head'), may hold values from -0.6 to 0.6
Outputs:
- layer_out: bfloat16 [65536, 1024], P(('ctx', 'head'))
All inputs are finite; a program needn't handle non-finite values. Where the computation divides by a largest or mean magnitude, that divisor is 1e-20 or more.
Results may differ from a plain program's by a relative error of at most 0.017.
The roundings to bfloat16 on the way count: a program that leaves them out, or rounds other values in their place, can miss the bound.
Values may be sent and summed in bfloat16 or wider, within the bound.
No kernel may reach another device: no remote copies, remote signals or barrier semaphores. Data moves between devices by JAX's collectives and lax.ppermute only.
A program may use at most 192 MiB of HBM per device.

v0:
```python
import jax
import jax.numpy as jnp
from jax import lax
from jax.sharding import PartitionSpec as P

M = 256
NS_STEPS = 6


def padded_2(x, sides, width):
    for axis, dim in sides:
        devices, length = (lax.axis_size(axis), x.shape[dim])
        up = [(i, (i + 1) % devices) for i in range(devices - 1)]
        down = [(j, i) for i, j in up]
        last = lax.slice_in_dim(x, length - width, length, axis=dim)
        first = lax.slice_in_dim(x, 0, width, axis=dim)
        before = lax.ppermute(last, axis, up)
        after = lax.ppermute(first, axis, down)
        x = jnp.concatenate([before, x, after], axis=dim)
    return x


def softmax_rows(scores):
    top = jnp.max(scores, axis=-1, keepdims=True)
    expo = jnp.exp(scores - top)
    return expo / jnp.sum(expo, axis=-1, keepdims=True)


def newton_pinv(kernel):
    col_sum = jnp.max(jnp.sum(jnp.abs(kernel), axis=1), axis=-1)
    row_sum = jnp.max(jnp.sum(jnp.abs(kernel), axis=2), axis=-1)
    approx = jnp.swapaxes(kernel, 1, 2) / (col_sum * row_sum)[:, None, None]
    ident = jnp.eye(kernel.shape[1], dtype=jnp.float32)[None]
    high = lax.Precision.HIGHEST
    for step in range(NS_STEPS):
        prod = jnp.einsum("hij,hjk->hik", kernel, approx, precision=high)
        inner = 7.0 * ident - prod
        inner = 15.0 * ident - jnp.einsum("hij,hjk->hik", prod, inner, precision=high)
        inner = 13.0 * ident - jnp.einsum("hij,hjk->hik", prod, inner, precision=high)
        approx = 0.25 * jnp.einsum("hij,hjk->hik", approx, inner, precision=high)
    return approx


def body(tokens, w_qkv, w_out, conv_weight):
    n_rows = tokens.shape[0]
    width = w_qkv.shape[2]
    local_heads = conv_weight.shape[0]
    head_size = width // local_heads
    scale = 1.0 / head_size**0.5
    proj = jnp.einsum("nd,cde->cne", tokens, w_qkv, preferred_element_type=jnp.float32).astype(
        jnp.bfloat16
    )
    query, key, value = (proj[0], proj[1], proj[2])
    land_dev = M // lax.axis_size("ctx")
    seg = n_rows // land_dev
    land_local = (
        jnp.sum(proj[:2].reshape(2, land_dev, seg, width), axis=2, dtype=jnp.float32) / seg
    ).astype(jnp.bfloat16)
    land_q, land_k = (
        lax.all_gather(land_local[0], "ctx", axis=0, tiled=True),
        lax.all_gather(land_local[1], "ctx", axis=0, tiled=True),
    )
    q_heads = query.reshape(n_rows, local_heads, head_size)
    k_heads = key.reshape(n_rows, local_heads, head_size)
    v_heads = value.reshape(n_rows, local_heads, head_size)
    lq_heads = land_q.reshape(M, local_heads, head_size)
    lk_heads = land_k.reshape(M, local_heads, head_size)
    kernel_a = softmax_rows(
        scale * jnp.einsum("mhe,khe->hmk", lq_heads, lk_heads, preferred_element_type=jnp.float32)
    )
    kernel_f = softmax_rows(
        scale * jnp.einsum("nhe,mhe->hnm", q_heads, lk_heads, preferred_element_type=jnp.float32)
    ).astype(jnp.bfloat16)
    scores_b = scale * jnp.einsum(
        "mhe,nhe->hmn", lq_heads, k_heads, preferred_element_type=jnp.float32
    )
    row_max = lax.pmax(jnp.max(scores_b, axis=2), "ctx")
    expo = jnp.exp(scores_b - row_max[..., None])
    total = jnp.sum(expo, axis=2)
    summed = jnp.einsum(
        "hmn,nhe->hme", expo.astype(jnp.bfloat16), v_heads, preferred_element_type=jnp.float32
    )
    total, summed = lax.psum((total, summed), "ctx")
    kernel_bv = summed / total[..., None]
    pinv_a = newton_pinv(kernel_a)
    mid = jnp.einsum("hmk,hke->hme", pinv_a, kernel_bv, precision=lax.Precision.HIGHEST).astype(
        jnp.bfloat16
    )
    attended = jnp.einsum("hnm,hme->nhe", kernel_f, mid, preferred_element_type=jnp.float32)
    half = conv_weight.shape[1] // 2
    padded = padded_2(value, (("ctx", 0),), half)
    padded = padded.reshape(n_rows + 2 * half, local_heads, head_size)
    conv = jnp.zeros((n_rows, local_heads, head_size), jnp.float32)
    for tap in range(conv_weight.shape[1]):
        conv = conv + conv_weight[:, tap][None, :, None] * padded[tap : tap + n_rows].astype(
            jnp.float32
        )
    head_out = (attended + conv).astype(jnp.bfloat16).reshape(n_rows, width)
    regrouped = lax.all_to_all(head_out, "head", split_axis=0, concat_axis=1, tiled=True)
    result = jnp.dot(regrouped, w_out, preferred_element_type=jnp.float32)
    return result.astype(jnp.bfloat16)


def solution(mesh):
    placed = (P("ctx", None), P(None, None, "head"), P(), P("head", None))
    return jax.shard_map(
        body, mesh=mesh, in_specs=placed, out_specs=P(("ctx", "head"), None), check_vma=False
    )
```

profile of v0, /device:TPU:8, one launch (start us, length us, event | category | flops | bytes accessed | tf_op | source)
XLA Modules:
  0.0 503.8 jit_solution(11014507252556465605)
XLA Ops:
  8.1 3.2 fusion.30
  14.2 3.4 reshape.182
  17.6 2.2 reduce_sum.54
  20.0 47.3 %all-gather = bf16[1,256,256]{2,0,1:T(2,128)(2,1)S(1)} all-gather(bf16[1,4,256]{2,0,1:T(2,128)(2,1)S(1)} %copy.46), channel_id=2, replica_groups=mesh['ctx'=64,'head'=4] {'ctx'}, dimensions={1}, use_global_device_ids=true | all-gather | bytes 133120 | tf_op jit(solution)/shard_map/all_gather | solution.py:60
  67.4 2.7 multiply_reduce_fusion
  70.1 126.6 %pmax.7 = f32[4,256]{1,0:T(4,128)S(1)} all-reduce(f32[4,256]{1,0:T(4,128)S(1)} %get-tuple-element.82), channel_id=1, replica_groups=mesh['ctx'=64,'head'=4] {'ctx'}, use_global_device_ids=true, to_apply=%region_8.0 | all-reduce | flops 1024 | bytes 8192 | tf_op jit(solution)/shard_map/pmax | solution.py:77
  196.7 3.8 fusion.7
  203.4 3.7 collective-permute-start
  207.1 40.9 %all-gather.1 = bf16[1,256,256]{2,0,1:T(2,128)(2,1)S(1)} all-gather(bf16[1,4,256]{2,0,1:T(2,128)(2,1)S(1)} %copy.48), channel_id=3, replica_groups=mesh['ctx'=64,'head'=4] {'ctx'}, dimensions={1}, use_global_device_ids=true | all-gather | bytes 133120 | tf_op jit(solution)/shard_map/all_gather | solution.py:61
  250.2 3.1 fusion.3
  255.4 4.8 online-softmax
  260.3 2.9 fusion.35
  264.4 2.9 convolution_multiply_fusion.5
  267.2 4.7 online-softmax.1
  271.9 2.9 fusion.38
  278.1 5.0 online-softmax.2
  283.2 2.9 fusion.41
  289.4 4.6 online-softmax.3
  294.0 2.9 fusion.44
  300.2 4.6 online-softmax.4
  304.9 2.9 fusion.47
  311.0 4.8 online-softmax.5
  315.9 2.9 fusion.50
  321.1 3.4 fusion.138
  325.4 126.8 %psum.15 = f32[4,256]{1,0:T(4,128)S(1)} all-reduce(f32[4,256]{1,0:T(4,128)S(1)} %fusion.3), channel_id=1, replica_groups=mesh['ctx'=64,'head'=4] {'ctx'}, use_global_device_ids=true, to_apply=%region_11.0 | all-reduce | flops 1024 | bytes 8192 | tf_op jit(solution)/shard_map/psum | solution.py:83
  452.1 5.2 %fusion.89 = (bf16[1024,256]{0,1:T(8,128)(2,1)}, bf16[1024,256]{0,1:T(8,128)(2,1)}, bf16[1024,256]{0,1:T(8,128)(2,1)}, bf16[1024,256]{0,1:T(8,128)(2,1)}, bf16[1...) fusion(bf16[16,256]{0,1:T(8,128)(2,1)} %collective-permute-done, ...), kind=kLoop, calls=%fused_computation.155 | loop fusion | flops 9437184 | bytes 5251072 | tf_op jit(solution)/shard_map/concatenate | solution.py:19
  457.3 4.3 fusion.98
  461.7 4.2 fusion.104
  465.9 3.6 fusion.113
  471.7 10.2 %fusion.55 = bf16[1024,4,64]{0,2,1:T(8,128)(2,1)S(1)} fusion(bf16[4,256,64]{1,2,0:T(8,128)(2,1)S(1)} %convolution_convert_fusion.1, f32[4,1024,256]{1,2,0:T(8,128)} %get-tuple-element.85, f32[4,1024]{1,0:T(4,128)S(1)} %get-tuple-element.84, bf16[1024,4,64]{0,2,1:T(8,128)(2,1)} %bitcast.170, bf16[1024,4,64]{0,2,1:T(8,128)(2,1)} %bitcast.171, ...), kind=kOutput, calls=%fused_computation.84 | convolution fusion | flops 162529280 | bytes 22168080 | tf_op jit(solution)/shard_map/hnm,hme->nhe/dot_general | solution.py:89
  482.3 11.3 %all_to_all.19 = bf16[4,256,256]{1,2,0:T(8,128)(2,1)S(1)} all-to-all(bf16[4,256,256]{1,2,0:T(8,128)(2,1)S(1)} %copy.54), channel_id=1, replica_groups=mesh['ctx'=64,'head'=4] {'head'}, dimensions={0} | all-to-all | bytes 1048576 | tf_op jit(solution)/shard_map/all_to_all | solution.py:99
  493.7 3.1 convolution_convert_fusion
  (78 shorter events, 32.2 us)
Async XLA Ops:
  6.5 1.6 copy-start
  6.5 463.0 %all-reduce.2.cloned.1.call-start = ((), (), s32[]{:S(2)}) async-start(), calls=%async_computation.1 | async-start | bytes 524288 | tf_op jit(solution)/shard_map/psum | solution.py:83
  11.4 1.8 copy-start.13
  14.2 182.5 %copy-start.15 = (bf16[1,1024,256]{1,2,0:T(8,128)(2,1)}, bf16[1,1024,256]{1,2,0:T(8,128)(2,1)S(1)}, u32[]{:S(2)}) copy-start(bf16[1,1024,256]{1,2,0:T(8,128)(2,1)S(1)} %get-tuple-element.44) | copy-start | bytes 1572868
  202.1 250.0 %collective-permute-start.1 = (bf16[16,256]{0,1:T(8,128)(2,1)}, bf16[16,256]{0,1:T(8,128)(2,1)}, u32[]{:S(2)}, u32[]{:S(2)}) collective-permute-start(bf16[16,256]{0,1:T(8,128)(2,1)} %get-tuple-element.41), channel_id=1, source_target_pairs={{4,0},{8,4},{12,8},{16,12},{20,16},{24,20},{28,24},{32,28},{36,32}... | collective-permute-start | bytes 24584 | tf_op jit(solution)/shard_map/ppermute | solution.py:18
  203.4 258.3 %collective-permute-start = (bf16[16,256]{0,1:T(8,128)(2,1)}, bf16[16,256]{0,1:T(8,128)(2,1)}, u32[]{:S(2)}, u32[]{:S(2)}) collective-permute-start(bf16[16,256]{0,1:T(8,128)(2,1)} %get-tuple-element.40), channel_id=1, source_target_pairs={{0,4},{4,8},{8,12},{12,16},{16,20},{20,24},{24,28},{28,32},{32,36}... | collective-permute-start | bytes 24584 | tf_op jit(solution)/shard_map/ppermute | solution.py:17
  260.3 2.9 copy-start.3
  271.9 2.9 copy-start.4
  271.9 4.1 copy-start.9
  283.1 2.9 copy-start.5
  283.1 4.1 copy-start.10
  294.0 2.9 copy-start.6
  294.0 4.1 copy-start.11
  304.8 2.9 copy-start.7
  304.8 4.1 copy-start.12
  315.9 2.9 copy-start.2
  315.9 4.1 copy-start.8
  318.7 2.4 copy-start.17
  319.9 4.6 copy-start.14
  465.9 5.8 %copy-start.16 = (bf16[1,1024,256]{1,2,0:T(8,128)(2,1)S(1)}, bf16[1,1024,256]{1,2,0:T(8,128)(2,1)}, u32[]{:S(2)}) copy-start(bf16[1,1024,256]{1,2,0:T(8,128)(2,1)} %copy-done.15) | copy-start | bytes 1572868
  471.7 25.1 %copy-start.1 = (bf16[1024,1024]{1,0:T(8,128)(2,1)S(1)}, bf16[1024,1024]{1,0:T(8,128)(2,1)}, u32[]{:S(2)}) copy-start(bf16[1024,1024]{1,0:T(8,128)(2,1)} %param.4) | copy-start | bytes 6291460
Sparse Core Ops, SparseCore 0:
  200.6 168.4 all-reduce.1
where the time goes:
time: 513 us; the launch traced here: 504 us
  blocking collectives  353 us (69%)
  matrix products  67.3 us (13%)
  Pallas kernels  28.6 us (6%)
  other arithmetic  25.3 us (5%)
  between operations  14 us (3%)
  local copies, waits for them, and re-layouts  10.7 us (2%)
    psum x1, blocking collectives, body(): total, summed = lax.psum((total, summed), 'ctx')  127 us
    pmax x1, blocking collectives, body(): row_max = lax.pmax(jnp.max(scores_b, axis=2), 'ctx')  127 us
    all_gather x1, blocking collectives, body(): lax.all_gather(land_local[0], 'ctx', axis=0, tiled=True)  47.3 us
    all_gather x1, blocking collectives, body(): lax.all_gather(land_local[1], 'ctx', axis=0, tiled=True)  40.9 us
    unnamed x6, Pallas kernels  28.6 us
    dot_general x12, matrix products, newton_pinv(): jnp.einsum('hij,hjk->hik', prod, inner, precision=high)  24.2 us
    concatenate x4, other arithmetic, padded_2(): x = jnp.concatenate([before, x, after], axis=dim)  17.4 us
    dot_general x6, matrix products, newton_pinv(): approx = 0.25 * jnp.einsum('hij,hjk->hik', approx, inner, precision=high)  12.6 us
  transfers between devices with their start and end apart: 3, of which 0 were waited for; matrix products, arithmetic and copies ran while one was open for 13% of the time, Pallas kernels for 6%

commit v1 on v0

v1 whole, which is shorter than its diff:
```python
import jax
import jax.numpy as jnp
from jax import lax
from jax.experimental import pallas as pl
from jax.experimental.pallas import tpu as pltpu
from jax.sharding import PartitionSpec as P

M = 256
NS_STEPS = 6
TAPS = 33
HALF = 16
HEADS = 4
HD = 64
WIDTH = 256
CHIPS = 32
ROWS = 1024
SCALE = 0.125
f32 = jnp.float32
bf16 = jnp.bfloat16
INTERPRET = False
VMEM = pl.BlockSpec(memory_space=pltpu.VMEM)
SMEM = pl.BlockSpec(memory_space=pltpu.SMEM)
HBM = pl.BlockSpec(memory_space=pltpu.HBM)
MIB = 1 << 20


def call(kernel, outs, scratch=(), specs=None, n_in=1, flops=0, moved=0, exps=0, limit=24):
    single = not isinstance(outs, (list, tuple))
    return pl.pallas_call(
        kernel,
        out_shape=outs,
        in_specs=specs or [VMEM] * n_in,
        out_specs=VMEM if single else [VMEM] * len(outs),
        scratch_shapes=list(scratch),
        compiler_params=pltpu.CompilerParams(vmem_limit_bytes=limit * MIB),
        cost_estimate=pl.CostEstimate(flops=flops, bytes_accessed=moved, transcendentals=exps),
        interpret=INTERPRET,
    )


def shaped(shape, dtype):
    return jax.ShapeDtypeStruct(shape, dtype)


def dot_nn(a, b):
    return lax.dot_general(a, b, (((1,), (0,)), ((), ())), preferred_element_type=f32)


def dot_nt(a, b):
    return lax.dot_general(a, b, (((1,), (1,)), ((), ())), preferred_element_type=f32)


def split_2(x):
    high = x.astype(bf16)
    return high, (x - high.astype(f32)).astype(bf16)


def split_3(x):
    high = x.astype(bf16)
    rest = x - high.astype(f32)
    middle = rest.astype(bf16)
    return high, middle, (rest - middle.astype(f32)).astype(bf16)


def dot_wide(a, b, transposed=False):
    (ah, al), (bh, bl) = a, b
    left = jnp.concatenate([ah, ah, al], axis=1)
    if transposed:
        return dot_nt(left, jnp.concatenate([bh, bl, bh], axis=1))
    return dot_nn(left, jnp.concatenate([bh, bl, bh], axis=0))


def head_mask(head):
    lane = lax.broadcasted_iota(jnp.int32, (M, WIDTH), 1)
    return (lane >= head * HD) & (lane < (head + 1) * HD)


def landmarks_kernel(tok_hbm, w_hbm, out_ref, tok_ref, w_ref, rows_ref, sems):
    seg = ROWS // 4
    copies = [
        pltpu.make_async_copy(
            tok_hbm.at[s * seg : (s + 1) * seg, :], tok_ref.at[s * seg : (s + 1) * seg, :], sems.at[s]
        )
        for s in range(4)
    ] + [pltpu.make_async_copy(w_hbm.at[c], w_ref.at[c], sems.at[4 + c]) for c in range(2)]
    for copy in copies:
        copy.start()
    sums = []
    for s in range(4):
        copies[s].wait()
        sums.append(
            jnp.sum(tok_ref[s * seg : (s + 1) * seg, :].astype(f32), axis=0, keepdims=True)
        )
    means = jnp.concatenate(sums, axis=0) * (1.0 / seg)
    high, middle, low = split_3(means)
    stacked = jnp.concatenate(
        [high.astype(f32), middle.astype(f32), low.astype(f32), jnp.zeros_like(means)], axis=0
    ).astype(bf16)
    for kind in range(2):
        copies[4 + kind].wait()
        product = dot_nn(stacked, w_ref[kind])
        land = product[0:4] + product[4:8] + product[8:12]
        for half in range(2):
            rows_ref[pl.ds(2 * kind + half, 4, stride=4), :] = land[:, half * 128 : half * 128 + 128]
    out_ref[...] = jnp.broadcast_to(rows_ref[...].astype(bf16)[None], out_ref.shape)


def project_kernel(
    core_ref, tok_hbm, w_hbm, q_ref, k_ref, vt_ref, near_ref, far_ref, tok_ref, w_ref, sems
):
    seg = ROWS // 4
    copies = [pltpu.make_async_copy(w_hbm.at[c], w_ref.at[c], sems.at[c]) for c in range(3)]
    copies += [
        pltpu.make_async_copy(
            tok_hbm.at[s * seg : (s + 1) * seg, :], tok_ref.at[s * seg : (s + 1) * seg, :], sems.at[3 + s]
        )
        for s in range(4)
    ]
    for copy in copies:
        copy.start()
    for copy in copies[:3]:
        copy.wait()
    edges = []
    for s in range(4):
        copies[3 + s].wait()
        rows = slice(s * seg, (s + 1) * seg)
        tok = tok_ref[rows, :]
        q_ref[rows, :] = dot_nn(tok, w_ref[0]).astype(bf16)
        k_ref[rows, :] = dot_nn(tok, w_ref[1]).astype(bf16)
        value = dot_nn(tok, w_ref[2]).astype(bf16)
        vt_ref[:, rows] = value.T
        edges.append(value)
    first = edges[0][:HALF].astype(f32)
    last = edges[3][seg - HALF :].astype(f32)
    is_first = core_ref[0] == 0
    near_ref[...] = jnp.where(is_first, last, first).astype(bf16)
    far_ref[...] = jnp.where(is_first, first, last).astype(bf16)


def scores_kernel(
    core_ref, own_ref, other_ref, k_ref, vt_ref, lq_ref, lk_ref, keep_ref, send_ref, land_rows, acc, level
):
    core = core_ref[0]
    count = CHIPS * 16
    land_rows[pl.ds(core * count, count), :] = own_ref[...].astype(f32).reshape(count, 128)
    land_rows[pl.ds((1 - core) * count, count), :] = other_ref[...].astype(f32).reshape(count, 128)
    picked = [land_rows[pl.ds(j, M, stride=4), :] for j in range(4)]
    lq = jnp.concatenate(picked[:2], axis=1)
    lk = jnp.concatenate(picked[2:], axis=1)
    lq_ref[...] = lq.astype(bf16)
    lk_ref[...] = lk.astype(bf16)
    key = k_ref[...]
    level[...] = jnp.zeros(level.shape, f32)
    for head in range(HEADS):
        rows = slice(head * HD, (head + 1) * HD)
        own = jnp.where(head_mask(head), lq, 0.0).astype(bf16)
        scores = dot_nt(key, own)
        top = jnp.max(scores, axis=0, keepdims=True)
        expo = jnp.exp((scores - top) * SCALE)
        total = jnp.sum(expo, axis=0, keepdims=True)
        acc[rows, :] = dot_nn(vt_ref[rows, :], expo.astype(bf16)) / total
        at = 8 * (head // 2) + head % 2
        level[at : at + 1, :] = top * SCALE + jnp.log(total)
    for ref, side in ((keep_ref, core), (send_ref, 1 - core)):
        ref[0:128, :] = acc[pl.ds(pl.multiple_of(side * 128, 128), 128), :]
        ref[128:136, :] = level[pl.ds(pl.multiple_of(side * 8, 8), 8), :]


def combine_kernel(keep_ref, other_ref, out_ref, acc_low, acc_high, out_rows):
    acc_rows = (acc_low, acc_high)
    span = CHIPS // 2 * 16
    for head in range(2):
        rows = slice(head * HD, (head + 1) * HD)
        level_a = keep_ref[128 + head : 129 + head, :]
        level_b = other_ref[128 + head : 129 + head, :]
        top = jnp.maximum(level_a, level_b)
        weight_a = jnp.exp(level_a - top)
        weight_b = jnp.exp(level_b - top)
        total = weight_a + weight_b
        mean = keep_ref[rows, :] * (weight_a / total) + other_ref[rows, :] * (weight_b / total)
        pieces = split_3(top + jnp.log(total))
        for half in range(2):
            lanes = slice(half * 128, half * 128 + 128)
            acc_rows[half][rows, :] = mean[:, lanes]
            for c in range(3):
                out_rows[pl.ds(head * span + half * 8 + 4 + c, 16, stride=16), :] = jnp.broadcast_to(
                    pieces[c][:, lanes].astype(f32), (16, 128)
                )
            out_rows[pl.ds(head * span + half * 8 + 7, 16, stride=16), :] = jnp.zeros((16, 128), f32)
    for half in range(2):
        for r in range(4):
            out_rows[pl.ds(half * 8 + r, CHIPS, stride=16), :] = acc_rows[half][
                pl.ds(r, CHIPS, stride=4), :
            ]
    out_ref[...] = out_rows[...].reshape(CHIPS, 16, 128).astype(bf16)


def pinv_kernel(head_ref, lq_ref, lk_ref, w_ref):
    own = jnp.where(head_mask(head_ref[0]), lq_ref[...].astype(f32), 0.0).astype(bf16)
    scores = dot_nt(own, lk_ref[...]) * SCALE
    expo = jnp.exp(scores - jnp.max(scores, axis=1, keepdims=True))
    kernel = expo / jnp.sum(expo, axis=1, keepdims=True)
    col_sum = jnp.max(jnp.sum(kernel, axis=0, keepdims=True))
    row_sum = jnp.max(jnp.sum(kernel, axis=1, keepdims=True))
    approx = kernel / (col_sum * row_sum)
    diagonal = lax.broadcasted_iota(jnp.int32, (M, M), 0) == lax.broadcasted_iota(jnp.int32, (M, M), 1)
    ident = jnp.where(diagonal, 1.0, 0.0)
    prod = dot_wide(split_2(approx), split_2(kernel), transposed=True)
    for step in range(NS_STEPS):
        parts = split_2(prod)
        square = dot_wide(parts, parts)
        last = step == NS_STEPS - 1
        right = 7.0 * ident - prod
        if not last:
            right = jnp.concatenate([right, 7.0 * prod - square], axis=1)
        both = dot_wide(split_2(square), split_2(right))
        factor = 0.25 * (13.0 * ident - 15.0 * prod + both[:, :M])
        if not last:
            prod = 0.25 * (13.0 * prod - 15.0 * square + both[:, M:])
        approx = dot_wide(split_2(factor), split_2(approx))
    w_ref[...] = approx


def middle_kernel(parts_ref, w_ref, out_ref, part_rows, out_rows):
    part_rows[...] = parts_ref[...].astype(f32).reshape(CHIPS * 16, 128)
    halves = []
    for half in range(2):
        rows = [part_rows[pl.ds(half * 8 + r, CHIPS, stride=16), :] for r in range(7)]
        level = (rows[4] + rows[5]) + rows[6]
        weight = jnp.exp(level - jnp.max(level, axis=0, keepdims=True))
        weight = weight / jnp.sum(weight, axis=0, keepdims=True)
        halves.append(
            jnp.concatenate(
                [jnp.sum(weight * rows[r], axis=0, keepdims=True) for r in range(4)]
                + [jnp.zeros((4, 128), f32)],
                axis=0,
            )
        )
    bv = jnp.concatenate(halves, axis=1)
    mid = dot_wide(split_2(bv), split_2(w_ref[...]))[0:4]
    for half in range(2):
        out_rows[pl.ds(half, 4, stride=2), :] = mid[:, half * 128 : half * 128 + 128]
    out_ref[...] = jnp.broadcast_to(out_rows[...].astype(bf16)[None], out_ref.shape)


def token_kernel(lk_ref, q_ref, out_ref):
    query = q_ref[...]
    lk = lk_ref[...].astype(f32)
    for head in range(HEADS):
        own = jnp.where(head_mask(head), lk, 0.0).astype(bf16)
        scores = dot_nt(own, query)
        expo = jnp.exp((scores - jnp.max(scores, axis=0, keepdims=True)) * SCALE)
        out_ref[head] = (expo / jnp.sum(expo, axis=0, keepdims=True)).astype(bf16)


def conv_kernel(core_ref, vt_ref, near_ref, far_ref, cw_ref, out_ref):
    blocks = ROWS // 128
    is_first = core_ref[0] == 0
    near = near_ref[...].astype(f32)
    far = far_ref[...].astype(f32)
    empty = jnp.zeros((128 - HALF, WIDTH), f32)
    before = jnp.concatenate([empty, jnp.where(is_first, far, near)], axis=0).T.astype(bf16)
    after = jnp.concatenate([jnp.where(is_first, near, far), empty], axis=0).T.astype(bf16)
    for head in range(HEADS):
        taps = jnp.concatenate([cw_ref[head : head + 1, :], jnp.zeros((1, 384 - TAPS), f32)], axis=1)
        band = pltpu.roll(
            jnp.broadcast_to(taps, (128, 384)), 128 - HALF, 1, stride=1, stride_axis=0
        )
        high, low = split_2(band)
        rows = slice(head * HD, (head + 1) * HD)
        pieces = [before[rows, :]]
        pieces += [vt_ref[rows, b * 128 : b * 128 + 128] for b in range(blocks)]
        pieces += [after[rows, :]]
        windows = jnp.concatenate(
            [jnp.concatenate(pieces[b : b + 3] * 2, axis=1) for b in range(blocks)], axis=0
        )
        out = dot_nt(windows, jnp.concatenate([high, low], axis=1))
        for b in range(blocks):
            out_ref[rows, b * 128 : b * 128 + 128] = out[b * HD : (b + 1) * HD, :]


def attend_kernel(core_ref, own_ref, other_ref, kf_ref, conv_ref, out_ref, mid_rows):
    core = core_ref[0]
    count = CHIPS * 8
    mid_rows[pl.ds(core * count, count), :] = own_ref[...].astype(f32).reshape(count, 128)
    mid_rows[pl.ds((1 - core) * count, count), :] = other_ref[...].astype(f32).reshape(count, 128)
    mid = jnp.concatenate(
        [mid_rows[pl.ds(half, M, stride=2), :] for half in range(2)], axis=1
    ).astype(bf16)
    outs = []
    for head in range(HEADS):
        rows = slice(head * HD, (head + 1) * HD)
        outs.append((dot_nn(mid[rows, :], kf_ref[head]) + conv_ref[rows, :]).astype(bf16))
    out = jnp.concatenate(outs, axis=0).T
    out_ref[...] = out.reshape(out_ref.shape)


def output_kernel(x_ref, w_ref, out_ref):
    groups = x_ref.shape[0]
    joined = jnp.concatenate([x_ref[g] for g in range(groups)], axis=1)
    out_ref[...] = dot_nn(joined, w_ref[...]).astype(bf16)


def body(tokens, w_qkv, w_out, conv_weight):
    groups = lax.axis_size("head")
    same_core = [[2 * chip + core for chip in range(CHIPS)] for core in range(2)]
    swap = [(i, i ^ 1) for i in range(2 * CHIPS)]
    onward = [(2 * chip + 1, 2 * chip + 2) for chip in range(CHIPS - 1)]
    onward += [(b, a) for a, b in onward]
    place = lax.axis_index("ctx").astype(jnp.int32)
    core = (place % 2).reshape(1)
    head_id = (2 * (place % 2) + place // CHIPS).reshape(1)

    def exchange(x):
        return lax.all_to_all(x, "ctx", 0, 0, tiled=True, axis_index_groups=same_core)

    own = call(
        landmarks_kernel,
        shaped((CHIPS, 16, 128), bf16),
        [
            pltpu.VMEM((ROWS, 1024), bf16),
            pltpu.VMEM((2, 1024, WIDTH), bf16),
            pltpu.VMEM((16, 128), f32),
            pltpu.SemaphoreType.DMA((6,)),
        ],
        specs=[HBM, HBM],
        flops=2 * 16 * 1024 * 512,
        moved=3 * MIB,
    )(tokens, w_qkv)
    land = exchange(own)
    land_other = lax.ppermute(land, "ctx", swap)
    query, key, value_t, near, far = call(
        project_kernel,
        [
            shaped((ROWS, WIDTH), bf16),
            shaped((ROWS, WIDTH), bf16),
            shaped((WIDTH, ROWS), bf16),
            shaped((HALF, WIDTH), bf16),
            shaped((HALF, WIDTH), bf16),
        ],
        [
            pltpu.VMEM((ROWS, 1024), bf16),
            pltpu.VMEM((3, 1024, WIDTH), bf16),
            pltpu.SemaphoreType.DMA((7,)),
        ],
        specs=[SMEM, HBM, HBM],
        flops=2 * 1024 * 1024 * 768,
        moved=6 * MIB,
    )(core, tokens, w_qkv)
    near = lax.ppermute(near, "ctx", swap)
    far = lax.ppermute(far, "ctx", onward)
    land_q, land_k, keep, send = call(
        scores_kernel,
        [
            shaped((M, WIDTH), bf16),
            shaped((M, WIDTH), bf16),
            shaped((136, M), f32),
            shaped((136, M), f32),
        ],
        [pltpu.VMEM((CHIPS * 32, 128), f32), pltpu.VMEM((M, M), f32), pltpu.VMEM((16, M), f32)],
        specs=[SMEM] + [VMEM] * 4,
        flops=4 * 4 * 1024 * 256 * 256,
        moved=2 * MIB,
        exps=MIB,
    )(core, land, land_other, key, value_t)
    received = lax.ppermute(send, "ctx", swap)
    parts = call(
        combine_kernel,
        shaped((CHIPS, 16, 128), bf16),
        [pltpu.VMEM((128, 128), f32), pltpu.VMEM((128, 128), f32), pltpu.VMEM((CHIPS * 16, 128), f32)],
        n_in=2,
        flops=MIB,
        moved=MIB // 2,
    )(keep, received)
    gathered = exchange(parts)
    inverse = call(
        pinv_kernel,
        shaped((M, M), f32),
        specs=[SMEM, VMEM, VMEM],
        flops=24 * 3 * 2 * 256**3,
        moved=MIB // 2,
        exps=65536,
    )(head_id, land_q, land_k)
    mid_own = call(
        middle_kernel,
        shaped((CHIPS, 8, 128), bf16),
        [pltpu.VMEM((CHIPS * 16, 128), f32), pltpu.VMEM((8, 128), f32)],
        n_in=2,
        flops=6 * 8 * 256 * 256,
        moved=MIB // 2,
    )(gathered, inverse)
    mids = exchange(mid_own)
    mids_other = lax.ppermute(mids, "ctx", swap)
    kernel_f = call(
        token_kernel,
        shaped((HEADS, M, ROWS), bf16),
        n_in=2,
        flops=4 * 2 * 1024 * 256 * 256,
        moved=3 * MIB,
        exps=MIB,
    )(land_k, query)
    conv = call(
        conv_kernel,
        shaped((WIDTH, ROWS), f32),
        specs=[SMEM] + [VMEM] * 4,
        flops=2 * 512 * 768 * 512,
        moved=2 * MIB,
    )(core, value_t, near, far, conv_weight)
    head_out = call(
        attend_kernel,
        shaped((groups, ROWS // groups, WIDTH), bf16),
        [pltpu.VMEM((CHIPS * 16, 128), f32)],
        specs=[SMEM] + [VMEM] * 4,
        flops=4 * 2 * 64 * 256 * 1024,
        moved=4 * MIB,
    )(core, mids, mids_other, kernel_f, conv)
    regrouped = lax.all_to_all(head_out, "head", 0, 0, tiled=True)
    return call(
        output_kernel,
        shaped((ROWS // groups, w_out.shape[1]), bf16),
        n_in=2,
        flops=2 * 256 * 1024 * 1024,
        moved=3 * MIB,
    )(regrouped, w_out)


def solution(mesh):
    placed = (P("ctx", None), P(None, None, "head"), P(), P("head", None))
    return jax.shard_map(
        body, mesh=mesh, in_specs=placed, out_specs=P(("ctx", "head"), None), check_vma=False
    )
```

time: 513 us -> 87 us (0.17)
  the two profiles are of different devices: /device:TPU:8 before, /device:TPU:2 now
where the time goes in v1:
time: 87 us; the launch traced here: 85.3 us
  starting transfers between devices  27.1 us (31%)
  Pallas kernels  20 us (23%)
  waiting for transfers between devices  19 us (22%)
  blocking collectives  14.5 us (17%)
  local copies, waits for them, and re-layouts  4.42 us (5%)
    all_to_all x3, starting transfers between devices, exchange(): lax.all_to_all(x, 'ctx', 0, 0, tiled=True, axis_index_groups=same_core)  21.8 us
    all_to_all x3, waiting for transfers between devices, exchange(): lax.all_to_all(x, 'ctx', 0, 0, tiled=True, axis_index_groups=same_core)  18 us
    all_to_all x1, blocking collectives, body(): regrouped = lax.all_to_all(head_out, 'head', 0, 0, tiled=True)  14.5 us
    pallas_call x1, Pallas kernels, body(): call(pinv_kernel, shaped((M, M), f32), specs=[SMEM, VMEM, VMEM], flops=24...  5.06 us
    ppermute x1, starting transfers between devices, body(): far = lax.ppermute(far, 'ctx', onward)  4.66 us
    unnamed x12, local copies, waits for them, and re-layouts  4.42 us
    pallas_call x1, Pallas kernels, body(): call(project_kernel, [shaped((ROWS, WIDTH), bf16), shaped((ROWS, WIDTH),...  3.34 us
    pallas_call x1, Pallas kernels, body(): call(scores_kernel, [shaped((M, WIDTH), bf16), shaped((M, WIDTH), bf16),...  2.95 us
  transfers between devices with their start and end apart: 8, of which 4 were waited for; matrix products, arithmetic and copies ran while one was open for 0% of the time, Pallas kernels for 13%

profile of v1, /device:TPU:2, one launch (start us, length us, event | category | flops | bytes accessed | tf_op | source)
XLA Modules:
  0.0 85.3 jit_solution(10879579655600481248)
XLA Ops:
  0.0 1.6 %copy-done.1 = bf16[1024,1024]{1,0:T(8,128)(2,1)S(1)} copy-done((bf16[1024,1024]{1,0:T(8,128)(2,1)S(1)}, bf16[1024,1024]{1,0:T(8,128)(2,1)}, u32[]{:S(2)}) %copy-start.1) | copy-done | bytes 2097176
  1.6 1.4 %copy-done.3 = bf16[3,1024,256]{2,1,0:T(8,128)(2,1)S(1)} copy-done((bf16[3,1024,256]{2,1,0:T(8,128)(2,1)S(1)}, bf16[3,1024,256]{2,1,0:T(8,128)(2,1)}, u32[]{:S(2)}) %copy-start.3) | copy-done | bytes 1572888
  3.0 1.9 %shard_map.46 = bf16[32,16,128]{2,1,0:T(8,128)(2,1)} custom-call(bf16[1024,1024]{1,0:T(8,128)(2,1)S(1)} %copy-done.1, bf16[3,1024,256]{2,1,0:T(8,128)(2,1)S(1)} %copy-done.3), custom_call_target="tpu_custom_call" | custom-call | flops 16777216 | bytes 3145728 | tf_op jit(solution)/shard_map/pallas_call | solution.py:317
  4.9 11.6 %all-to-all-start = ((bf16[32,16,128]{2,1,0:T(8,128)(2,1)}), bf16[32,16,128]{2,1,0:T(8,128)(2,1)S(1)}, u32[]{:S(2)}, u32[]{:S(2)}) async-start(bf16[32,16,128]{2,1,0:T(8,128)(2,1)} %shard_map.46), calls=%async_computation | async-start | bytes 262144 | tf_op jit(solution)/shard_map/all_to_all | solution.py:315
  16.5 9.1 %all-to-all-done.own_ref = bf16[32,16,128]{2,1,0:T(8,128)(2,1)S(1)} async-done(((bf16[32,16,128]{2,1,0:T(8,128)(2,1)}), bf16[32,16,128]{2,1,0:T(8,128)(2,1)S(1)}, u32[]{:S(2)}, u32[]{:S(2)}) %all-to-all-start) | async-done | bytes 131104 | tf_op jit(solution)/shard_map/all_to_all | solution.py:315
  25.6 0.0 collective-permute-start
  25.6 1.4 %copy-done.4 = bf16[3,1024,256]{2,1,0:T(8,128)(2,1)S(1)} copy-done((bf16[3,1024,256]{2,1,0:T(8,128)(2,1)S(1)}, bf16[3,1024,256]{2,1,0:T(8,128)(2,1)}, u32[]{:S(2)}) %copy-start.4) | copy-done | bytes 1572888
  27.0 3.3 %shard_map.47 = (bf16[1024,256]{1,0:T(8,128)(2,1)S(1)}, bf16[1024,256]{1,0:T(8,128)(2,1)S(1)}, bf16[256,1024]{1,0:T(8,128)(2,1)S(1)}, bf16[16,256]{1,0:T(8,128)(2,1)S(1)}, bf16[16,256]{1,0:T(8,128)(2,1)S(1)}) custom-call(s32[1]{0:T(128)} %bitcast.core_ref, bf16[1024,1024]{1,0:T(8,128)(2,1)S(1)} %copy-done.2, bf16[3,1024,256]{2,1,0:T(8,128)(2,1)S(1)} %copy-done.4), custom_call_target="tpu_custom_call" | custom-call | flops 1610612736 | bytes 6291456 | tf_op jit(solution)/shard_map/pallas_call | solution.py:332
  30.4 0.0 collective-permute-done.other_ref
  30.4 3.0 %shard_map.48 = (bf16[256,256]{1,0:T(8,128)(2,1)S(1)}, bf16[256,256]{1,0:T(8,128)(2,1)S(1)}, f32[136,256]{1,0:T(8,128)S(1)}, f32[136,256]{1,0:T(8,128)S(1)}) custom-call(s32[1]{0:T(128)} %bitcast.core_ref, bf16[32,16,128]{2,1,0:T(8,128)(2,1)S(1)} %all-to-all-done.own_ref, bf16[32,16,128]{2,1,0:T(8,128)(2,1)S(1)} %collective-permute-done.other_ref, ...), custom_call_target="tpu_custom_call" | custom-call | flops 1073741824 | bytes 2097152 | tf_op jit(solution)/shard_map/pallas_call | solution.py:352
  33.4 0.6 collective-permute-start.1
  34.0 1.0 %collective-permute-done.1.other_ref = f32[136,256]{1,0:T(8,128)S(1)} collective-permute-done((f32[136,256]{1,0:T(8,128)S(1)}, f32[136,256]{1,0:T(8,128)S(1)}, u32[]{:S(2)}, u32[]{:S(2)}) %collective-permute-start.1) | collective-permute-done | bytes 139296 | tf_op jit(solution)/shard_map/ppermute | solution.py:366
  35.0 0.8 shard_map.49
  35.7 5.0 %all-to-all-start.1 = ((bf16[32,16,128]{2,1,0:T(8,128)(2,1)}), bf16[32,16,128]{2,1,0:T(8,128)(2,1)S(1)}, u32[]{:S(2)}, u32[]{:S(2)}) async-start(bf16[32,16,128]{2,1,0:T(8,128)(2,1)} %shard_map.49), calls=%async_computation.1 | async-start | bytes 262144 | tf_op jit(solution)/shard_map/all_to_all | solution.py:315
  40.8 0.0 copy-start.5
  40.8 5.1 %shard_map.50.w_ref = f32[256,256]{1,0:T(8,128)S(1)} custom-call(s32[1]{0:T(128)} %bitcast.1.head_ref, bf16[256,256]{1,0:T(8,128)(2,1)S(1)} %get-tuple-element.18.lq_ref, bf16[256,256]{1,0:T(8,128)(2,1)S(1)} %get-tuple-element.19.lk_ref), custom_call_target="tpu_custom_call" | custom-call | flops 2415919104 | bytes 524288 | tf_op jit(solution)/shard_map/pallas_call | solution.py:376
  45.8 4.8 %all-to-all-done.1.parts_ref = bf16[32,16,128]{2,1,0:T(8,128)(2,1)S(1)} async-done(((bf16[32,16,128]{2,1,0:T(8,128)(2,1)}), bf16[32,16,128]{2,1,0:T(8,128)(2,1)S(1)}, u32[]{:S(2)}, u32[]{:S(2)}) %all-to-all-start.1) | async-done | bytes 131104 | tf_op jit(solution)/shard_map/all_to_all | solution.py:315
  50.6 0.9 %shard_map.51 = bf16[32,8,128]{2,1,0:T(8,128)(2,1)} custom-call(bf16[32,16,128]{2,1,0:T(8,128)(2,1)S(1)} %all-to-all-done.1.parts_ref, f32[256,256]{1,0:T(8,128)S(1)} %shard_map.50.w_ref), custom_call_target="tpu_custom_call" | custom-call | flops 3145728 | bytes 524288 | tf_op jit(solution)/shard_map/pallas_call | solution.py:384
  51.6 5.1 %all-to-all-start.2 = ((bf16[32,8,128]{2,1,0:T(8,128)(2,1)}), bf16[32,8,128]{2,1,0:T(8,128)(2,1)S(1)}, u32[]{:S(2)}, u32[]{:S(2)}) async-start(bf16[32,8,128]{2,1,0:T(8,128)(2,1)} %shard_map.51), calls=%async_computation.2 | async-start | bytes 131072 | tf_op jit(solution)/shard_map/all_to_all | solution.py:315
  56.7 0.1 collective-permute-start.3
  56.8 4.7 %collective-permute-start.4 = (bf16[16,256]{1,0:T(8,128)(2,1)S(1)}, bf16[16,256]{1,0:T(8,128)(2,1)S(1)}, u32[]{:S(2)}, u32[]{:S(2)}) collective-permute-start(bf16[16,256]{1,0:T(8,128)(2,1)S(1)} %get-tuple-element.22), channel_id=1, source_target_pairs={{4,8},{12,16},{20,24},{28,32},{36,40},{44,48},{52,56},{60,64},{68,... | collective-permute-start | bytes 24584 | tf_op jit(solution)/shard_map/ppermute | solution.py:351
  61.5 4.1 %all-to-all-done.2.own_ref = bf16[32,8,128]{2,1,0:T(8,128)(2,1)S(1)} async-done(((bf16[32,8,128]{2,1,0:T(8,128)(2,1)}), bf16[32,8,128]{2,1,0:T(8,128)(2,1)S(1)}, u32[]{:S(2)}, u32[]{:S(2)}) %all-to-all-start.2) | async-done | bytes 65568 | tf_op jit(solution)/shard_map/all_to_all | solution.py:315
  65.6 0.0 collective-permute-start.2
  65.6 0.0 collective-permute-done.3.near_ref
  65.6 0.0 collective-permute-done.4.far_ref
  65.7 1.1 %shard_map.53.conv_ref = f32[256,1024]{1,0:T(8,128)S(1)} custom-call(s32[1]{0:T(128)} %bitcast.core_ref, bf16[256,1024]{1,0:T(8,128)(2,1)S(1)} %get-tuple-element.15.vt_ref, bf16[16,256]{1,0:T(8,128)(2,1)S(1)} %collective-permute-done.3.near_ref, bf16[16,256]{1,0:T(8,128)(2,1)S(1)} %collective-permute-done.4.far_ref, f32[4,33]{1,0:T(4,128)S(1)} %copy-done.5), custom_call_target="tpu_custom_call" | custom-call | flops 402653184 | bytes 2097152 | tf_op jit(solution)/shard_map/pallas_call | solution.py:402
  66.7 1.9 %shard_map.52.kf_ref = bf16[4,256,1024]{2,1,0:T(8,128)(2,1)S(1)} custom-call(bf16[256,256]{1,0:T(8,128)(2,1)S(1)} %get-tuple-element.19.lk_ref, bf16[1024,256]{1,0:T(8,128)(2,1)S(1)} %get-tuple-element.20.q_ref), custom_call_target="tpu_custom_call" | custom-call | flops 536870912 | bytes 3145728 | tf_op jit(solution)/shard_map/pallas_call | solution.py:394
  68.6 0.0 copy-start
  68.6 0.0 collective-permute-done.2.other_ref
  68.6 0.6 shard_map.54
  69.2 14.5 %all_to_all.20.x_ref = bf16[4,256,256]{2,1,0:T(8,128)(2,1)S(1)} all-to-all(bf16[4,256,256]{2,1,0:T(8,128)(2,1)S(1)} %shard_map.54), channel_id=1, replica_groups=mesh['ctx'=64,'head'=4] {'head'}, dimensions={0} | all-to-all | bytes 1048576 | tf_op jit(solution)/shard_map/all_to_all | solution.py:417
  83.8 1.5 %shard_map.55 = bf16[256,1024]{1,0:T(8,128)(2,1)} custom-call(bf16[4,256,256]{2,1,0:T(8,128)(2,1)S(1)} %all_to_all.20.x_ref, bf16[1024,1024]{1,0:T(8,128)(2,1)S(1)} %copy-done), custom_call_target="tpu_custom_call" | custom-call | flops 536870912 | bytes 3145728 | tf_op jit(solution)/shard_map/pallas_call | solution.py:418
  (7 shorter events, 0.0 us)
Async XLA Ops:
  0.0 1.6 %copy-start.1 = (bf16[1024,1024]{1,0:T(8,128)(2,1)S(1)}, bf16[1024,1024]{1,0:T(8,128)(2,1)}, u32[]{:S(2)}) copy-start(bf16[1024,1024]{1,0:T(8,128)(2,1)} %tok_hbm.3) | copy-start | bytes 6291460
  1.6 1.4 %copy-start.3 = (bf16[3,1024,256]{2,1,0:T(8,128)(2,1)S(1)}, bf16[3,1024,256]{2,1,0:T(8,128)(2,1)}, u32[]{:S(2)}) copy-start(bf16[3,1024,256]{2,1,0:T(8,128)(2,1)} %w_hbm.3) | copy-start | bytes 4718596
  3.0 22.6 %copy-start.2 = (bf16[1024,1024]{1,0:T(8,128)(2,1)S(1)}, bf16[1024,1024]{1,0:T(8,128)(2,1)}, u32[]{:S(2)}) copy-start(bf16[1024,1024]{1,0:T(8,128)(2,1)} %tok_hbm.3) | copy-start | bytes 6291460
  4.9 20.7 %all-to-all-start = ((bf16[32,16,128]{2,1,0:T(8,128)(2,1)}), bf16[32,16,128]{2,1,0:T(8,128)(2,1)S(1)}, u32[]{:S(2)}, u32[]{:S(2)}) async-start(bf16[32,16,128]{2,1,0:T(8,128)(2,1)} %shard_map.46), calls=%async_computation | async-start | bytes 262144 | tf_op jit(solution)/shard_map/all_to_all | solution.py:315
  25.6 4.8 %collective-permute-start = (bf16[32,16,128]{2,1,0:T(8,128)(2,1)S(1)}, bf16[32,16,128]{2,1,0:T(8,128)(2,1)S(1)}, u32[]{:S(2)}, u32[]{:S(2)}) collective-permute-start(bf16[32,16,128]{2,1,0:T(8,128)(2,1)S(1)} %all-to-all-done.own_ref), channel_id=1, source_target_pairs={{0,4},{4,0},{8,12},{12,8},{16,20},{20,16},{24,28},{28,24},{32,36},... | collective-permute-start | bytes 393224 | tf_op jit(solution)/shard_map/ppermute | solution.py:331
  25.6 1.4 %copy-start.4 = (bf16[3,1024,256]{2,1,0:T(8,128)(2,1)S(1)}, bf16[3,1024,256]{2,1,0:T(8,128)(2,1)}, u32[]{:S(2)}) copy-start(bf16[3,1024,256]{2,1,0:T(8,128)(2,1)} %w_hbm.3) | copy-start | bytes 4718596
  33.4 1.6 %collective-permute-start.1 = (f32[136,256]{1,0:T(8,128)S(1)}, f32[136,256]{1,0:T(8,128)S(1)}, u32[]{:S(2)}, u32[]{:S(2)}) collective-permute-start(f32[136,256]{1,0:T(8,128)S(1)} %get-tuple-element.17), channel_id=1, source_target_pairs={{0,4},{4,0},{8,12},{12,8},{16,20},{20,16},{24,28},{28,24},{32,36},... | collective-permute-start | bytes 417800 | tf_op jit(solution)/shard_map/ppermute | solution.py:366
  35.7 14.9 %all-to-all-start.1 = ((bf16[32,16,128]{2,1,0:T(8,128)(2,1)}), bf16[32,16,128]{2,1,0:T(8,128)(2,1)S(1)}, u32[]{:S(2)}, u32[]{:S(2)}) async-start(bf16[32,16,128]{2,1,0:T(8,128)(2,1)} %shard_map.49), calls=%async_computation.1 | async-start | bytes 262144 | tf_op jit(solution)/shard_map/all_to_all | solution.py:315
  40.8 24.9 %copy-start.5 = (f32[4,33]{1,0:T(4,128)S(1)}, f32[4,33]{1,0:T(4,128)}, u32[]{:S(2)}) copy-start(f32[4,33]{1,0:T(4,128)} %cw_ref.1) | copy-start | bytes 1588
  51.6 14.1 %all-to-all-start.2 = ((bf16[32,8,128]{2,1,0:T(8,128)(2,1)}), bf16[32,8,128]{2,1,0:T(8,128)(2,1)S(1)}, u32[]{:S(2)}, u32[]{:S(2)}) async-start(bf16[32,8,128]{2,1,0:T(8,128)(2,1)} %shard_map.51), calls=%async_computation.2 | async-start | bytes 131072 | tf_op jit(solution)/shard_map/all_to_all | solution.py:315
  56.7 8.9 %collective-permute-start.3 = (bf16[16,256]{1,0:T(8,128)(2,1)S(1)}, bf16[16,256]{1,0:T(8,128)(2,1)S(1)}, u32[]{:S(2)}, u32[]{:S(2)}) collective-permute-start(bf16[16,256]{1,0:T(8,128)(2,1)S(1)} %get-tuple-element.21), channel_id=1, source_target_pairs={{0,4},{4,0},{8,12},{12,8},{16,20},{20,16},{24,28},{28,24},{32,36},... | collective-permute-start | bytes 24584 | tf_op jit(solution)/shard_map/ppermute | solution.py:350
  56.8 8.8 %collective-permute-start.4 = (bf16[16,256]{1,0:T(8,128)(2,1)S(1)}, bf16[16,256]{1,0:T(8,128)(2,1)S(1)}, u32[]{:S(2)}, u32[]{:S(2)}) collective-permute-start(bf16[16,256]{1,0:T(8,128)(2,1)S(1)} %get-tuple-element.22), channel_id=1, source_target_pairs={{4,8},{12,16},{20,24},{28,32},{36,40},{44,48},{52,56},{60,64},{68,... | collective-permute-start | bytes 24584 | tf_op jit(solution)/shard_map/ppermute | solution.py:351
  65.6 3.0 %collective-permute-start.2 = (bf16[32,8,128]{2,1,0:T(8,128)(2,1)S(1)}, bf16[32,8,128]{2,1,0:T(8,128)(2,1)S(1)}, u32[]{:S(2)}, u32[]{:S(2)}) collective-permute-start(bf16[32,8,128]{2,1,0:T(8,128)(2,1)S(1)} %all-to-all-done.2.own_ref), channel_id=1, source_target_pairs={{0,4},{4,0},{8,12},{12,8},{16,20},{20,16},{24,28},{28,24},{32,36},... | collective-permute-start | bytes 196616 | tf_op jit(solution)/shard_map/ppermute | solution.py:393
  68.6 15.2 %copy-start = (bf16[1024,1024]{1,0:T(8,128)(2,1)S(1)}, bf16[1024,1024]{1,0:T(8,128)(2,1)}, u32[]{:S(2)}) copy-start(bf16[1024,1024]{1,0:T(8,128)(2,1)} %w_ref.1) | copy-start | bytes 6291460

commit v2 on v1

--- a/solution.py
+++ b/solution.py
@@ -24,13 +24,15 @@
 MIB = 1 << 20
 
 
-def call(kernel, outs, scratch=(), specs=None, n_in=1, flops=0, moved=0, exps=0, limit=24):
+def call(
+    kernel, outs, scratch=(), specs=None, out_specs=None, n_in=1, flops=0, moved=0, exps=0, limit=24
+):
     single = not isinstance(outs, (list, tuple))
     return pl.pallas_call(
         kernel,
         out_shape=outs,
         in_specs=specs or [VMEM] * n_in,
-        out_specs=VMEM if single else [VMEM] * len(outs),
+        out_specs=out_specs or (VMEM if single else [VMEM] * len(outs)),
         scratch_shapes=list(scratch),
         compiler_params=pltpu.CompilerParams(vmem_limit_bytes=limit * MIB),
         cost_estimate=pl.CostEstimate(flops=flops, bytes_accessed=moved, transcendentals=exps),
@@ -138,8 +140,28 @@
 
 
 def scores_kernel(
-    core_ref, own_ref, other_ref, k_ref, vt_ref, lq_ref, lk_ref, keep_ref, send_ref, land_rows, acc, level
+    core_ref,
+    own_ref,
+    other_ref,
+    k_hbm,
+    vt_hbm,
+    lq_ref,
+    lk_ref,
+    keep_ref,
+    send_ref,
+    k_ref,
+    vt_ref,
+    land_rows,
+    acc,
+    level,
+    sems,
 ):
+    loads = [
+        pltpu.make_async_copy(k_hbm, k_ref, sems.at[0]),
+        pltpu.make_async_copy(vt_hbm, vt_ref, sems.at[1]),
+    ]
+    for copy in loads:
+        copy.start()
     core = core_ref[0]
     count = CHIPS * 16
     land_rows[pl.ds(core * count, count), :] = own_ref[...].astype(f32).reshape(count, 128)
@@ -149,15 +171,17 @@
     lk = jnp.concatenate(picked[2:], axis=1)
     lq_ref[...] = lq.astype(bf16)
     lk_ref[...] = lk.astype(bf16)
-    key = k_ref[...]
     level[...] = jnp.zeros(level.shape, f32)
+    loads[0].wait()
     for head in range(HEADS):
         rows = slice(head * HD, (head + 1) * HD)
         own = jnp.where(head_mask(head), lq, 0.0).astype(bf16)
-        scores = dot_nt(key, own)
+        scores = dot_nt(k_ref[...], own)
         top = jnp.max(scores, axis=0, keepdims=True)
         expo = jnp.exp((scores - top) * SCALE)
         total = jnp.sum(expo, axis=0, keepdims=True)
+        if head == 0:
+            loads[1].wait()
         acc[rows, :] = dot_nn(vt_ref[rows, :], expo.astype(bf16)) / total
         at = 8 * (head // 2) + head % 2
         level[at : at + 1, :] = top * SCALE + jnp.log(total)
@@ -279,7 +303,10 @@
             out_ref[rows, b * 128 : b * 128 + 128] = out[b * HD : (b + 1) * HD, :]
 
 
-def attend_kernel(core_ref, own_ref, other_ref, kf_ref, conv_ref, out_ref, mid_rows):
+def attend_kernel(core_ref, group_ref, own_ref, other_ref, kf_ref, conv_ref, *refs):
+    out_refs, (mid_rows, joined) = refs[:-2], refs[-2:]
+    groups = len(out_refs)
+    seg = ROWS // groups
     core = core_ref[0]
     count = CHIPS * 8
     mid_rows[pl.ds(core * count, count), :] = own_ref[...].astype(f32).reshape(count, 128)
@@ -291,14 +318,22 @@
     for head in range(HEADS):
         rows = slice(head * HD, (head + 1) * HD)
         outs.append((dot_nn(mid[rows, :], kf_ref[head]) + conv_ref[rows, :]).astype(bf16))
-    out = jnp.concatenate(outs, axis=0).T
-    out_ref[...] = out.reshape(out_ref.shape)
-
-
-def output_kernel(x_ref, w_ref, out_ref):
-    groups = x_ref.shape[0]
-    joined = jnp.concatenate([x_ref[g] for g in range(groups)], axis=1)
-    out_ref[...] = dot_nn(joined, w_ref[...]).astype(bf16)
+    joined[...] = jnp.concatenate(outs, axis=0).T
+    for step in range(groups):
+        to = lax.rem(group_ref[0] + step, groups)
+        out_refs[step][...] = joined[pl.ds(pl.multiple_of(to * seg, seg), seg), :]
+
+
+def output_kernel(group_ref, w_ref, *refs):
+    x_refs, out_ref = refs[:-1], refs[-1]
+    groups = len(x_refs)
+    total = None
+    for step in range(groups):
+        source = lax.rem(group_ref[0] + groups - step, groups)
+        rows = pl.ds(pl.multiple_of(source * WIDTH, WIDTH), WIDTH)
+        part = dot_nn(x_refs[step][...], w_ref[rows, :])
+        total = part if total is None else total + part
+    out_ref[...] = total.astype(bf16)
 
 
 def body(tokens, w_qkv, w_out, conv_weight):
@@ -308,6 +343,8 @@
     onward = [(2 * chip + 1, 2 * chip + 2) for chip in range(CHIPS - 1)]
     onward += [(b, a) for a, b in onward]
     place = lax.axis_index("ctx").astype(jnp.int32)
+    group = lax.axis_index("head").astype(jnp.int32).reshape(1)
+    seg = ROWS // groups
     core = (place % 2).reshape(1)
     head_id = (2 * (place % 2) + place // CHIPS).reshape(1)
 
@@ -326,9 +363,9 @@
         specs=[HBM, HBM],
         flops=2 * 16 * 1024 * 512,
         moved=3 * MIB,
+        limit=63,
     )(tokens, w_qkv)
     land = exchange(own)
-    land_other = lax.ppermute(land, "ctx", swap)
     query, key, value_t, near, far = call(
         project_kernel,
         [
@@ -346,7 +383,12 @@
         specs=[SMEM, HBM, HBM],
         flops=2 * 1024 * 1024 * 768,
         moved=6 * MIB,
+        limit=48,
     )(core, tokens, w_qkv)
+    land, query, key, value_t, near, far = lax.optimization_barrier(
+        (land, query, key, value_t, near, far)
+    )
+    land_other = lax.ppermute(land, "ctx", swap)
     near = lax.ppermute(near, "ctx", swap)
     far = lax.ppermute(far, "ctx", onward)
     land_q, land_k, keep, send = call(
@@ -357,11 +399,19 @@
             shaped((136, M), f32),
             shaped((136, M), f32),
         ],
-        [pltpu.VMEM((CHIPS * 32, 128), f32), pltpu.VMEM((M, M), f32), pltpu.VMEM((16, M), f32)],
-        specs=[SMEM] + [VMEM] * 4,
+        [
+            pltpu.VMEM((ROWS, WIDTH), bf16),
+            pltpu.VMEM((WIDTH, ROWS), bf16),
+            pltpu.VMEM((CHIPS * 32, 128), f32),
+            pltpu.VMEM((M, M), f32),
+            pltpu.VMEM((16, M), f32),
+            pltpu.SemaphoreType.DMA((2,)),
+        ],
+        specs=[SMEM, VMEM, VMEM, HBM, HBM],
         flops=4 * 4 * 1024 * 256 * 256,
         moved=2 * MIB,
         exps=MIB,
+        limit=48,
     )(core, land, land_other, key, value_t)
     received = lax.ppermute(send, "ctx", swap)
     parts = call(
@@ -390,7 +440,6 @@
         moved=MIB // 2,
     )(gathered, inverse)
     mids = exchange(mid_own)
-    mids_other = lax.ppermute(mids, "ctx", swap)
     kernel_f = call(
         token_kernel,
         shaped((HEADS, M, ROWS), bf16),
@@ -406,22 +455,27 @@
         flops=2 * 512 * 768 * 512,
         moved=2 * MIB,
     )(core, value_t, near, far, conv_weight)
+    mids, kernel_f, conv = lax.optimization_barrier((mids, kernel_f, conv))
+    mids_other = lax.ppermute(mids, "ctx", swap)
     head_out = call(
         attend_kernel,
-        shaped((groups, ROWS // groups, WIDTH), bf16),
-        [pltpu.VMEM((CHIPS * 16, 128), f32)],
-        specs=[SMEM] + [VMEM] * 4,
+        [shaped((seg, WIDTH), bf16)] * groups,
+        [pltpu.VMEM((CHIPS * 16, 128), f32), pltpu.VMEM((ROWS, WIDTH), bf16)],
+        specs=[SMEM, SMEM] + [VMEM] * 4,
         flops=4 * 2 * 64 * 256 * 1024,
         moved=4 * MIB,
-    )(core, mids, mids_other, kernel_f, conv)
-    regrouped = lax.all_to_all(head_out, "head", 0, 0, tiled=True)
+    )(core, group, mids, mids_other, kernel_f, conv)
+    arrived = [head_out[0]]
+    for step in range(1, groups):
+        ring = [(i, (i + step) % groups) for i in range(groups)]
+        arrived.append(lax.ppermute(head_out[step], "head", ring))
     return call(
         output_kernel,
-        shaped((ROWS // groups, w_out.shape[1]), bf16),
-        n_in=2,
+        shaped((seg, w_out.shape[1]), bf16),
+        specs=[SMEM] + [VMEM] * (1 + groups),
         flops=2 * 256 * 1024 * 1024,
         moved=3 * MIB,
-    )(regrouped, w_out)
+    )(group, w_out, *arrived)
 
 
 def solution(mesh):

time: 87 us -> 80.1 us (0.921); the launches traced: 85.3 us -> 79.7 us
  blocking collectives: 14.5 us -> 0 us
  starting transfers between devices: 27.1 us -> 35.9 us
  waiting for transfers between devices: 19 us -> 17.5 us
  Pallas kernels: 20 us -> 21.2 us
    all_to_all x1 -> x0, blocking collectives: 14.5 us -> none  [body(): regrouped = lax.all_to_all(head_out, 'head', 0, 0, tiled=True)]
    all_to_all x3, waiting for transfers between devices: 18 us -> 6.28 us  [exchange(): lax.all_to_all(x, 'ctx', 0, 0, tiled=True, axis_index_groups=same_core)]
    ppermute x0 -> x3, starting transfers between devices: none -> 5.9 us  [body(): arrived.append(lax.ppermute(head_out[step], 'head', ring))]
    ppermute x0 -> x3, waiting for transfers between devices: none -> 5 us  [body(): arrived.append(lax.ppermute(head_out[step], 'head', ring))]
    all_to_all x3, starting transfers between devices: 21.8 us -> 24.9 us  [exchange(): lax.all_to_all(x, 'ctx', 0, 0, tiled=True, axis_index_groups=same_core)]
    ppermute x1, waiting for transfers between devices: 0.01 us -> 2.4 us  [body(): far = lax.ppermute(far, 'ctx', onward)]
    ppermute x1, waiting for transfers between devices: 0.01 us -> 1.35 us  [body(): land_other = lax.ppermute(land, 'ctx', swap)]
    ppermute x1, waiting for transfers between devices: 0.01 us -> 1.23 us  [body(): mids_other = lax.ppermute(mids, 'ctx', swap)]
  transfers between devices with their start and end apart: 8 -> 11, of which waited for: 4 -> 8; matrix products, arithmetic and copies ran while one was open for 0% -> 0% of each run, Pallas kernels for 13% -> 14%
where the time goes in v2:
time: 80.1 us; the launch traced here: 79.7 us
  starting transfers between devices  35.9 us (45%)
  Pallas kernels  21.2 us (26%)
  waiting for transfers between devices  17.5 us (22%)
  local copies, waits for them, and re-layouts  4.83 us (6%)
    all_to_all x3, starting transfers between devices, exchange(): lax.all_to_all(x, 'ctx', 0, 0, tiled=True, axis_index_groups=same_core)  24.9 us
    all_to_all x3, waiting for transfers between devices, exchange(): lax.all_to_all(x, 'ctx', 0, 0, tiled=True, axis_index_groups=same_core)  6.28 us
    ppermute x3, starting transfers between devices, body(): arrived.append(lax.ppermute(head_out[step], 'head', ring))  5.9 us
    pallas_call x1, Pallas kernels, body(): call(pinv_kernel, shaped((M, M), f32), specs=[SMEM, VMEM, VMEM], flops=24...  5.05 us
    ppermute x3, waiting for transfers between devices, body(): arrived.append(lax.ppermute(head_out[step], 'head', ring))  5 us
    unnamed x12, local copies, waits for them, and re-layouts  4.83 us
    ppermute x1, starting transfers between devices, body(): far = lax.ppermute(far, 'ctx', onward)  4.67 us
    pallas_call x1, Pallas kernels, body(): call(project_kernel, [shaped((ROWS, WIDTH), bf16), shaped((ROWS, WIDTH),...  3.34 us
  transfers between devices with their start and end apart: 11, of which 8 were waited for; matrix products, arithmetic and copies ran while one was open for 0% of the time, Pallas kernels for 14%

profile of v2, /device:TPU:2, one launch (start us, length us, event | category | flops | bytes accessed | tf_op | source)
XLA Modules:
  0.0 79.7 jit_solution(14338277405620825383)
XLA Ops:
  0.0 2.9 %shard_map.46 = bf16[32,16,128]{2,1,0:T(8,128)(2,1)} custom-call(bf16[1024,1024]{1,0:T(8,128)(2,1)} %tok_hbm.3, bf16[3,1024,256]{2,1,0:T(8,128)(2,1)} %w_hbm.3), custom_call_target="tpu_custom_call" | custom-call | flops 16777216 | bytes 3145728 | tf_op jit(solution)/shard_map/pallas_call | solution.py:354
  2.9 11.6 %all-to-all-start = ((bf16[32,16,128]{2,1,0:T(8,128)(2,1)}), bf16[32,16,128]{2,1,0:T(8,128)(2,1)S(1)}, u32[]{:S(2)}, u32[]{:S(2)}) async-start(bf16[32,16,128]{2,1,0:T(8,128)(2,1)} %shard_map.46), calls=%async_computation | async-start | bytes 262144 | tf_op jit(solution)/shard_map/all_to_all | solution.py:352
  14.6 1.6 %copy-done = bf16[1024,1024]{1,0:T(8,128)(2,1)S(1)} copy-done((bf16[1024,1024]{1,0:T(8,128)(2,1)S(1)}, bf16[1024,1024]{1,0:T(8,128)(2,1)}, u32[]{:S(2)}) %copy-start) | copy-done | bytes 2097176
  16.1 1.4 %copy-done.2 = bf16[3,1024,256]{2,1,0:T(8,128)(2,1)S(1)} copy-done((bf16[3,1024,256]{2,1,0:T(8,128)(2,1)S(1)}, bf16[3,1024,256]{2,1,0:T(8,128)(2,1)}, u32[]{:S(2)}) %copy-start.2) | copy-done | bytes 1572888
  17.6 3.3 %shard_map.47 = (bf16[1024,256]{1,0:T(8,128)(2,1)S(1)}, bf16[1024,256]{1,0:T(8,128)(2,1)S(1)}, bf16[256,1024]{1,0:T(8,128)(2,1)S(1)}, bf16[16,256]{1,0:T(8,128)(2,1)S(1)}, bf16[16,256]{1,0:T(8,128)(2,1)S(1)}) custom-call(s32[1]{0:T(128)} %bitcast.1.core_ref, bf16[1024,1024]{1,0:T(8,128)(2,1)S(1)} %copy-done, bf16[3,1024,256]{2,1,0:T(8,128)(2,1)S(1)} %copy-done.2), custom_call_target="tpu_custom_call" | custom-call | flops 1610612736 | bytes 6291456 | tf_op jit(solution)/shard_map/pallas_call | solution.py:369
  20.9 0.8 copy-done.3
  21.7 1.9 %all-to-all-done.own_ref = bf16[32,16,128]{2,1,0:T(8,128)(2,1)S(1)} async-done(((bf16[32,16,128]{2,1,0:T(8,128)(2,1)}), bf16[32,16,128]{2,1,0:T(8,128)(2,1)S(1)}, u32[]{:S(2)}, u32[]{:S(2)}) %all-to-all-start) | async-done | bytes 131104 | tf_op jit(solution)/shard_map/all_to_all | solution.py:352
  23.6 1.3 %collective-permute-done.other_ref = bf16[32,16,128]{2,1,0:T(8,128)(2,1)S(1)} collective-permute-done((bf16[32,16,128]{2,1,0:T(8,128)(2,1)S(1)}, bf16[32,16,128]{2,1,0:T(8,128)(2,1)S(1)}, u32[]{:S(2)}, u32[]{:S(2)}) %collective-permute-start) | collective-permute-done | bytes 131104 | tf_op jit(solution)/shard_map/ppermute | solution.py:391
  25.0 3.2 %shard_map.48 = (bf16[256,256]{1,0:T(8,128)(2,1)S(1)}, bf16[256,256]{1,0:T(8,128)(2,1)S(1)}, f32[136,256]{1,0:T(8,128)S(1)}, f32[136,256]{1,0:T(8,128)S(1)}) custom-call(s32[1]{0:T(128)} %bitcast.1.core_ref, bf16[32,16,128]{2,1,0:T(8,128)(2,1)S(1)} %all-to-all-done.own_ref, bf16[32,16,128]{2,1,0:T(8,128)(2,1)S(1)} %collective-permute-done.other_ref, ...), custom_call_target="tpu_custom_call" | custom-call | flops 1073741824 | bytes 2097152 | tf_op jit(solution)/shard_map/pallas_call | solution.py:394
  28.2 0.2 collective-permute-start.1
  28.4 1.2 %collective-permute-done.1.other_ref = f32[136,256]{1,0:T(8,128)S(1)} collective-permute-done((f32[136,256]{1,0:T(8,128)S(1)}, f32[136,256]{1,0:T(8,128)S(1)}, u32[]{:S(2)}, u32[]{:S(2)}) %collective-permute-start.1) | collective-permute-done | bytes 139296 | tf_op jit(solution)/shard_map/ppermute | solution.py:416
  29.6 0.8 shard_map.49
  30.4 7.9 %all-to-all-start.1 = ((bf16[32,16,128]{2,1,0:T(8,128)(2,1)}), bf16[32,16,128]{2,1,0:T(8,128)(2,1)S(1)}, u32[]{:S(2)}, u32[]{:S(2)}) async-start(bf16[32,16,128]{2,1,0:T(8,128)(2,1)} %shard_map.49), calls=%async_computation.1 | async-start | bytes 262144 | tf_op jit(solution)/shard_map/all_to_all | solution.py:352
  38.3 5.1 %shard_map.50.w_ref = f32[256,256]{1,0:T(8,128)S(1)} custom-call(s32[1]{0:T(128)} %bitcast.2.head_ref, bf16[256,256]{1,0:T(8,128)(2,1)S(1)} %get-tuple-element.37.lq_ref, bf16[256,256]{1,0:T(8,128)(2,1)S(1)} %get-tuple-element.38.lk_ref), custom_call_target="tpu_custom_call" | custom-call | flops 2415919104 | bytes 524288 | tf_op jit(solution)/shard_map/pallas_call | solution.py:426
  43.4 4.3 %all-to-all-done.1.parts_ref = bf16[32,16,128]{2,1,0:T(8,128)(2,1)S(1)} async-done(((bf16[32,16,128]{2,1,0:T(8,128)(2,1)}), bf16[32,16,128]{2,1,0:T(8,128)(2,1)S(1)}, u32[]{:S(2)}, u32[]{:S(2)}) %all-to-all-start.1) | async-done | bytes 131104 | tf_op jit(solution)/shard_map/all_to_all | solution.py:352
  47.7 0.9 %shard_map.51 = bf16[32,8,128]{2,1,0:T(8,128)(2,1)} custom-call(bf16[32,16,128]{2,1,0:T(8,128)(2,1)S(1)} %all-to-all-done.1.parts_ref, f32[256,256]{1,0:T(8,128)S(1)} %shard_map.50.w_ref), custom_call_target="tpu_custom_call" | custom-call | flops 3145728 | bytes 524288 | tf_op jit(solution)/shard_map/pallas_call | solution.py:434
  48.6 5.4 %all-to-all-start.2 = ((bf16[32,8,128]{2,1,0:T(8,128)(2,1)}), bf16[32,8,128]{2,1,0:T(8,128)(2,1)S(1)}, u32[]{:S(2)}, u32[]{:S(2)}) async-start(bf16[32,8,128]{2,1,0:T(8,128)(2,1)} %shard_map.51), calls=%async_computation.2 | async-start | bytes 131072 | tf_op jit(solution)/shard_map/all_to_all | solution.py:352
  54.1 0.1 collective-permute-start.2
  54.2 4.7 %collective-permute-start.3 = (bf16[16,256]{1,0:T(8,128)(2,1)S(1)}, bf16[16,256]{1,0:T(8,128)(2,1)S(1)}, u32[]{:S(2)}, u32[]{:S(2)}) collective-permute-start(bf16[16,256]{1,0:T(8,128)(2,1)S(1)} %get-tuple-element.41), channel_id=1, source_target_pairs={{4,8},{12,16},{20,24},{28,32},{36,40},{44,48},{52,56},{60,64},{68,... | collective-permute-start | bytes 24584 | tf_op jit(solution)/shard_map/ppermute | solution.py:393
  58.9 2.4 %collective-permute-done.3.far_ref = bf16[16,256]{1,0:T(8,128)(2,1)S(1)} collective-permute-done((bf16[16,256]{1,0:T(8,128)(2,1)S(1)}, bf16[16,256]{1,0:T(8,128)(2,1)S(1)}, u32[]{:S(2)}, u32[]{:S(2)}) %collective-permute-start.3) | collective-permute-done | bytes 8224 | tf_op jit(solution)/shard_map/ppermute | solution.py:393
  61.3 1.1 %shard_map.53.conv_ref = f32[256,1024]{1,0:T(8,128)S(1)} custom-call(s32[1]{0:T(128)} %bitcast.1.core_ref, bf16[256,1024]{1,0:T(8,128)(2,1)S(1)} %get-tuple-element.34.vt_hbm.vt_ref, bf16[16,256]{1,0:T(8,128)(2,1)S(1)} %collective-permute-done.2.near_ref, bf16[16,256]{1,0:T(8,128)(2,1)S(1)} %collective-permute-done.3.far_ref, f32[4,33]{1,0:T(4,128)S(1)} %copy-done.5), custom_call_target="tpu_custom_call" | custom-call | flops 402653184 | bytes 2097152 | tf_op jit(solution)/shard_map/pallas_call | solution.py:451
  62.4 1.0 %copy-done.4 = bf16[1024,256]{1,0:T(8,128)(2,1)S(1)} copy-done((bf16[1024,256]{1,0:T(8,128)(2,1)S(1)}, bf16[1024,256]{1,0:T(8,128)(2,1)}, u32[]{:S(2)}) %copy-start.4) | copy-done | bytes 524312
  63.4 1.9 %shard_map.52.kf_ref = bf16[4,256,1024]{2,1,0:T(8,128)(2,1)S(1)} custom-call(bf16[256,256]{1,0:T(8,128)(2,1)S(1)} %get-tuple-element.38.lk_ref, bf16[1024,256]{1,0:T(8,128)(2,1)S(1)} %copy-done.4), custom_call_target="tpu_custom_call" | custom-call | flops 536870912 | bytes 3145728 | tf_op jit(solution)/shard_map/pallas_call | solution.py:443
  65.3 0.1 collective-permute-start.4
  65.4 1.2 %collective-permute-done.4.other_ref = bf16[32,8,128]{2,1,0:T(8,128)(2,1)S(1)} collective-permute-done((bf16[32,8,128]{2,1,0:T(8,128)(2,1)S(1)}, bf16[32,8,128]{2,1,0:T(8,128)(2,1)S(1)}, u32[]{:S(2)}, u32[]{:S(2)}) %collective-permute-start.4) | collective-permute-done | bytes 65568 | tf_op jit(solution)/shard_map/ppermute | solution.py:459
  66.7 0.6 shard_map.54
  67.3 1.7 %collective-permute-start.5 = (bf16[256,256]{1,0:T(8,128)(2,1)S(1)}, bf16[256,256]{1,0:T(8,128)(2,1)S(1)}, u32[]{:S(2)}, u32[]{:S(2)}) collective-permute-start(bf16[256,256]{1,0:T(8,128)(2,1)S(1)} %get-tuple-element.46), channel_id=1, source_target_pairs={{0,1},{1,2},{2,3},{3,0},{4,5},{5,6},{6,7},{7,4},{8,9},{9,10},{10,1... | collective-permute-start | bytes 393224 | tf_op jit(solution)/shard_map/ppermute | solution.py:471
  68.9 2.9 %collective-permute-start.6 = (bf16[256,256]{1,0:T(8,128)(2,1)S(1)}, bf16[256,256]{1,0:T(8,128)(2,1)S(1)}, u32[]{:S(2)}, u32[]{:S(2)}) collective-permute-start(bf16[256,256]{1,0:T(8,128)(2,1)S(1)} %get-tuple-element.47), channel_id=1, source_target_pairs={{0,2},{1,3},{2,0},{3,1},{4,6},{5,7},{6,4},{7,5},{8,10},{9,11},{10,... | collective-permute-start | bytes 393224 | tf_op jit(solution)/shard_map/ppermute | solution.py:471
  71.8 1.3 %collective-permute-start.7 = (bf16[256,256]{1,0:T(8,128)(2,1)S(1)}, bf16[256,256]{1,0:T(8,128)(2,1)S(1)}, u32[]{:S(2)}, u32[]{:S(2)}) collective-permute-start(bf16[256,256]{1,0:T(8,128)(2,1)S(1)} %get-tuple-element.48), channel_id=1, source_target_pairs={{0,3},{1,0},{2,1},{3,2},{4,7},{5,4},{6,5},{7,6},{8,11},{9,8},{10,9... | collective-permute-start | bytes 393224 | tf_op jit(solution)/shard_map/ppermute | solution.py:471
  73.2 1.0 %collective-permute-done.5.refs_1_ = bf16[256,256]{1,0:T(8,128)(2,1)S(1)} collective-permute-done((bf16[256,256]{1,0:T(8,128)(2,1)S(1)}, bf16[256,256]{1,0:T(8,128)(2,1)S(1)}, u32[]{:S(2)}, u32[]{:S(2)}) %collective-permute-start.5) | collective-permute-done | bytes 131104 | tf_op jit(solution)/shard_map/ppermute | solution.py:471
  74.2 4.0 %collective-permute-done.6.refs_2_ = bf16[256,256]{1,0:T(8,128)(2,1)S(1)} collective-permute-done((bf16[256,256]{1,0:T(8,128)(2,1)S(1)}, bf16[256,256]{1,0:T(8,128)(2,1)S(1)}, u32[]{:S(2)}, u32[]{:S(2)}) %collective-permute-start.6) | collective-permute-done | bytes 131104 | tf_op jit(solution)/shard_map/ppermute | solution.py:471
  78.2 1.5 %shard_map.55 = bf16[256,1024]{1,0:T(8,128)(2,1)} custom-call(s32[1]{0:T(128)} %bitcast.group_ref, bf16[1024,1024]{1,0:T(8,128)(2,1)S(1)} %copy-done.1, bf16[256,256]{1,0:T(8,128)(2,1)S(1)} %get-tuple-element.45.refs_0_, bf16[256,256]{1,0:T(8,128)(2,1)S(1)} %collective-permute-done.5.refs_1_, bf16[256,256]{1,0:T(8,128)(2,1)S(1)} %collective-permute-done.6.refs_2_, ...), custom_call_target="tpu_custom_call" | custom-call | flops 536870912 | bytes 3145728 | tf_op jit(solution)/shard_map/pallas_call | solution.py:472
  (12 shorter events, 0.0 us)
Async XLA Ops:
  2.9 20.7 %all-to-all-start = ((bf16[32,16,128]{2,1,0:T(8,128)(2,1)}), bf16[32,16,128]{2,1,0:T(8,128)(2,1)S(1)}, u32[]{:S(2)}, u32[]{:S(2)}) async-start(bf16[32,16,128]{2,1,0:T(8,128)(2,1)} %shard_map.46), calls=%async_computation | async-start | bytes 262144 | tf_op jit(solution)/shard_map/all_to_all | solution.py:352
  14.6 1.6 %copy-start = (bf16[1024,1024]{1,0:T(8,128)(2,1)S(1)}, bf16[1024,1024]{1,0:T(8,128)(2,1)}, u32[]{:S(2)}) copy-start(bf16[1024,1024]{1,0:T(8,128)(2,1)} %tok_hbm.3) | copy-start | bytes 6291460
  16.1 1.4 %copy-start.2 = (bf16[3,1024,256]{2,1,0:T(8,128)(2,1)S(1)}, bf16[3,1024,256]{2,1,0:T(8,128)(2,1)}, u32[]{:S(2)}) copy-start(bf16[3,1024,256]{2,1,0:T(8,128)(2,1)} %w_hbm.3) | copy-start | bytes 4718596
  20.9 0.8 copy-start.3
  23.6 1.3 %collective-permute-start = (bf16[32,16,128]{2,1,0:T(8,128)(2,1)S(1)}, bf16[32,16,128]{2,1,0:T(8,128)(2,1)S(1)}, u32[]{:S(2)}, u32[]{:S(2)}) collective-permute-start(bf16[32,16,128]{2,1,0:T(8,128)(2,1)S(1)} %all-to-all-done.own_ref), channel_id=1, source_target_pairs={{0,4},{4,0},{8,12},{12,8},{16,20},{20,16},{24,28},{28,24},{32,36},... | collective-permute-start | bytes 393224 | tf_op jit(solution)/shard_map/ppermute | solution.py:391
  28.2 1.4 %collective-permute-start.1 = (f32[136,256]{1,0:T(8,128)S(1)}, f32[136,256]{1,0:T(8,128)S(1)}, u32[]{:S(2)}, u32[]{:S(2)}) collective-permute-start(f32[136,256]{1,0:T(8,128)S(1)} %get-tuple-element.36), channel_id=1, source_target_pairs={{0,4},{4,0},{8,12},{12,8},{16,20},{20,16},{24,28},{28,24},{32,36},... | collective-permute-start | bytes 417800 | tf_op jit(solution)/shard_map/ppermute | solution.py:416
  30.4 17.3 %all-to-all-start.1 = ((bf16[32,16,128]{2,1,0:T(8,128)(2,1)}), bf16[32,16,128]{2,1,0:T(8,128)(2,1)S(1)}, u32[]{:S(2)}, u32[]{:S(2)}) async-start(bf16[32,16,128]{2,1,0:T(8,128)(2,1)} %shard_map.49), calls=%async_computation.1 | async-start | bytes 262144 | tf_op jit(solution)/shard_map/all_to_all | solution.py:352
  38.3 23.0 %copy-start.5 = (f32[4,33]{1,0:T(4,128)S(1)}, f32[4,33]{1,0:T(4,128)}, u32[]{:S(2)}) copy-start(f32[4,33]{1,0:T(4,128)} %cw_ref.1) | copy-start | bytes 1588
  48.6 16.7 %all-to-all-start.2 = ((bf16[32,8,128]{2,1,0:T(8,128)(2,1)}), bf16[32,8,128]{2,1,0:T(8,128)(2,1)S(1)}, u32[]{:S(2)}, u32[]{:S(2)}) async-start(bf16[32,8,128]{2,1,0:T(8,128)(2,1)} %shard_map.51), calls=%async_computation.2 | async-start | bytes 131072 | tf_op jit(solution)/shard_map/all_to_all | solution.py:352
  54.1 4.8 %collective-permute-start.2 = (bf16[16,256]{1,0:T(8,128)(2,1)S(1)}, bf16[16,256]{1,0:T(8,128)(2,1)S(1)}, u32[]{:S(2)}, u32[]{:S(2)}) collective-permute-start(bf16[16,256]{1,0:T(8,128)(2,1)S(1)} %get-tuple-element.40), channel_id=1, source_target_pairs={{0,4},{4,0},{8,12},{12,8},{16,20},{20,16},{24,28},{28,24},{32,36},... | collective-permute-start | bytes 24584 | tf_op jit(solution)/shard_map/ppermute | solution.py:392
  54.2 7.1 %collective-permute-start.3 = (bf16[16,256]{1,0:T(8,128)(2,1)S(1)}, bf16[16,256]{1,0:T(8,128)(2,1)S(1)}, u32[]{:S(2)}, u32[]{:S(2)}) collective-permute-start(bf16[16,256]{1,0:T(8,128)(2,1)S(1)} %get-tuple-element.41), channel_id=1, source_target_pairs={{4,8},{12,16},{20,24},{28,32},{36,40},{44,48},{52,56},{60,64},{68,... | collective-permute-start | bytes 24584 | tf_op jit(solution)/shard_map/ppermute | solution.py:393
  62.4 1.0 %copy-start.4 = (bf16[1024,256]{1,0:T(8,128)(2,1)S(1)}, bf16[1024,256]{1,0:T(8,128)(2,1)}, u32[]{:S(2)}) copy-start(bf16[1024,256]{1,0:T(8,128)(2,1)} %copy-done.3) | copy-start | bytes 1572868
  65.3 1.3 %collective-permute-start.4 = (bf16[32,8,128]{2,1,0:T(8,128)(2,1)S(1)}, bf16[32,8,128]{2,1,0:T(8,128)(2,1)S(1)}, u32[]{:S(2)}, u32[]{:S(2)}) collective-permute-start(bf16[32,8,128]{2,1,0:T(8,128)(2,1)S(1)} %all-to-all-done.2.own_ref), channel_id=1, source_target_pairs={{0,4},{4,0},{8,12},{12,8},{16,20},{20,16},{24,28},{28,24},{32,36},... | collective-permute-start | bytes 196616 | tf_op jit(solution)/shard_map/ppermute | solution.py:459
  65.4 12.8 %copy-start.1 = (bf16[1024,1024]{1,0:T(8,128)(2,1)S(1)}, bf16[1024,1024]{1,0:T(8,128)(2,1)}, u32[]{:S(2)}) copy-start(bf16[1024,1024]{1,0:T(8,128)(2,1)} %w_ref.1) | copy-start | bytes 6291460
  67.3 6.9 %collective-permute-start.5 = (bf16[256,256]{1,0:T(8,128)(2,1)S(1)}, bf16[256,256]{1,0:T(8,128)(2,1)S(1)}, u32[]{:S(2)}, u32[]{:S(2)}) collective-permute-start(bf16[256,256]{1,0:T(8,128)(2,1)S(1)} %get-tuple-element.46), channel_id=1, source_target_pairs={{0,1},{1,2},{2,3},{3,0},{4,5},{5,6},{6,7},{7,4},{8,9},{9,10},{10,1... | collective-permute-start | bytes 393224 | tf_op jit(solution)/shard_map/ppermute | solution.py:471
  68.9 9.2 %collective-permute-start.6 = (bf16[256,256]{1,0:T(8,128)(2,1)S(1)}, bf16[256,256]{1,0:T(8,128)(2,1)S(1)}, u32[]{:S(2)}, u32[]{:S(2)}) collective-permute-start(bf16[256,256]{1,0:T(8,128)(2,1)S(1)} %get-tuple-element.47), channel_id=1, source_target_pairs={{0,2},{1,3},{2,0},{3,1},{4,6},{5,7},{6,4},{7,5},{8,10},{9,11},{10,... | collective-permute-start | bytes 393224 | tf_op jit(solution)/shard_map/ppermute | solution.py:471
  71.8 6.3 %collective-permute-start.7 = (bf16[256,256]{1,0:T(8,128)(2,1)S(1)}, bf16[256,256]{1,0:T(8,128)(2,1)S(1)}, u32[]{:S(2)}, u32[]{:S(2)}) collective-permute-start(bf16[256,256]{1,0:T(8,128)(2,1)S(1)} %get-tuple-element.48), channel_id=1, source_target_pairs={{0,3},{1,0},{2,1},{3,2},{4,7},{5,4},{6,5},{7,6},{8,11},{9,8},{10,9... | collective-permute-start | bytes 393224 | tf_op jit(solution)/shard_map/ppermute | solution.py:471

commit v3 on v2

v3 whole, which is shorter than its diff:
```python
import jax
import jax.numpy as jnp
from jax import lax
from jax.experimental import pallas as pl
from jax.experimental.pallas import tpu as pltpu
from jax.sharding import PartitionSpec as P

M = 256
NS_STEPS = 6
TAPS = 33
HALF = 16
HEADS = 4
HD = 64
WIDTH = 256
CHIPS = 32
ROWS = 1024
SCALE = 0.125
f32 = jnp.float32
bf16 = jnp.bfloat16
INTERPRET = False
VMEM = pl.BlockSpec(memory_space=pltpu.VMEM)
SMEM = pl.BlockSpec(memory_space=pltpu.SMEM)
HBM = pl.BlockSpec(memory_space=pltpu.HBM)
MIB = 1 << 20


def call(
    kernel, outs, scratch=(), specs=None, out_specs=None, n_in=1, flops=0, moved=0, exps=0, limit=24
):
    single = not isinstance(outs, (list, tuple))
    return pl.pallas_call(
        kernel,
        out_shape=outs,
        in_specs=specs or [VMEM] * n_in,
        out_specs=out_specs or (VMEM if single else [VMEM] * len(outs)),
        scratch_shapes=list(scratch),
        compiler_params=pltpu.CompilerParams(vmem_limit_bytes=limit * MIB),
        cost_estimate=pl.CostEstimate(flops=flops, bytes_accessed=moved, transcendentals=exps),
        interpret=INTERPRET,
    )


def shaped(shape, dtype):
    return jax.ShapeDtypeStruct(shape, dtype)


def dot_nn(a, b):
    return lax.dot_general(a, b, (((1,), (0,)), ((), ())), preferred_element_type=f32)


def dot_nt(a, b):
    return lax.dot_general(a, b, (((1,), (1,)), ((), ())), preferred_element_type=f32)


def split_2(x):
    high = x.astype(bf16)
    return high, (x - high.astype(f32)).astype(bf16)


def split_3(x):
    high = x.astype(bf16)
    rest = x - high.astype(f32)
    middle = rest.astype(bf16)
    return high, middle, (rest - middle.astype(f32)).astype(bf16)


def dot_wide(a, b, transposed=False):
    (ah, al), (bh, bl) = a, b
    left = jnp.concatenate([ah, ah, al], axis=1)
    if transposed:
        return dot_nt(left, jnp.concatenate([bh, bl, bh], axis=1))
    return dot_nn(left, jnp.concatenate([bh, bl, bh], axis=0))


def head_mask(head):
    lane = lax.broadcasted_iota(jnp.int32, (M, WIDTH), 1)
    return (lane >= head * HD) & (lane < (head + 1) * HD)


def landmarks_kernel(tok_hbm, w_hbm, out_ref, tok_ref, w_ref, rows_ref, sems):
    seg = ROWS // 4
    copies = [
        pltpu.make_async_copy(
            tok_hbm.at[s * seg : (s + 1) * seg, :], tok_ref.at[s * seg : (s + 1) * seg, :], sems.at[s]
        )
        for s in range(4)
    ] + [pltpu.make_async_copy(w_hbm.at[c], w_ref.at[c], sems.at[4 + c]) for c in range(2)]
    for copy in copies:
        copy.start()
    sums = []
    for s in range(4):
        copies[s].wait()
        sums.append(
            jnp.sum(tok_ref[s * seg : (s + 1) * seg, :].astype(f32), axis=0, keepdims=True)
        )
    means = jnp.concatenate(sums, axis=0) * (1.0 / seg)
    high, middle, low = split_3(means)
    stacked = jnp.concatenate(
        [high.astype(f32), middle.astype(f32), low.astype(f32), jnp.zeros_like(means)], axis=0
    ).astype(bf16)
    for kind in range(2):
        copies[4 + kind].wait()
        product = dot_nn(stacked, w_ref[kind])
        land = product[0:4] + product[4:8] + product[8:12]
        for half in range(2):
            rows_ref[pl.ds(2 * kind + half, 4, stride=4), :] = land[:, half * 128 : half * 128 + 128]
    out_ref[...] = jnp.broadcast_to(rows_ref[...].astype(bf16)[None], out_ref.shape)


def project_kernel(core_ref, own_ref, other_ref, w_ref, k_ref, vt_ref, k2_ref, vt2_ref, near_ref, far_ref):
    edges = []
    for tok_ref, key_ref, value_ref in ((own_ref, k_ref, vt_ref), (other_ref, k2_ref, vt2_ref)):
        tok = tok_ref[...]
        key_ref[...] = dot_nn(tok, w_ref[1]).astype(bf16)
        value = dot_nn(tok, w_ref[2]).astype(bf16)
        value_ref[...] = value.T
        edges.append((value[:HALF].astype(f32), value[ROWS - HALF :].astype(f32)))
    is_first = core_ref[0] == 0
    near_ref[...] = jnp.where(is_first, edges[1][0], edges[1][1]).astype(bf16)
    far_ref[...] = jnp.where(is_first, edges[0][0], edges[0][1]).astype(bf16)


def query_kernel(tok_ref, w_ref, q_ref):
    q_ref[...] = dot_nn(tok_ref[...], w_ref[0]).astype(bf16)


def pick_rows(land_rows, first, count, at):
    return jnp.concatenate(
        [land_rows[pl.ds(first + at + half, count, stride=4), :] for half in range(2)], axis=1
    )


def scores_kernel(land_ref, k_ref, vt_ref, k2_ref, vt2_ref, out_ref, land_rows):
    land_rows[...] = land_ref[...].astype(f32).reshape(CHIPS * 16, 128)
    lq = pick_rows(land_rows, 0, CHIPS * 4, 0)
    lane = lax.broadcasted_iota(jnp.int32, lq.shape, 1)
    own = [
        jnp.concatenate(
            [
                jnp.where((lane >= head * HD) & (lane < (head + 1) * HD), lq, 0.0)
                for head in (2 * pair, 2 * pair + 1)
            ],
            axis=0,
        ).astype(bf16)
        for pair in range(2)
    ]
    found = []
    for key_ref, value_ref in ((k_ref, vt_ref), (k2_ref, vt2_ref)):
        for pair in range(2):
            scores = dot_nt(key_ref[...], own[pair])
            top = jnp.max(scores, axis=0, keepdims=True)
            expo = jnp.exp((scores - top) * SCALE)
            total = jnp.sum(expo, axis=0, keepdims=True)
            rows = slice(pair * 128, pair * 128 + 128)
            found.append((top, total, dot_nn(value_ref[rows, :], expo.astype(bf16))))
    each = CHIPS // HEADS
    for pair in range(2):
        top_a, total_a, sum_a = found[pair]
        top_b, total_b, sum_b = found[2 + pair]
        top = jnp.maximum(top_a, top_b)
        scale_a = jnp.exp((top_a - top) * SCALE)
        scale_b = jnp.exp((top_b - top) * SCALE)
        total = total_a * scale_a + total_b * scale_b
        mean = sum_a * (scale_a / total) + sum_b * (scale_b / total)
        level = [p.astype(f32) for p in split_3(top * SCALE + jnp.log(total))]
        level = jnp.concatenate(level + [jnp.zeros((5, 256), f32)], axis=0)
        for side in range(2):
            lanes = slice(side * 128, side * 128 + 128)
            block = mean[side * HD : (side + 1) * HD, lanes].reshape(each, 8, 128)
            tail = jnp.broadcast_to(level[None, :, lanes], (each, 8, 128))
            at = (2 * pair + side) * each
            out_ref[at : at + each] = jnp.concatenate([block, tail], axis=1).astype(bf16)


def pinv_kernel(core_ref, head_ref, own_ref, other_ref, lk_ref, w_ref, land_rows):
    core = core_ref[0]
    count = CHIPS * 16
    land_rows[pl.ds(core * count, count), :] = own_ref[...].astype(f32).reshape(count, 128)
    land_rows[pl.ds((1 - core) * count, count), :] = other_ref[...].astype(f32).reshape(count, 128)
    lk_ref[...] = pick_rows(land_rows, 0, M, 2).astype(bf16)
    own = jnp.where(head_mask(head_ref[0]), pick_rows(land_rows, 0, M, 0), 0.0).astype(bf16)
    scores = dot_nt(own, lk_ref[...]) * SCALE
    expo = jnp.exp(scores - jnp.max(scores, axis=1, keepdims=True))
    kernel = expo / jnp.sum(expo, axis=1, keepdims=True)
    col_sum = jnp.max(jnp.sum(kernel, axis=0, keepdims=True))
    row_sum = jnp.max(jnp.sum(kernel, axis=1, keepdims=True))
    approx = kernel / (col_sum * row_sum)
    diagonal = lax.broadcasted_iota(jnp.int32, (M, M), 0) == lax.broadcasted_iota(jnp.int32, (M, M), 1)
    ident = jnp.where(diagonal, 1.0, 0.0)
    prod = dot_wide(split_2(approx), split_2(kernel), transposed=True)
    for step in range(NS_STEPS):
        parts = split_2(prod)
        square = dot_wide(parts, parts)
        last = step == NS_STEPS - 1
        right = 7.0 * ident - prod
        if not last:
            right = jnp.concatenate([right, 7.0 * prod - square], axis=1)
        both = dot_wide(split_2(square), split_2(right))
        factor = 0.25 * (13.0 * ident - 15.0 * prod + both[:, :M])
        if not last:
            prod = 0.25 * (13.0 * prod - 15.0 * square + both[:, M:])
        approx = dot_wide(split_2(factor), split_2(approx))
    w_ref[...] = approx


def middle_kernel(core_ref, own_ref, other_ref, w_ref, out_ref):
    sides = []
    for ref in (own_ref, other_ref):
        parts = ref[...].astype(f32)
        level = (parts[:, 8] + parts[:, 9]) + parts[:, 10]
        weight = jnp.exp(level - jnp.max(level, axis=0, keepdims=True))
        weight = weight / jnp.sum(weight, axis=0, keepdims=True)
        sides.append(jnp.sum(parts[:, 0:8] * weight[:, None, :], axis=0))
    is_first = core_ref[0] == 0
    bv = jnp.concatenate(
        [jnp.where(is_first, sides[0], sides[1]), jnp.where(is_first, sides[1], sides[0])], axis=1
    )
    mid = dot_wide(split_2(bv), split_2(w_ref[...]))
    rows = jnp.concatenate([mid[:, :128], mid[:, 128:]], axis=0)
    out_ref[...] = jnp.broadcast_to(rows.astype(bf16)[None], out_ref.shape)


def token_kernel(lk_ref, q_ref, out_ref):
    query = q_ref[...]
    lk = lk_ref[...].astype(f32)
    for head in range(HEADS):
        own = jnp.where(head_mask(head), lk, 0.0).astype(bf16)
        scores = dot_nt(own, query)
        expo = jnp.exp((scores - jnp.max(scores, axis=0, keepdims=True)) * SCALE)
        out_ref[head] = (expo / jnp.sum(expo, axis=0, keepdims=True)).astype(bf16)


def conv_kernel(core_ref, vt_ref, near_ref, far_ref, cw_ref, out_ref):
    blocks = ROWS // 128
    is_first = core_ref[0] == 0
    near = near_ref[...].astype(f32)
    far = far_ref[...].astype(f32)
    empty = jnp.zeros((128 - HALF, WIDTH), f32)
    before = jnp.concatenate([empty, jnp.where(is_first, far, near)], axis=0).T.astype(bf16)
    after = jnp.concatenate([jnp.where(is_first, near, far), empty], axis=0).T.astype(bf16)
    for head in range(HEADS):
        taps = jnp.concatenate([cw_ref[head : head + 1, :], jnp.zeros((1, 384 - TAPS), f32)], axis=1)
        band = pltpu.roll(
            jnp.broadcast_to(taps, (128, 384)), 128 - HALF, 1, stride=1, stride_axis=0
        )
        high, low = split_2(band)
        rows = slice(head * HD, (head + 1) * HD)
        pieces = [before[rows, :]]
        pieces += [vt_ref[rows, b * 128 : b * 128 + 128] for b in range(blocks)]
        pieces += [after[rows, :]]
        windows = jnp.concatenate(
            [jnp.concatenate(pieces[b : b + 3] * 2, axis=1) for b in range(blocks)], axis=0
        )
        out = dot_nt(windows, jnp.concatenate([high, low], axis=1))
        for b in range(blocks):
            out_ref[rows, b * 128 : b * 128 + 128] = out[b * HD : (b + 1) * HD, :]


def attend_kernel(group_ref, mid_ref, kf_ref, conv_ref, *refs):
    out_refs, joined = refs[:-1], refs[-1]
    groups = len(out_refs)
    seg = ROWS // groups
    mid = mid_ref[...].astype(f32)
    mid = jnp.concatenate(
        [mid[:, :8].reshape(M, 128), mid[:, 8:].reshape(M, 128)], axis=1
    ).astype(bf16)
    outs = []
    for head in range(HEADS):
        rows = slice(head * HD, (head + 1) * HD)
        outs.append((dot_nn(mid[rows, :], kf_ref[head]) + conv_ref[rows, :]).astype(bf16))
    joined[...] = jnp.concatenate(outs, axis=0).T
    for step in range(groups):
        to = lax.rem(group_ref[0] + step, groups)
        out_refs[step][...] = joined[pl.ds(pl.multiple_of(to * seg, seg), seg), :]


def output_kernel(group_ref, w_ref, *refs):
    x_refs, (out_hbm, joined, out_ref, sems) = refs[:-4], refs[-4:]
    groups = len(x_refs)
    for step in range(groups):
        source = lax.rem(group_ref[0] + groups - step, groups)
        joined[:, pl.ds(pl.multiple_of(source * WIDTH, WIDTH), WIDTH)] = x_refs[step][...]
    copies = []
    for part in range(4):
        lanes = slice(part * 256, part * 256 + 256)
        out_ref[:, lanes] = dot_nn(joined[...], w_ref[:, lanes]).astype(bf16)
        copies.append(pltpu.make_async_copy(out_ref.at[:, lanes], out_hbm.at[:, lanes], sems.at[part]))
        copies[-1].start()
    for copy in copies:
        copy.wait()


def body(tokens, w_qkv, w_out, conv_weight):
    groups = lax.axis_size("head")
    same_core = [[2 * chip + core for chip in range(CHIPS)] for core in range(2)]
    swap = [(i, i ^ 1) for i in range(2 * CHIPS)]
    onward = [(2 * chip + 1, 2 * chip + 2) for chip in range(CHIPS - 1)]
    onward += [(b, a) for a, b in onward]
    place = lax.axis_index("ctx").astype(jnp.int32)
    group = lax.axis_index("head").astype(jnp.int32).reshape(1)
    seg = ROWS // groups
    core = (place % 2).reshape(1)
    head_id = (place // (2 * CHIPS // HEADS)).reshape(1)

    def exchange(x):
        return lax.all_to_all(x, "ctx", 0, 0, tiled=True, axis_index_groups=same_core)

    tokens_other = lax.ppermute(tokens, "ctx", swap)
    own = call(
        landmarks_kernel,
        shaped((CHIPS, 16, 128), bf16),
        [
            pltpu.VMEM((ROWS, 1024), bf16),
            pltpu.VMEM((2, 1024, WIDTH), bf16),
            pltpu.VMEM((16, 128), f32),
            pltpu.SemaphoreType.DMA((6,)),
        ],
        specs=[HBM, HBM],
        flops=2 * 16 * 1024 * 512,
        moved=3 * MIB,
        limit=63,
    )(tokens, w_qkv)
    land = exchange(own)
    key, value_t, key_other, value_other, near, far = call(
        project_kernel,
        [shaped((ROWS, WIDTH), bf16), shaped((WIDTH, ROWS), bf16)] * 2
        + [shaped((HALF, WIDTH), bf16)] * 2,
        specs=[SMEM, VMEM, VMEM, VMEM],
        flops=4 * 1024 * 1024 * 512,
        moved=8 * MIB,
    )(core, tokens, tokens_other, w_qkv)
    land, key, value_t, near, far, key_other, value_other = lax.optimization_barrier(
        (land, key, value_t, near, far, key_other, value_other)
    )
    parts = call(
        scores_kernel,
        shaped((CHIPS, 16, 128), bf16),
        [pltpu.VMEM((CHIPS * 16, 128), f32)],
        n_in=5,
        flops=4 * 4 * 1024 * 256 * 256,
        moved=4 * MIB,
        exps=MIB,
    )(land, key, value_t, key_other, value_other)
    gathered = exchange(parts)
    land, parts = lax.optimization_barrier((land, parts))
    land_other = lax.ppermute(land, "ctx", swap)
    land_k, inverse = call(
        pinv_kernel,
        [shaped((M, WIDTH), bf16), shaped((M, M), f32)],
        [pltpu.VMEM((CHIPS * 32, 128), f32)],
        specs=[SMEM, SMEM, VMEM, VMEM],
        flops=24 * 3 * 2 * 256**3,
        moved=MIB // 2,
        exps=65536,
    )(core, head_id, land, land_other)
    late_tokens, late_w, inverse = lax.optimization_barrier((tokens, w_qkv, inverse))
    query = call(
        query_kernel,
        shaped((ROWS, WIDTH), bf16),
        n_in=2,
        flops=2 * 1024 * 1024 * 256,
        moved=4 * MIB,
    )(late_tokens, late_w)
    gathered, query = lax.optimization_barrier((gathered, query))
    gathered_other = lax.ppermute(gathered, "ctx", swap)
    mid_own = call(
        middle_kernel,
        shaped((CHIPS, 16, 128), bf16),
        specs=[SMEM] + [VMEM] * 3,
        flops=6 * 8 * 256 * 256,
        moved=MIB // 2,
    )(core, gathered, gathered_other, inverse)
    mids = exchange(mid_own)
    far = lax.ppermute(far, "ctx", onward)
    kernel_f = call(
        token_kernel,
        shaped((HEADS, M, ROWS), bf16),
        n_in=2,
        flops=4 * 2 * 1024 * 256 * 256,
        moved=3 * MIB,
        exps=MIB,
    )(land_k, query)
    far, kernel_f = lax.optimization_barrier((far, kernel_f))
    conv = call(
        conv_kernel,
        shaped((WIDTH, ROWS), f32),
        specs=[SMEM] + [VMEM] * 4,
        flops=2 * 512 * 768 * 512,
        moved=2 * MIB,
    )(core, value_t, near, far, conv_weight)
    mids, kernel_f, conv = lax.optimization_barrier((mids, kernel_f, conv))
    head_out = call(
        attend_kernel,
        [shaped((seg, WIDTH), bf16)] * groups,
        [pltpu.VMEM((ROWS, WIDTH), bf16)],
        specs=[SMEM] + [VMEM] * 3,
        flops=4 * 2 * 64 * 256 * 1024,
        moved=4 * MIB,
    )(group, mids, kernel_f, conv)
    arrived = [head_out[0]]
    for step in range(1, groups):
        ring = [(i, (i + step) % groups) for i in range(groups)]
        arrived.append(lax.ppermute(head_out[step], "head", ring))
    return call(
        output_kernel,
        shaped((seg, w_out.shape[1]), bf16),
        [
            pltpu.VMEM((seg, w_out.shape[0]), bf16),
            pltpu.VMEM((seg, w_out.shape[1]), bf16),
            pltpu.SemaphoreType.DMA((4,)),
        ],
        specs=[SMEM] + [VMEM] * (1 + groups),
        out_specs=HBM,
        flops=2 * 256 * 1024 * 1024,
        moved=3 * MIB,
    )(group, w_out, *arrived)


def solution(mesh):
    placed = (P("ctx", None), P(None, None, "head"), P(), P("head", None))
    return jax.shard_map(
        body, mesh=mesh, in_specs=placed, out_specs=P(("ctx", "head"), None), check_vma=False
    )
```

time: 80.1 us -> 74.9 us (0.935)
  waiting for transfers between devices: 17.5 us -> 13.2 us
  starting transfers between devices: 35.9 us -> 34.4 us
    ppermute x3, waiting for transfers between devices: 5 us -> 3.62 us  [body(): arrived.append(lax.ppermute(head_out[step], 'head', ring))]
    ppermute x1, waiting for transfers between devices: 1.35 us -> 0.01 us  [body(): land_other = lax.ppermute(land, 'ctx', swap)]
    ppermute x3 -> x2, waiting for transfers between devices: 2.44 us -> 1.35 us  [the longest x1 1.35 us: body(): gathered_other = lax.ppermute(gathered, 'ctx', swap)]
    ppermute x1, waiting for transfers between devices: 2.4 us -> 1.42 us  [body(): far = lax.ppermute(far, 'ctx', onward)]
    ppermute x1, starting transfers between devices: 4.67 us -> 3.77 us  [body(): far = lax.ppermute(far, 'ctx', onward)]
    unnamed x12 -> x16, local copies, waits for them, and re-layouts: 4.83 us -> 4.06 us
  transfers between devices with their start and end apart: 11 -> 10, of which waited for: 8 -> 8; matrix products, arithmetic and copies ran while one was open for 0% -> 0% of each run, Pallas kernels for 14% -> 21%
where the time goes in v3:
time: 74.9 us; the launch traced here: 74 us
  starting transfers between devices  34.4 us (46%)
  Pallas kernels  22 us (29%)
  waiting for transfers between devices  13.2 us (18%)
  local copies, waits for them, and re-layouts  4.06 us (5%)
    all_to_all x3, starting transfers between devices, exchange(): lax.all_to_all(x, 'ctx', 0, 0, tiled=True, axis_index_groups=same_core)  24.7 us
    all_to_all x3, waiting for transfers between devices, exchange(): lax.all_to_all(x, 'ctx', 0, 0, tiled=True, axis_index_groups=same_core)  6.82 us
    ppermute x3, starting transfers between devices, body(): arrived.append(lax.ppermute(head_out[step], 'head', ring))  5.9 us
    pallas_call x1, Pallas kernels, body(): call(pinv_kernel, [shaped((M, WIDTH), bf16), shaped((M, M), f32)], [pltpu...  5.1 us
    unnamed x16, local copies, waits for them, and re-layouts  4.06 us
    pallas_call x1, Pallas kernels, body(): call(project_kernel, [shaped((ROWS, WIDTH), bf16), shaped((WIDTH, ROWS),...  3.97 us
    ppermute x1, starting transfers between devices, body(): far = lax.ppermute(far, 'ctx', onward)  3.77 us
    ppermute x3, waiting for transfers between devices, body(): arrived.append(lax.ppermute(head_out[step], 'head', ring))  3.62 us
  transfers between devices with their start and end apart: 10, of which 8 were waited for; matrix products, arithmetic and copies ran while one was open for 0% of the time, Pallas kernels for 21%

profile of v3, /device:TPU:2, one launch (start us, length us, event | category | flops | bytes accessed | tf_op | source)
XLA Modules:
  0.0 74.0 jit_solution(12077308252472301409)
XLA Ops:
  0.0 2.9 %shard_map.46 = bf16[32,16,128]{2,1,0:T(8,128)(2,1)} custom-call(bf16[1024,1024]{1,0:T(8,128)(2,1)} %tok_ref, bf16[3,1024,256]{2,1,0:T(8,128)(2,1)} %w_ref.3), custom_call_target="tpu_custom_call" | custom-call | flops 16777216 | bytes 3145728 | tf_op jit(solution)/shard_map/pallas_call | solution.py:309
  2.9 11.6 %all-to-all-start = ((bf16[32,16,128]{2,1,0:T(8,128)(2,1)}), bf16[32,16,128]{2,1,0:T(8,128)(2,1)S(1)}, u32[]{:S(2)}, u32[]{:S(2)}) async-start(bf16[32,16,128]{2,1,0:T(8,128)(2,1)} %shard_map.46), calls=%async_computation | async-start | bytes 262144 | tf_op jit(solution)/shard_map/all_to_all | solution.py:306
  14.6 0.0 copy-start
  14.6 1.6 %copy-done = bf16[1024,1024]{1,0:T(8,128)(2,1)S(1)} copy-done((bf16[1024,1024]{1,0:T(8,128)(2,1)S(1)}, bf16[1024,1024]{1,0:T(8,128)(2,1)}, u32[]{:S(2)}) %copy-start) | copy-done | bytes 2097176
  16.2 1.4 %copy-done.2 = bf16[3,1024,256]{2,1,0:T(8,128)(2,1)S(1)} copy-done((bf16[3,1024,256]{2,1,0:T(8,128)(2,1)S(1)}, bf16[3,1024,256]{2,1,0:T(8,128)(2,1)}, u32[]{:S(2)}) %copy-start.2) | copy-done | bytes 1572888
  17.6 4.0 %shard_map.47 = (bf16[1024,256]{1,0:T(8,128)(2,1)S(1)}, bf16[256,1024]{1,0:T(8,128)(2,1)S(1)}, bf16[1024,256]{1,0:T(8,128)(2,1)S(1)}, bf16[256,1024]{1,0:T(8,128...) custom-call(s32[1]{0:T(128)} %bitcast.1.core_ref, bf16[1024,1024]{1,0:T(8,128)(2,1)S(1)} %copy-done, ...), custom_call_target="tpu_custom_call" | custom-call | flops 2147483648 | bytes 8388608 | tf_op jit(solution)/shard_map/pallas_call | solution.py:324
  21.6 0.0 copy-start.5
  21.6 2.7 %all-to-all-done.land_ref.own_ref = bf16[32,16,128]{2,1,0:T(8,128)(2,1)S(1)} async-done(((bf16[32,16,128]{2,1,0:T(8,128)(2,1)}), bf16[32,16,128]{2,1,0:T(8,128)(2,1)S(1)}, u32[]{:S(2)}, u32[]{:S(2)}) %all-to-all-start) | async-done | bytes 131104 | tf_op jit(solution)/shard_map/all_to_all | solution.py:306
  24.3 3.3 %shard_map.48 = bf16[32,16,128]{2,1,0:T(8,128)(2,1)} custom-call(bf16[32,16,128]{2,1,0:T(8,128)(2,1)S(1)} %all-to-all-done.land_ref.own_ref, bf16[1024,256]{1,0:T(8,128)(2,1)S(1)} %get-tuple-element.42.k_ref, bf16[256,1024]{1,0:T(8,128)(2,1)S(1)} %get-tuple-element.43.vt_ref, bf16[1024,256]{1,0:T(8,128)(2,1)S(1)} %get-tuple-element.44.k2_ref, ...), custom_call_target="tpu_custom_call" | custom-call | flops 1073741824 | bytes 4194304 | tf_op jit(solution)/shard_map/pallas_call | solution.py:335
  27.6 7.1 %all-to-all-start.1 = ((bf16[32,16,128]{2,1,0:T(8,128)(2,1)}), bf16[32,16,128]{2,1,0:T(8,128)(2,1)S(1)}, u32[]{:S(2)}, u32[]{:S(2)}) async-start(bf16[32,16,128]{2,1,0:T(8,128)(2,1)} %shard_map.48), calls=%async_computation.1 | async-start | bytes 262144 | tf_op jit(solution)/shard_map/all_to_all | solution.py:306
  34.7 0.0 copy-start.1
  34.7 0.0 copy-start.3
  34.7 5.1 %shard_map.49 = (bf16[256,256]{1,0:T(8,128)(2,1)S(1)}, f32[256,256]{1,0:T(8,128)S(1)}) custom-call(s32[1]{0:T(128)} %bitcast.1.core_ref, s32[1]{0:T(128)} %bitcast.2.head_ref, bf16[32,16,128]{2,1,0:T(8,128)(2,1)S(1)} %all-to-all-done.land_ref.own_ref, bf16[32,16,128]{2,1,0:T(8,128)(2,1)S(1)} %collective-permute-done.1.other_ref), custom_call_target="tpu_custom_call" | custom-call | flops 2415919104 | bytes 524288 | tf_op jit(solution)/shard_map/pallas_call | solution.py:347
  39.8 0.7 shard_map.50.q_ref
  40.5 3.9 %all-to-all-done.1.own_ref = bf16[32,16,128]{2,1,0:T(8,128)(2,1)S(1)} async-done(((bf16[32,16,128]{2,1,0:T(8,128)(2,1)}), bf16[32,16,128]{2,1,0:T(8,128)(2,1)S(1)}, u32[]{:S(2)}, u32[]{:S(2)}) %all-to-all-start.1) | async-done | bytes 131104 | tf_op jit(solution)/shard_map/all_to_all | solution.py:306
  44.4 1.3 %collective-permute-done.2.other_ref = bf16[32,16,128]{2,1,0:T(8,128)(2,1)S(1)} collective-permute-done((bf16[32,16,128]{2,1,0:T(8,128)(2,1)S(1)}, bf16[32,16,128]{2,1,0:T(8,128)(2,1)S(1)}, u32[]{:S(2)}, u32[]{:S(2)}) %collective-permute-start.2) | collective-permute-done | bytes 131104 | tf_op jit(solution)/shard_map/ppermute | solution.py:365
  45.8 1.0 %shard_map.51 = bf16[32,16,128]{2,1,0:T(8,128)(2,1)} custom-call(s32[1]{0:T(128)} %bitcast.1.core_ref, bf16[32,16,128]{2,1,0:T(8,128)(2,1)S(1)} %all-to-all-done.1.own_ref, bf16[32,16,128]{2,1,0:T(8,128)(2,1)S(1)} %collective-permute-done.2.other_ref, f32[256,256]{1,0:T(8,128)S(1)} %get-tuple-element.51.w_ref), custom_call_target="tpu_custom_call" | custom-call | flops 3145728 | bytes 524288 | tf_op jit(solution)/shard_map/pallas_call | solution.py:366
  46.8 6.0 %all-to-all-start.2 = ((bf16[32,16,128]{2,1,0:T(8,128)(2,1)}), bf16[32,16,128]{2,1,0:T(8,128)(2,1)S(1)}, u32[]{:S(2)}, u32[]{:S(2)}) async-start(bf16[32,16,128]{2,1,0:T(8,128)(2,1)} %shard_map.51), calls=%async_computation.2 | async-start | bytes 262144 | tf_op jit(solution)/shard_map/all_to_all | solution.py:306
  52.8 3.8 %collective-permute-start.3 = (bf16[16,256]{1,0:T(8,128)(2,1)S(1)}, bf16[16,256]{1,0:T(8,128)(2,1)S(1)}, u32[]{:S(2)}, u32[]{:S(2)}) collective-permute-start(bf16[16,256]{1,0:T(8,128)(2,1)S(1)} %get-tuple-element.52), channel_id=1, source_target_pairs={{4,8},{12,16},{20,24},{28,32},{36,40},{44,48},{52,56},{60,64},{68,... | collective-permute-start | bytes 24584 | tf_op jit(solution)/shard_map/ppermute | solution.py:374
  56.6 1.9 %shard_map.52.kf_ref = bf16[4,256,1024]{2,1,0:T(8,128)(2,1)S(1)} custom-call(bf16[256,256]{1,0:T(8,128)(2,1)S(1)} %get-tuple-element.53.lk_ref, bf16[1024,256]{1,0:T(8,128)(2,1)S(1)} %shard_map.50.q_ref), custom_call_target="tpu_custom_call" | custom-call | flops 536870912 | bytes 3145728 | tf_op jit(solution)/shard_map/pallas_call | solution.py:375
  58.5 1.4 %collective-permute-done.3.far_ref = bf16[16,256]{1,0:T(8,128)(2,1)S(1)} collective-permute-done((bf16[16,256]{1,0:T(8,128)(2,1)S(1)}, bf16[16,256]{1,0:T(8,128)(2,1)S(1)}, u32[]{:S(2)}, u32[]{:S(2)}) %collective-permute-start.3) | collective-permute-done | bytes 8224 | tf_op jit(solution)/shard_map/ppermute | solution.py:374
  59.9 1.0 %copy-done.6 = bf16[256,1024]{1,0:T(8,128)(2,1)S(1)} copy-done((bf16[256,1024]{1,0:T(8,128)(2,1)S(1)}, bf16[256,1024]{1,0:T(8,128)(2,1)}, u32[]{:S(2)}) %copy-start.6) | copy-done | bytes 524312
  60.9 1.1 %shard_map.53.conv_ref = f32[256,1024]{1,0:T(8,128)S(1)} custom-call(s32[1]{0:T(128)} %bitcast.1.core_ref, bf16[256,1024]{1,0:T(8,128)(2,1)S(1)} %copy-done.6, bf16[16,256]{1,0:T(8,128)(2,1)S(1)} %get-tuple-element.56.near_ref, bf16[16,256]{1,0:T(8,128)(2,1)S(1)} %collective-permute-done.3.far_ref, f32[4,33]{1,0:T(4,128)S(1)} %copy-done.7), custom_call_target="tpu_custom_call" | custom-call | flops 402653184 | bytes 2097152 | tf_op jit(solution)/shard_map/pallas_call | solution.py:384
  62.0 0.2 all-to-all-done.2.mid_ref
  62.2 0.6 shard_map.54
  62.9 1.7 %collective-permute-start.4 = (bf16[256,256]{1,0:T(8,128)(2,1)S(1)}, bf16[256,256]{1,0:T(8,128)(2,1)S(1)}, u32[]{:S(2)}, u32[]{:S(2)}) collective-permute-start(bf16[256,256]{1,0:T(8,128)(2,1)S(1)} %get-tuple-element.62), channel_id=1, source_target_pairs={{0,1},{1,2},{2,3},{3,0},{4,5},{5,6},{6,7},{7,4},{8,9},{9,10},{10,1... | collective-permute-start | bytes 393224 | tf_op jit(solution)/shard_map/ppermute | solution.py:403
  64.5 2.9 %collective-permute-start.5 = (bf16[256,256]{1,0:T(8,128)(2,1)S(1)}, bf16[256,256]{1,0:T(8,128)(2,1)S(1)}, u32[]{:S(2)}, u32[]{:S(2)}) collective-permute-start(bf16[256,256]{1,0:T(8,128)(2,1)S(1)} %get-tuple-element.63), channel_id=1, source_target_pairs={{0,2},{1,3},{2,0},{3,1},{4,6},{5,7},{6,4},{7,5},{8,10},{9,11},{10,... | collective-permute-start | bytes 393224 | tf_op jit(solution)/shard_map/ppermute | solution.py:403
  67.4 1.3 %collective-permute-start.6 = (bf16[256,256]{1,0:T(8,128)(2,1)S(1)}, bf16[256,256]{1,0:T(8,128)(2,1)S(1)}, u32[]{:S(2)}, u32[]{:S(2)}) collective-permute-start(bf16[256,256]{1,0:T(8,128)(2,1)S(1)} %get-tuple-element.64), channel_id=1, source_target_pairs={{0,3},{1,0},{2,1},{3,2},{4,7},{5,4},{6,5},{7,6},{8,11},{9,8},{10,9... | collective-permute-start | bytes 393224 | tf_op jit(solution)/shard_map/ppermute | solution.py:403
  68.8 1.8 %collective-permute-done.4.refs_1_ = bf16[256,256]{1,0:T(8,128)(2,1)S(1)} collective-permute-done((bf16[256,256]{1,0:T(8,128)(2,1)S(1)}, bf16[256,256]{1,0:T(8,128)(2,1)S(1)}, u32[]{:S(2)}, u32[]{:S(2)}) %collective-permute-start.4) | collective-permute-done | bytes 131104 | tf_op jit(solution)/shard_map/ppermute | solution.py:403
  70.5 1.5 %collective-permute-done.5.refs_2_ = bf16[256,256]{1,0:T(8,128)(2,1)S(1)} collective-permute-done((bf16[256,256]{1,0:T(8,128)(2,1)S(1)}, bf16[256,256]{1,0:T(8,128)(2,1)S(1)}, u32[]{:S(2)}, u32[]{:S(2)}) %collective-permute-start.5) | collective-permute-done | bytes 131104 | tf_op jit(solution)/shard_map/ppermute | solution.py:403
  72.0 0.3 collective-permute-done.6.refs_3_
  72.4 1.5 %shard_map.55 = bf16[256,1024]{1,0:T(8,128)(2,1)} custom-call(s32[1]{0:T(128)} %bitcast.group_ref, bf16[1024,1024]{1,0:T(8,128)(2,1)S(1)} %copy-done.4, bf16[256,256]{1,0:T(8,128)(2,1)S(1)} %get-tuple-element.61.refs_0_, bf16[256,256]{1,0:T(8,128)(2,1)S(1)} %collective-permute-done.4.refs_1_, bf16[256,256]{1,0:T(8,128)(2,1)S(1)} %collective-permute-done.5.refs_2_, ...), custom_call_target="tpu_custom_call" | custom-call | flops 536870912 | bytes 3145728 | tf_op jit(solution)/shard_map/pallas_call | solution.py:404
  (14 shorter events, 0.0 us)
Async XLA Ops:
  0.0 14.6 %collective-permute-start = (bf16[1024,1024]{1,0:T(8,128)(2,1)}, bf16[1024,1024]{1,0:T(8,128)(2,1)}, u32[]{:S(2)}, u32[]{:S(2)}) collective-permute-start(bf16[1024,1024]{1,0:T(8,128)(2,1)} %tok_ref), channel_id=1, source_target_pairs={{0,4},{4,0},{8,12},{12,8},{16,20},{20,16},{24,28},{28,24},{32,36},... | collective-permute-start | bytes 6291464 | tf_op jit(solution)/shard_map/ppermute | solution.py:308
  2.9 21.4 %all-to-all-start = ((bf16[32,16,128]{2,1,0:T(8,128)(2,1)}), bf16[32,16,128]{2,1,0:T(8,128)(2,1)S(1)}, u32[]{:S(2)}, u32[]{:S(2)}) async-start(bf16[32,16,128]{2,1,0:T(8,128)(2,1)} %shard_map.46), calls=%async_computation | async-start | bytes 262144 | tf_op jit(solution)/shard_map/all_to_all | solution.py:306
  14.6 1.6 %copy-start = (bf16[1024,1024]{1,0:T(8,128)(2,1)S(1)}, bf16[1024,1024]{1,0:T(8,128)(2,1)}, u32[]{:S(2)}) copy-start(bf16[1024,1024]{1,0:T(8,128)(2,1)} %tok_ref) | copy-start | bytes 6291460
  16.2 1.4 %copy-start.2 = (bf16[3,1024,256]{2,1,0:T(8,128)(2,1)S(1)}, bf16[3,1024,256]{2,1,0:T(8,128)(2,1)}, u32[]{:S(2)}) copy-start(bf16[3,1024,256]{2,1,0:T(8,128)(2,1)} %w_ref.3) | copy-start | bytes 4718596
  21.6 6.0 %copy-start.5 = (bf16[256,1024]{1,0:T(8,128)(2,1)}, bf16[256,1024]{1,0:T(8,128)(2,1)S(1)}, u32[]{:S(2)}) copy-start(bf16[256,1024]{1,0:T(8,128)(2,1)S(1)} %get-tuple-element.43.vt_ref) | copy-start | bytes 1572868
  27.6 7.1 %collective-permute-start.1 = (bf16[32,16,128]{2,1,0:T(8,128)(2,1)S(1)}, bf16[32,16,128]{2,1,0:T(8,128)(2,1)S(1)}, u32[]{:S(2)}, u32[]{:S(2)}) collective-permute-start(bf16[32,16,128]{2,1,0:T(8,128)(2,1)S(1)} %all-to-all-done.land_ref.own_ref), channel_id=1, source_target_pairs={{0,4},{4,0},{8,12},{12,8},{16,20},{20,16},{24,28},{28,24},{32,36},... | collective-permute-start | bytes 393224 | tf_op jit(solution)/shard_map/ppermute | solution.py:346
  27.6 16.8 %all-to-all-start.1 = ((bf16[32,16,128]{2,1,0:T(8,128)(2,1)}), bf16[32,16,128]{2,1,0:T(8,128)(2,1)S(1)}, u32[]{:S(2)}, u32[]{:S(2)}) async-start(bf16[32,16,128]{2,1,0:T(8,128)(2,1)} %shard_map.48), calls=%async_computation.1 | async-start | bytes 262144 | tf_op jit(solution)/shard_map/all_to_all | solution.py:306
  34.7 5.1 %copy-start.1 = (bf16[1024,1024]{1,0:T(8,128)(2,1)S(1)}, bf16[1024,1024]{1,0:T(8,128)(2,1)}, u32[]{:S(2)}) copy-start(bf16[1024,1024]{1,0:T(8,128)(2,1)} %tok_ref) | copy-start | bytes 6291460
  34.7 5.1 %copy-start.3 = (bf16[3,1024,256]{2,1,0:T(8,128)(2,1)S(1)}, bf16[3,1024,256]{2,1,0:T(8,128)(2,1)}, u32[]{:S(2)}) copy-start(bf16[3,1024,256]{2,1,0:T(8,128)(2,1)} %w_ref.3) | copy-start | bytes 4718596
  40.5 19.4 %copy-start.7 = (f32[4,33]{1,0:T(4,128)S(1)}, f32[4,33]{1,0:T(4,128)}, u32[]{:S(2)}) copy-start(f32[4,33]{1,0:T(4,128)} %cw_ref.1) | copy-start | bytes 1588
  44.4 1.3 %collective-permute-start.2 = (bf16[32,16,128]{2,1,0:T(8,128)(2,1)S(1)}, bf16[32,16,128]{2,1,0:T(8,128)(2,1)S(1)}, u32[]{:S(2)}, u32[]{:S(2)}) collective-permute-start(bf16[32,16,128]{2,1,0:T(8,128)(2,1)S(1)} %all-to-all-done.1.own_ref), channel_id=1, source_target_pairs={{0,4},{4,0},{8,12},{12,8},{16,20},{20,16},{24,28},{28,24},{32,36},... | collective-permute-start | bytes 393224 | tf_op jit(solution)/shard_map/ppermute | solution.py:365
  46.8 15.5 %all-to-all-start.2 = ((bf16[32,16,128]{2,1,0:T(8,128)(2,1)}), bf16[32,16,128]{2,1,0:T(8,128)(2,1)S(1)}, u32[]{:S(2)}, u32[]{:S(2)}) async-start(bf16[32,16,128]{2,1,0:T(8,128)(2,1)} %shard_map.51), calls=%async_computation.2 | async-start | bytes 262144 | tf_op jit(solution)/shard_map/all_to_all | solution.py:306
  52.8 7.1 %collective-permute-start.3 = (bf16[16,256]{1,0:T(8,128)(2,1)S(1)}, bf16[16,256]{1,0:T(8,128)(2,1)S(1)}, u32[]{:S(2)}, u32[]{:S(2)}) collective-permute-start(bf16[16,256]{1,0:T(8,128)(2,1)S(1)} %get-tuple-element.52), channel_id=1, source_target_pairs={{4,8},{12,16},{20,24},{28,32},{36,40},{44,48},{52,56},{60,64},{68,... | collective-permute-start | bytes 24584 | tf_op jit(solution)/shard_map/ppermute | solution.py:374
  59.9 1.0 %copy-start.6 = (bf16[256,1024]{1,0:T(8,128)(2,1)S(1)}, bf16[256,1024]{1,0:T(8,128)(2,1)}, u32[]{:S(2)}) copy-start(bf16[256,1024]{1,0:T(8,128)(2,1)} %copy-done.5) | copy-start | bytes 1572868
  62.2 10.1 %copy-start.4 = (bf16[1024,1024]{1,0:T(8,128)(2,1)S(1)}, bf16[1024,1024]{1,0:T(8,128)(2,1)}, u32[]{:S(2)}) copy-start(bf16[1024,1024]{1,0:T(8,128)(2,1)} %w_ref.4) | copy-start | bytes 6291460
  62.9 7.7 %collective-permute-start.4 = (bf16[256,256]{1,0:T(8,128)(2,1)S(1)}, bf16[256,256]{1,0:T(8,128)(2,1)S(1)}, u32[]{:S(2)}, u32[]{:S(2)}) collective-permute-start(bf16[256,256]{1,0:T(8,128)(2,1)S(1)} %get-tuple-element.62), channel_id=1, source_target_pairs={{0,1},{1,2},{2,3},{3,0},{4,5},{5,6},{6,7},{7,4},{8,9},{9,10},{10,1... | collective-permute-start | bytes 393224 | tf_op jit(solution)/shard_map/ppermute | solution.py:403
  64.5 7.5 %collective-permute-start.5 = (bf16[256,256]{1,0:T(8,128)(2,1)S(1)}, bf16[256,256]{1,0:T(8,128)(2,1)S(1)}, u32[]{:S(2)}, u32[]{:S(2)}) collective-permute-start(bf16[256,256]{1,0:T(8,128)(2,1)S(1)} %get-tuple-element.63), channel_id=1, source_target_pairs={{0,2},{1,3},{2,0},{3,1},{4,6},{5,7},{6,4},{7,5},{8,10},{9,11},{10,... | collective-permute-start | bytes 393224 | tf_op jit(solution)/shard_map/ppermute | solution.py:403
  67.4 5.0 %collective-permute-start.6 = (bf16[256,256]{1,0:T(8,128)(2,1)S(1)}, bf16[256,256]{1,0:T(8,128)(2,1)S(1)}, u32[]{:S(2)}, u32[]{:S(2)}) collective-permute-start(bf16[256,256]{1,0:T(8,128)(2,1)S(1)} %get-tuple-element.64), channel_id=1, source_target_pairs={{0,3},{1,0},{2,1},{3,2},{4,7},{5,4},{6,5},{7,6},{8,11},{9,8},{10,9... | collective-permute-start | bytes 393224 | tf_op jit(solution)/shard_map/ppermute | solution.py:403

commit v4 on v3

--- a/solution.py
+++ b/solution.py
@@ -15,6 +15,7 @@
 CHIPS = 32
 ROWS = 1024
 SCALE = 0.125
+LOG2_E = 1.4426950408889634
 f32 = jnp.float32
 bf16 = jnp.bfloat16
 INTERPRET = False
@@ -107,17 +108,51 @@
     out_ref[...] = jnp.broadcast_to(rows_ref[...].astype(bf16)[None], out_ref.shape)
 
 
-def project_kernel(core_ref, own_ref, other_ref, w_ref, k_ref, vt_ref, k2_ref, vt2_ref, near_ref, far_ref):
+def project_kernel(
+    core_ref,
+    own_hbm,
+    other_hbm,
+    w_hbm,
+    k_ref,
+    vt_ref,
+    k2_ref,
+    vt2_ref,
+    near_ref,
+    far_ref,
+    tok_ref,
+    w_ref,
+    sems,
+):
+    cut = ROWS // 4
+    loads = [pltpu.make_async_copy(w_hbm.at[1 + c], w_ref.at[c], sems.at[8 + c]) for c in range(2)]
+    copies = [
+        pltpu.make_async_copy(
+            source.at[s * cut : (s + 1) * cut, :],
+            tok_ref.at[side, s * cut : (s + 1) * cut, :],
+            sems.at[4 * side + s],
+        )
+        for side, source in enumerate((own_hbm, other_hbm))
+        for s in range(4)
+    ]
+    for copy in loads + copies:
+        copy.start()
+    for copy in loads:
+        copy.wait()
     edges = []
-    for tok_ref, key_ref, value_ref in ((own_ref, k_ref, vt_ref), (other_ref, k2_ref, vt2_ref)):
-        tok = tok_ref[...]
-        key_ref[...] = dot_nn(tok, w_ref[1]).astype(bf16)
-        value = dot_nn(tok, w_ref[2]).astype(bf16)
-        value_ref[...] = value.T
-        edges.append((value[:HALF].astype(f32), value[ROWS - HALF :].astype(f32)))
+    for side, (key_ref, value_ref) in enumerate(((k_ref, vt_ref), (k2_ref, vt2_ref))):
+        for s in range(4):
+            copies[4 * side + s].wait()
+            rows = slice(s * cut, (s + 1) * cut)
+            tok = tok_ref[side, rows, :]
+            key_ref[rows, :] = dot_nn(tok, w_ref[0]).astype(bf16)
+            value = dot_nn(tok, w_ref[1]).astype(bf16)
+            value_ref[:, rows] = value.T
+            edges.append(value)
     is_first = core_ref[0] == 0
-    near_ref[...] = jnp.where(is_first, edges[1][0], edges[1][1]).astype(bf16)
-    far_ref[...] = jnp.where(is_first, edges[0][0], edges[0][1]).astype(bf16)
+    first, last = edges[0][:HALF].astype(f32), edges[3][cut - HALF :].astype(f32)
+    far_ref[...] = jnp.where(is_first, first, last).astype(bf16)
+    first, last = edges[4][:HALF].astype(f32), edges[7][cut - HALF :].astype(f32)
+    near_ref[...] = jnp.where(is_first, first, last).astype(bf16)
 
 
 def query_kernel(tok_ref, w_ref, q_ref):
@@ -145,14 +180,18 @@
         for pair in range(2)
     ]
     found = []
-    for key_ref, value_ref in ((k_ref, vt_ref), (k2_ref, vt2_ref)):
-        for pair in range(2):
-            scores = dot_nt(key_ref[...], own[pair])
-            top = jnp.max(scores, axis=0, keepdims=True)
-            expo = jnp.exp((scores - top) * SCALE)
-            total = jnp.sum(expo, axis=0, keepdims=True)
-            rows = slice(pair * 128, pair * 128 + 128)
-            found.append((top, total, dot_nn(value_ref[rows, :], expo.astype(bf16))))
+    keys, values = (k_ref, k2_ref), (vt_ref, vt2_ref)
+    ahead = dot_nt(keys[0][...], own[0])
+    for step in range(4):
+        side, pair = step // 2, step % 2
+        scores = ahead
+        if step < 3:
+            ahead = dot_nt(keys[(step + 1) // 2][...], own[1 - pair])
+        top = jnp.max(scores, axis=0, keepdims=True)
+        expo = jnp.exp2((scores - top) * (SCALE * LOG2_E))
+        total = jnp.sum(expo, axis=0, keepdims=True)
+        rows = slice(pair * 128, pair * 128 + 128)
+        found.append((top, total, dot_nn(values[side][rows, :], expo.astype(bf16))))
     each = CHIPS // HEADS
     for pair in range(2):
         top_a, total_a, sum_a = found[pair]
@@ -203,18 +242,18 @@
     w_ref[...] = approx
 
 
+def reduce_kernel(parts_ref, out_ref):
+    parts = parts_ref[...].astype(f32)
+    level = (parts[:, 8] + parts[:, 9]) + parts[:, 10]
+    weight = jnp.exp(level - jnp.max(level, axis=0, keepdims=True))
+    weight = weight / jnp.sum(weight, axis=0, keepdims=True)
+    out_ref[...] = jnp.sum(parts[:, 0:8] * weight[:, None, :], axis=0)
+
+
 def middle_kernel(core_ref, own_ref, other_ref, w_ref, out_ref):
-    sides = []
-    for ref in (own_ref, other_ref):
-        parts = ref[...].astype(f32)
-        level = (parts[:, 8] + parts[:, 9]) + parts[:, 10]
-        weight = jnp.exp(level - jnp.max(level, axis=0, keepdims=True))
-        weight = weight / jnp.sum(weight, axis=0, keepdims=True)
-        sides.append(jnp.sum(parts[:, 0:8] * weight[:, None, :], axis=0))
+    own, other = own_ref[...], other_ref[...]
     is_first = core_ref[0] == 0
-    bv = jnp.concatenate(
-        [jnp.where(is_first, sides[0], sides[1]), jnp.where(is_first, sides[1], sides[0])], axis=1
-    )
+    bv = jnp.concatenate([jnp.where(is_first, own, other), jnp.where(is_first, other, own)], axis=1)
     mid = dot_wide(split_2(bv), split_2(w_ref[...]))
     rows = jnp.concatenate([mid[:, :128], mid[:, 128:]], axis=0)
     out_ref[...] = jnp.broadcast_to(rows.astype(bf16)[None], out_ref.shape)
@@ -226,8 +265,8 @@
     for head in range(HEADS):
         own = jnp.where(head_mask(head), lk, 0.0).astype(bf16)
         scores = dot_nt(own, query)
-        expo = jnp.exp((scores - jnp.max(scores, axis=0, keepdims=True)) * SCALE)
-        out_ref[head] = (expo / jnp.sum(expo, axis=0, keepdims=True)).astype(bf16)
+        expo = jnp.exp2((scores - jnp.max(scores, axis=0, keepdims=True)) * (SCALE * LOG2_E))
+        out_ref[head] = (expo * (1.0 / jnp.sum(expo, axis=0, keepdims=True))).astype(bf16)
 
 
 def conv_kernel(core_ref, vt_ref, near_ref, far_ref, cw_ref, out_ref):
@@ -325,7 +364,13 @@
         project_kernel,
         [shaped((ROWS, WIDTH), bf16), shaped((WIDTH, ROWS), bf16)] * 2
         + [shaped((HALF, WIDTH), bf16)] * 2,
-        specs=[SMEM, VMEM, VMEM, VMEM],
+        [
+            pltpu.VMEM((2, ROWS, 1024), bf16),
+            pltpu.VMEM((2, 1024, WIDTH), bf16),
+            pltpu.SemaphoreType.DMA((10,)),
+        ],
+        specs=[SMEM, HBM, HBM, HBM],
+        limit=51,
         flops=4 * 1024 * 1024 * 512,
         moved=8 * MIB,
     )(core, tokens, tokens_other, w_qkv)
@@ -362,14 +407,17 @@
         moved=4 * MIB,
     )(late_tokens, late_w)
     gathered, query = lax.optimization_barrier((gathered, query))
-    gathered_other = lax.ppermute(gathered, "ctx", swap)
+    reduced = call(
+        reduce_kernel, shaped((8, 128), f32), flops=32 * 8 * 128 * 2, moved=MIB // 8
+    )(gathered)
+    reduced_other = lax.ppermute(reduced, "ctx", swap)
     mid_own = call(
         middle_kernel,
         shaped((CHIPS, 16, 128), bf16),
         specs=[SMEM] + [VMEM] * 3,
         flops=6 * 8 * 256 * 256,
         moved=MIB // 2,
-    )(core, gathered, gathered_other, inverse)
+    )(core, reduced, reduced_other, inverse)
     mids = exchange(mid_own)
     far = lax.ppermute(far, "ctx", onward)
     kernel_f = call(

time: 74.9 us -> 72 us (0.961)
  local copies, waits for them, and re-layouts: 4.06 us -> 1.07 us
  waiting for transfers between devices: 13.2 us -> 14.8 us
  starting transfers between devices: 34.4 us -> 32.9 us
    unnamed x16 -> x12, local copies, waits for them, and re-layouts: 4.06 us -> 1.07 us
    all_to_all x3, starting transfers between devices: 24.7 us -> 23.1 us  [exchange(): lax.all_to_all(x, 'ctx', 0, 0, tiled=True, axis_index_groups=same_core)]
    all_to_all x3, waiting for transfers between devices: 6.82 us -> 8.39 us  [exchange(): lax.all_to_all(x, 'ctx', 0, 0, tiled=True, axis_index_groups=same_core)]
    pallas_call x1, Pallas kernels: 3.97 us -> 5.42 us  [body(): call(project_kernel, [shaped((ROWS, WIDTH), bf16), shaped((WIDTH, ROWS),...]
    pallas_call x1, Pallas kernels: 3.27 us -> 2.32 us  [body(): call(scores_kernel, shaped((CHIPS, 16, 128), bf16), [pltpu.VMEM((CHIPS *...]
  transfers between devices with their start and end apart: 10 -> 10, of which waited for: 8 -> 8; matrix products, arithmetic and copies ran while one was open for 0% -> 0% of each run, Pallas kernels for 21% -> 24%
where the time goes in v4:
time: 72 us; the launch traced here: 71.3 us
  starting transfers between devices  32.9 us (46%)
  Pallas kernels  22.2 us (31%)
  waiting for transfers between devices  14.8 us (21%)
  local copies, waits for them, and re-layouts  1.07 us (1%)
    all_to_all x3, starting transfers between devices, exchange(): lax.all_to_all(x, 'ctx', 0, 0, tiled=True, axis_index_groups=same_core)  23.1 us
    all_to_all x3, waiting for transfers between devices, exchange(): lax.all_to_all(x, 'ctx', 0, 0, tiled=True, axis_index_groups=same_core)  8.39 us
    ppermute x3, starting transfers between devices, body(): arrived.append(lax.ppermute(head_out[step], 'head', ring))  5.9 us
    pallas_call x1, Pallas kernels, body(): call(project_kernel, [shaped((ROWS, WIDTH), bf16), shaped((WIDTH, ROWS),...  5.42 us
    pallas_call x1, Pallas kernels, body(): call(pinv_kernel, [shaped((M, WIDTH), bf16), shaped((M, M), f32)], [pltpu...  5.1 us
    ppermute x1, starting transfers between devices, body(): far = lax.ppermute(far, 'ctx', onward)  3.79 us
    ppermute x3, waiting for transfers between devices, body(): arrived.append(lax.ppermute(head_out[step], 'head', ring))  3.62 us
    pallas_call x1, Pallas kernels, body(): call(landmarks_kernel, shaped((CHIPS, 16, 128), bf16), [pltpu.VMEM((ROWS,...  2.89 us
  transfers between devices with their start and end apart: 10, of which 8 were waited for; matrix products, arithmetic and copies ran while one was open for 0% of the time, Pallas kernels for 24%

profile of v4, /device:TPU:2, one launch (start us, length us, event | category | flops | bytes accessed | tf_op | source)
XLA Modules:
  0.0 71.3 jit_solution(7134169991265918756)
XLA Ops:
  0.0 2.9 %shard_map.46 = bf16[32,16,128]{2,1,0:T(8,128)(2,1)} custom-call(bf16[1024,1024]{1,0:T(8,128)(2,1)} %tok_ref, bf16[3,1024,256]{2,1,0:T(8,128)(2,1)} %w_ref.1), custom_call_target="tpu_custom_call" | custom-call | flops 16777216 | bytes 3145728 | tf_op jit(solution)/shard_map/pallas_call | solution.py:348
  2.9 11.6 %all-to-all-start = ((bf16[32,16,128]{2,1,0:T(8,128)(2,1)}), bf16[32,16,128]{2,1,0:T(8,128)(2,1)S(1)}, u32[]{:S(2)}, u32[]{:S(2)}) async-start(bf16[32,16,128]{2,1,0:T(8,128)(2,1)} %shard_map.46), calls=%async_computation | async-start | bytes 262144 | tf_op jit(solution)/shard_map/all_to_all | solution.py:345
  14.6 5.4 %shard_map.47 = (bf16[1024,256]{1,0:T(8,128)(2,1)S(1)}, bf16[256,1024]{1,0:T(8,128)(2,1)S(1)}, bf16[1024,256]{1,0:T(8,128)(2,1)S(1)}, bf16[256,1024]{1,0:T(8,128...) custom-call(s32[1]{0:T(128)} %bitcast.1.core_ref, bf16[1024,1024]{1,0:T(8,128)(2,1)} %tok_ref, ...), custom_call_target="tpu_custom_call" | custom-call | flops 2147483648 | bytes 8388608 | tf_op jit(solution)/shard_map/pallas_call | solution.py:363
  20.0 0.0 copy-start.3
  20.0 4.3 %all-to-all-done.land_ref.own_ref = bf16[32,16,128]{2,1,0:T(8,128)(2,1)S(1)} async-done(((bf16[32,16,128]{2,1,0:T(8,128)(2,1)}), bf16[32,16,128]{2,1,0:T(8,128)(2,1)S(1)}, u32[]{:S(2)}, u32[]{:S(2)}) %all-to-all-start) | async-done | bytes 131104 | tf_op jit(solution)/shard_map/all_to_all | solution.py:345
  24.3 2.3 %shard_map.48 = bf16[32,16,128]{2,1,0:T(8,128)(2,1)} custom-call(bf16[32,16,128]{2,1,0:T(8,128)(2,1)S(1)} %all-to-all-done.land_ref.own_ref, bf16[1024,256]{1,0:T(8,128)(2,1)S(1)} %get-tuple-element.42.k_ref, bf16[256,1024]{1,0:T(8,128)(2,1)S(1)} %get-tuple-element.43.vt_ref, bf16[1024,256]{1,0:T(8,128)(2,1)S(1)} %get-tuple-element.44.k2_ref, ...), custom_call_target="tpu_custom_call" | custom-call | flops 1073741824 | bytes 4194304 | tf_op jit(solution)/shard_map/pallas_call | solution.py:380
  26.6 5.5 %all-to-all-start.1 = ((bf16[32,16,128]{2,1,0:T(8,128)(2,1)}), bf16[32,16,128]{2,1,0:T(8,128)(2,1)S(1)}, u32[]{:S(2)}, u32[]{:S(2)}) async-start(bf16[32,16,128]{2,1,0:T(8,128)(2,1)} %shard_map.48), calls=%async_computation.1 | async-start | bytes 262144 | tf_op jit(solution)/shard_map/all_to_all | solution.py:345
  32.2 0.0 copy-start
  32.2 0.0 copy-start.1
  32.2 5.1 %shard_map.49 = (bf16[256,256]{1,0:T(8,128)(2,1)S(1)}, f32[256,256]{1,0:T(8,128)S(1)}) custom-call(s32[1]{0:T(128)} %bitcast.1.core_ref, s32[1]{0:T(128)} %bitcast.2.head_ref, bf16[32,16,128]{2,1,0:T(8,128)(2,1)S(1)} %all-to-all-done.land_ref.own_ref, bf16[32,16,128]{2,1,0:T(8,128)(2,1)S(1)} %collective-permute-done.1.other_ref), custom_call_target="tpu_custom_call" | custom-call | flops 2415919104 | bytes 524288 | tf_op jit(solution)/shard_map/pallas_call | solution.py:392
  37.3 0.7 shard_map.50.q_ref
  38.0 0.0 copy-start.5
  38.0 3.9 %all-to-all-done.1.parts_ref = bf16[32,16,128]{2,1,0:T(8,128)(2,1)S(1)} async-done(((bf16[32,16,128]{2,1,0:T(8,128)(2,1)}), bf16[32,16,128]{2,1,0:T(8,128)(2,1)S(1)}, u32[]{:S(2)}, u32[]{:S(2)}) %all-to-all-start.1) | async-done | bytes 131104 | tf_op jit(solution)/shard_map/all_to_all | solution.py:345
  41.9 0.1 shard_map.51.own_ref
  42.0 0.1 collective-permute-start.2
  42.1 1.2 %collective-permute-done.2.other_ref = f32[8,128]{1,0:T(8,128)S(1)} collective-permute-done((f32[8,128]{1,0:T(8,128)S(1)}, f32[8,128]{1,0:T(8,128)S(1)}, u32[]{:S(2)}, u32[]{:S(2)}) %collective-permute-start.2) | collective-permute-done | bytes 4128 | tf_op jit(solution)/shard_map/ppermute | solution.py:413
  43.3 0.8 %shard_map.52 = bf16[32,16,128]{2,1,0:T(8,128)(2,1)} custom-call(s32[1]{0:T(128)} %bitcast.1.core_ref, f32[8,128]{1,0:T(8,128)S(1)} %shard_map.51.own_ref, f32[8,128]{1,0:T(8,128)S(1)} %collective-permute-done.2.other_ref, f32[256,256]{1,0:T(8,128)S(1)} %get-tuple-element.51.w_ref), custom_call_target="tpu_custom_call" | custom-call | flops 3145728 | bytes 524288 | tf_op jit(solution)/shard_map/pallas_call | solution.py:414
  44.1 5.9 %all-to-all-start.2 = ((bf16[32,16,128]{2,1,0:T(8,128)(2,1)}), bf16[32,16,128]{2,1,0:T(8,128)(2,1)S(1)}, u32[]{:S(2)}, u32[]{:S(2)}) async-start(bf16[32,16,128]{2,1,0:T(8,128)(2,1)} %shard_map.52), calls=%async_computation.2 | async-start | bytes 262144 | tf_op jit(solution)/shard_map/all_to_all | solution.py:345
  50.0 3.8 %collective-permute-start.3 = (bf16[16,256]{1,0:T(8,128)(2,1)S(1)}, bf16[16,256]{1,0:T(8,128)(2,1)S(1)}, u32[]{:S(2)}, u32[]{:S(2)}) collective-permute-start(bf16[16,256]{1,0:T(8,128)(2,1)S(1)} %get-tuple-element.52), channel_id=1, source_target_pairs={{4,8},{12,16},{20,24},{28,32},{36,40},{44,48},{52,56},{60,64},{68,... | collective-permute-start | bytes 24584 | tf_op jit(solution)/shard_map/ppermute | solution.py:422
  53.8 1.7 %shard_map.53.kf_ref = bf16[4,256,1024]{2,1,0:T(8,128)(2,1)S(1)} custom-call(bf16[256,256]{1,0:T(8,128)(2,1)S(1)} %get-tuple-element.53.lk_ref, bf16[1024,256]{1,0:T(8,128)(2,1)S(1)} %shard_map.50.q_ref), custom_call_target="tpu_custom_call" | custom-call | flops 536870912 | bytes 3145728 | tf_op jit(solution)/shard_map/pallas_call | solution.py:423
  55.5 1.6 %collective-permute-done.3.far_ref = bf16[16,256]{1,0:T(8,128)(2,1)S(1)} collective-permute-done((bf16[16,256]{1,0:T(8,128)(2,1)S(1)}, bf16[16,256]{1,0:T(8,128)(2,1)S(1)}, u32[]{:S(2)}, u32[]{:S(2)}) %collective-permute-start.3) | collective-permute-done | bytes 8224 | tf_op jit(solution)/shard_map/ppermute | solution.py:422
  57.1 1.0 %copy-done.4 = bf16[256,1024]{1,0:T(8,128)(2,1)S(1)} copy-done((bf16[256,1024]{1,0:T(8,128)(2,1)S(1)}, bf16[256,1024]{1,0:T(8,128)(2,1)}, u32[]{:S(2)}) %copy-start.4) | copy-done | bytes 524312
  58.2 1.1 %shard_map.54.conv_ref = f32[256,1024]{1,0:T(8,128)S(1)} custom-call(s32[1]{0:T(128)} %bitcast.1.core_ref, bf16[256,1024]{1,0:T(8,128)(2,1)S(1)} %copy-done.4, bf16[16,256]{1,0:T(8,128)(2,1)S(1)} %get-tuple-element.56.near_ref, bf16[16,256]{1,0:T(8,128)(2,1)S(1)} %collective-permute-done.3.far_ref, f32[4,33]{1,0:T(4,128)S(1)} %copy-done.5), custom_call_target="tpu_custom_call" | custom-call | flops 402653184 | bytes 2097152 | tf_op jit(solution)/shard_map/pallas_call | solution.py:432
  59.3 0.2 all-to-all-done.2.mid_ref
  59.5 0.6 shard_map.55
  60.1 1.7 %collective-permute-start.4 = (bf16[256,256]{1,0:T(8,128)(2,1)S(1)}, bf16[256,256]{1,0:T(8,128)(2,1)S(1)}, u32[]{:S(2)}, u32[]{:S(2)}) collective-permute-start(bf16[256,256]{1,0:T(8,128)(2,1)S(1)} %get-tuple-element.62), channel_id=1, source_target_pairs={{0,1},{1,2},{2,3},{3,0},{4,5},{5,6},{6,7},{7,4},{8,9},{9,10},{10,1... | collective-permute-start | bytes 393224 | tf_op jit(solution)/shard_map/ppermute | solution.py:451
  61.8 2.9 %collective-permute-start.5 = (bf16[256,256]{1,0:T(8,128)(2,1)S(1)}, bf16[256,256]{1,0:T(8,128)(2,1)S(1)}, u32[]{:S(2)}, u32[]{:S(2)}) collective-permute-start(bf16[256,256]{1,0:T(8,128)(2,1)S(1)} %get-tuple-element.63), channel_id=1, source_target_pairs={{0,2},{1,3},{2,0},{3,1},{4,6},{5,7},{6,4},{7,5},{8,10},{9,11},{10,... | collective-permute-start | bytes 393224 | tf_op jit(solution)/shard_map/ppermute | solution.py:451
  64.7 1.3 %collective-permute-start.6 = (bf16[256,256]{1,0:T(8,128)(2,1)S(1)}, bf16[256,256]{1,0:T(8,128)(2,1)S(1)}, u32[]{:S(2)}, u32[]{:S(2)}) collective-permute-start(bf16[256,256]{1,0:T(8,128)(2,1)S(1)} %get-tuple-element.64), channel_id=1, source_target_pairs={{0,3},{1,0},{2,1},{3,2},{4,7},{5,4},{6,5},{7,6},{8,11},{9,8},{10,9... | collective-permute-start | bytes 393224 | tf_op jit(solution)/shard_map/ppermute | solution.py:451
  66.0 1.8 %collective-permute-done.4.refs_1_ = bf16[256,256]{1,0:T(8,128)(2,1)S(1)} collective-permute-done((bf16[256,256]{1,0:T(8,128)(2,1)S(1)}, bf16[256,256]{1,0:T(8,128)(2,1)S(1)}, u32[]{:S(2)}, u32[]{:S(2)}) %collective-permute-start.4) | collective-permute-done | bytes 131104 | tf_op jit(solution)/shard_map/ppermute | solution.py:451
  67.8 1.5 %collective-permute-done.5.refs_2_ = bf16[256,256]{1,0:T(8,128)(2,1)S(1)} collective-permute-done((bf16[256,256]{1,0:T(8,128)(2,1)S(1)}, bf16[256,256]{1,0:T(8,128)(2,1)S(1)}, u32[]{:S(2)}, u32[]{:S(2)}) %collective-permute-start.5) | collective-permute-done | bytes 131104 | tf_op jit(solution)/shard_map/ppermute | solution.py:451
  69.3 0.3 collective-permute-done.6.refs_3_
  69.6 1.5 %shard_map.56 = bf16[256,1024]{1,0:T(8,128)(2,1)} custom-call(s32[1]{0:T(128)} %bitcast.group_ref, bf16[1024,1024]{1,0:T(8,128)(2,1)S(1)} %copy-done.2, bf16[256,256]{1,0:T(8,128)(2,1)S(1)} %get-tuple-element.61.refs_0_, bf16[256,256]{1,0:T(8,128)(2,1)S(1)} %collective-permute-done.4.refs_1_, bf16[256,256]{1,0:T(8,128)(2,1)S(1)} %collective-permute-done.5.refs_2_, ...), custom_call_target="tpu_custom_call" | custom-call | flops 536870912 | bytes 3145728 | tf_op jit(solution)/shard_map/pallas_call | solution.py:452
  (11 shorter events, 0.0 us)
Async XLA Ops:
  0.0 14.6 %collective-permute-start = (bf16[1024,1024]{1,0:T(8,128)(2,1)}, bf16[1024,1024]{1,0:T(8,128)(2,1)}, u32[]{:S(2)}, u32[]{:S(2)}) collective-permute-start(bf16[1024,1024]{1,0:T(8,128)(2,1)} %tok_ref), channel_id=1, source_target_pairs={{0,4},{4,0},{8,12},{12,8},{16,20},{20,16},{24,28},{28,24},{32,36},... | collective-permute-start | bytes 6291464 | tf_op jit(solution)/shard_map/ppermute | solution.py:347
  2.9 21.4 %all-to-all-start = ((bf16[32,16,128]{2,1,0:T(8,128)(2,1)}), bf16[32,16,128]{2,1,0:T(8,128)(2,1)S(1)}, u32[]{:S(2)}, u32[]{:S(2)}) async-start(bf16[32,16,128]{2,1,0:T(8,128)(2,1)} %shard_map.46), calls=%async_computation | async-start | bytes 262144 | tf_op jit(solution)/shard_map/all_to_all | solution.py:345
  20.0 6.6 %copy-start.3 = (bf16[256,1024]{1,0:T(8,128)(2,1)}, bf16[256,1024]{1,0:T(8,128)(2,1)S(1)}, u32[]{:S(2)}) copy-start(bf16[256,1024]{1,0:T(8,128)(2,1)S(1)} %get-tuple-element.43.vt_ref) | copy-start | bytes 1572868
  26.6 5.5 %collective-permute-start.1 = (bf16[32,16,128]{2,1,0:T(8,128)(2,1)S(1)}, bf16[32,16,128]{2,1,0:T(8,128)(2,1)S(1)}, u32[]{:S(2)}, u32[]{:S(2)}) collective-permute-start(bf16[32,16,128]{2,1,0:T(8,128)(2,1)S(1)} %all-to-all-done.land_ref.own_ref), channel_id=1, source_target_pairs={{0,4},{4,0},{8,12},{12,8},{16,20},{20,16},{24,28},{28,24},{32,36},... | collective-permute-start | bytes 393224 | tf_op jit(solution)/shard_map/ppermute | solution.py:391
  26.6 15.3 %all-to-all-start.1 = ((bf16[32,16,128]{2,1,0:T(8,128)(2,1)}), bf16[32,16,128]{2,1,0:T(8,128)(2,1)S(1)}, u32[]{:S(2)}, u32[]{:S(2)}) async-start(bf16[32,16,128]{2,1,0:T(8,128)(2,1)} %shard_map.48), calls=%async_computation.1 | async-start | bytes 262144 | tf_op jit(solution)/shard_map/all_to_all | solution.py:345
  32.2 5.1 %copy-start = (bf16[1024,1024]{1,0:T(8,128)(2,1)S(1)}, bf16[1024,1024]{1,0:T(8,128)(2,1)}, u32[]{:S(2)}) copy-start(bf16[1024,1024]{1,0:T(8,128)(2,1)} %tok_ref) | copy-start | bytes 6291460
  32.2 5.1 %copy-start.1 = (bf16[3,1024,256]{2,1,0:T(8,128)(2,1)S(1)}, bf16[3,1024,256]{2,1,0:T(8,128)(2,1)}, u32[]{:S(2)}) copy-start(bf16[3,1024,256]{2,1,0:T(8,128)(2,1)} %w_ref.1) | copy-start | bytes 4718596
  38.0 19.1 %copy-start.5 = (f32[4,33]{1,0:T(4,128)S(1)}, f32[4,33]{1,0:T(4,128)}, u32[]{:S(2)}) copy-start(f32[4,33]{1,0:T(4,128)} %cw_ref.1) | copy-start | bytes 1588
  42.0 1.3 %collective-permute-start.2 = (f32[8,128]{1,0:T(8,128)S(1)}, f32[8,128]{1,0:T(8,128)S(1)}, u32[]{:S(2)}, u32[]{:S(2)}) collective-permute-start(f32[8,128]{1,0:T(8,128)S(1)} %shard_map.51.own_ref), channel_id=1, source_target_pairs={{0,4},{4,0},{8,12},{12,8},{16,20},{20,16},{24,28},{28,24},{32,36},... | collective-permute-start | bytes 12296 | tf_op jit(solution)/shard_map/ppermute | solution.py:413
  44.1 15.4 %all-to-all-start.2 = ((bf16[32,16,128]{2,1,0:T(8,128)(2,1)}), bf16[32,16,128]{2,1,0:T(8,128)(2,1)S(1)}, u32[]{:S(2)}, u32[]{:S(2)}) async-start(bf16[32,16,128]{2,1,0:T(8,128)(2,1)} %shard_map.52), calls=%async_computation.2 | async-start | bytes 262144 | tf_op jit(solution)/shard_map/all_to_all | solution.py:345
  50.0 7.1 %collective-permute-start.3 = (bf16[16,256]{1,0:T(8,128)(2,1)S(1)}, bf16[16,256]{1,0:T(8,128)(2,1)S(1)}, u32[]{:S(2)}, u32[]{:S(2)}) collective-permute-start(bf16[16,256]{1,0:T(8,128)(2,1)S(1)} %get-tuple-element.52), channel_id=1, source_target_pairs={{4,8},{12,16},{20,24},{28,32},{36,40},{44,48},{52,56},{60,64},{68,... | collective-permute-start | bytes 24584 | tf_op jit(solution)/shard_map/ppermute | solution.py:422
  57.1 1.0 %copy-start.4 = (bf16[256,1024]{1,0:T(8,128)(2,1)S(1)}, bf16[256,1024]{1,0:T(8,128)(2,1)}, u32[]{:S(2)}) copy-start(bf16[256,1024]{1,0:T(8,128)(2,1)} %copy-done.3) | copy-start | bytes 1572868
  59.5 10.1 %copy-start.2 = (bf16[1024,1024]{1,0:T(8,128)(2,1)S(1)}, bf16[1024,1024]{1,0:T(8,128)(2,1)}, u32[]{:S(2)}) copy-start(bf16[1024,1024]{1,0:T(8,128)(2,1)} %w_ref.2) | copy-start | bytes 6291460
  60.1 7.7 %collective-permute-start.4 = (bf16[256,256]{1,0:T(8,128)(2,1)S(1)}, bf16[256,256]{1,0:T(8,128)(2,1)S(1)}, u32[]{:S(2)}, u32[]{:S(2)}) collective-permute-start(bf16[256,256]{1,0:T(8,128)(2,1)S(1)} %get-tuple-element.62), channel_id=1, source_target_pairs={{0,1},{1,2},{2,3},{3,0},{4,5},{5,6},{6,7},{7,4},{8,9},{9,10},{10,1... | collective-permute-start | bytes 393224 | tf_op jit(solution)/shard_map/ppermute | solution.py:451
  61.8 7.5 %collective-permute-start.5 = (bf16[256,256]{1,0:T(8,128)(2,1)S(1)}, bf16[256,256]{1,0:T(8,128)(2,1)S(1)}, u32[]{:S(2)}, u32[]{:S(2)}) collective-permute-start(bf16[256,256]{1,0:T(8,128)(2,1)S(1)} %get-tuple-element.63), channel_id=1, source_target_pairs={{0,2},{1,3},{2,0},{3,1},{4,6},{5,7},{6,4},{7,5},{8,10},{9,11},{10,... | collective-permute-start | bytes 393224 | tf_op jit(solution)/shard_map/ppermute | solution.py:451
  64.7 5.0 %collective-permute-start.6 = (bf16[256,256]{1,0:T(8,128)(2,1)S(1)}, bf16[256,256]{1,0:T(8,128)(2,1)S(1)}, u32[]{:S(2)}, u32[]{:S(2)}) collective-permute-start(bf16[256,256]{1,0:T(8,128)(2,1)S(1)} %get-tuple-element.64), channel_id=1, source_target_pairs={{0,3},{1,0},{2,1},{3,2},{4,7},{5,4},{6,5},{7,6},{8,11},{9,8},{10,9... | collective-permute-start | bytes 393224 | tf_op jit(solution)/shard_map/ppermute | solution.py:451

commit v5 on v4

--- a/solution.py
+++ b/solution.py
@@ -95,14 +95,12 @@
             jnp.sum(tok_ref[s * seg : (s + 1) * seg, :].astype(f32), axis=0, keepdims=True)
         )
     means = jnp.concatenate(sums, axis=0) * (1.0 / seg)
-    high, middle, low = split_3(means)
-    stacked = jnp.concatenate(
-        [high.astype(f32), middle.astype(f32), low.astype(f32), jnp.zeros_like(means)], axis=0
-    ).astype(bf16)
+    high, low = split_2(means)
+    stacked = jnp.concatenate([high.astype(f32), low.astype(f32)], axis=0).astype(bf16)
     for kind in range(2):
         copies[4 + kind].wait()
         product = dot_nn(stacked, w_ref[kind])
-        land = product[0:4] + product[4:8] + product[8:12]
+        land = product[0:4] + product[4:8]
         for half in range(2):
             rows_ref[pl.ds(2 * kind + half, 4, stride=4), :] = land[:, half * 128 : half * 128 + 128]
     out_ref[...] = jnp.broadcast_to(rows_ref[...].astype(bf16)[None], out_ref.shape)
@@ -227,9 +225,12 @@
     diagonal = lax.broadcasted_iota(jnp.int32, (M, M), 0) == lax.broadcasted_iota(jnp.int32, (M, M), 1)
     ident = jnp.where(diagonal, 1.0, 0.0)
     prod = dot_wide(split_2(approx), split_2(kernel), transposed=True)
+    factor = None
     for step in range(NS_STEPS):
         parts = split_2(prod)
         square = dot_wide(parts, parts)
+        if factor is not None:
+            approx = dot_wide(split_2(factor), split_2(approx))
         last = step == NS_STEPS - 1
         right = 7.0 * ident - prod
         if not last:
@@ -238,8 +239,7 @@
         factor = 0.25 * (13.0 * ident - 15.0 * prod + both[:, :M])
         if not last:
             prod = 0.25 * (13.0 * prod - 15.0 * square + both[:, M:])
-        approx = dot_wide(split_2(factor), split_2(approx))
-    w_ref[...] = approx
+    w_ref[0], w_ref[1] = split_2(dot_wide(split_2(factor), split_2(approx)))
 
 
 def reduce_kernel(parts_ref, out_ref):
@@ -254,7 +254,7 @@
     own, other = own_ref[...], other_ref[...]
     is_first = core_ref[0] == 0
     bv = jnp.concatenate([jnp.where(is_first, own, other), jnp.where(is_first, other, own)], axis=1)
-    mid = dot_wide(split_2(bv), split_2(w_ref[...]))
+    mid = dot_wide(split_2(bv), (w_ref[0], w_ref[1]))
     rows = jnp.concatenate([mid[:, :128], mid[:, 128:]], axis=0)
     out_ref[...] = jnp.broadcast_to(rows.astype(bf16)[None], out_ref.shape)
 
@@ -391,22 +391,14 @@
     land_other = lax.ppermute(land, "ctx", swap)
     land_k, inverse = call(
         pinv_kernel,
-        [shaped((M, WIDTH), bf16), shaped((M, M), f32)],
+        [shaped((M, WIDTH), bf16), shaped((2, M, M), bf16)],
         [pltpu.VMEM((CHIPS * 32, 128), f32)],
         specs=[SMEM, SMEM, VMEM, VMEM],
         flops=24 * 3 * 2 * 256**3,
         moved=MIB // 2,
         exps=65536,
     )(core, head_id, land, land_other)
-    late_tokens, late_w, inverse = lax.optimization_barrier((tokens, w_qkv, inverse))
-    query = call(
-        query_kernel,
-        shaped((ROWS, WIDTH), bf16),
-        n_in=2,
-        flops=2 * 1024 * 1024 * 256,
-        moved=4 * MIB,
-    )(late_tokens, late_w)
-    gathered, query = lax.optimization_barrier((gathered, query))
+    gathered, inverse = lax.optimization_barrier((gathered, inverse))
     reduced = call(
         reduce_kernel, shaped((8, 128), f32), flops=32 * 8 * 128 * 2, moved=MIB // 8
     )(gathered)
@@ -418,6 +410,14 @@
         flops=6 * 8 * 256 * 256,
         moved=MIB // 2,
     )(core, reduced, reduced_other, inverse)
+    late_tokens, late_w, mid_own = lax.optimization_barrier((tokens, w_qkv, mid_own))
+    query = call(
+        query_kernel,
+        shaped((ROWS, WIDTH), bf16),
+        n_in=2,
+        flops=2 * 1024 * 1024 * 256,
+        moved=4 * MIB,
+    )(late_tokens, late_w)
     mids = exchange(mid_own)
     far = lax.ppermute(far, "ctx", onward)
     kernel_f = call(

time: 72 us -> 71.4 us (level)
    ppermute x1, waiting for transfers between devices: 1.6 us -> 0.01 us  [body(): far = lax.ppermute(far, 'ctx', onward)]
    all_to_all x3, waiting for transfers between devices: 8.39 us -> 9.44 us  [exchange(): lax.all_to_all(x, 'ctx', 0, 0, tiled=True, axis_index_groups=same_core)]
  transfers between devices with their start and end apart: 10 -> 10, of which waited for: 8 -> 6; matrix products, arithmetic and copies ran while one was open for 0% -> 0% of each run, Pallas kernels for 24% -> 24%
where the time goes in v5:
time: 71.4 us; the launch traced here: 71 us
  starting transfers between devices  32.3 us (45%)
  Pallas kernels  22.3 us (31%)
  waiting for transfers between devices  14.6 us (20%)
  local copies, waits for them, and re-layouts  1.43 us (2%)
    all_to_all x3, starting transfers between devices, exchange(): lax.all_to_all(x, 'ctx', 0, 0, tiled=True, axis_index_groups=same_core)  22.4 us
    all_to_all x3, waiting for transfers between devices, exchange(): lax.all_to_all(x, 'ctx', 0, 0, tiled=True, axis_index_groups=same_core)  9.44 us
    ppermute x3, starting transfers between devices, body(): arrived.append(lax.ppermute(head_out[step], 'head', ring))  5.9 us
    pallas_call x1, Pallas kernels, body(): call(project_kernel, [shaped((ROWS, WIDTH), bf16), shaped((WIDTH, ROWS),...  5.42 us
    pallas_call x1, Pallas kernels, body(): call(pinv_kernel, [shaped((M, WIDTH), bf16), shaped((2, M, M), bf16)], [p...  5.15 us
    ppermute x3, waiting for transfers between devices, body(): arrived.append(lax.ppermute(head_out[step], 'head', ring))  4.02 us
    ppermute x1, starting transfers between devices, body(): far = lax.ppermute(far, 'ctx', onward)  3.97 us
    pallas_call x1, Pallas kernels, body(): call(landmarks_kernel, shaped((CHIPS, 16, 128), bf16), [pltpu.VMEM((ROWS,...  2.89 us
  transfers between devices with their start and end apart: 10, of which 6 were waited for; matrix products, arithmetic and copies ran while one was open for 0% of the time, Pallas kernels for 24%

profile of v5, /device:TPU:2, one launch (start us, length us, event | category | flops | bytes accessed | tf_op | source)
XLA Modules:
  0.0 71.0 jit_solution(13881307315670086560)
XLA Ops:
  0.0 2.9 %shard_map.46 = bf16[32,16,128]{2,1,0:T(8,128)(2,1)} custom-call(bf16[1024,1024]{1,0:T(8,128)(2,1)} %tok_ref, bf16[3,1024,256]{2,1,0:T(8,128)(2,1)} %w_ref.1), custom_call_target="tpu_custom_call" | custom-call | flops 16777216 | bytes 3145728 | tf_op jit(solution)/shard_map/pallas_call | solution.py:348
  2.9 11.6 %all-to-all-start = ((bf16[32,16,128]{2,1,0:T(8,128)(2,1)}), bf16[32,16,128]{2,1,0:T(8,128)(2,1)S(1)}, u32[]{:S(2)}, u32[]{:S(2)}) async-start(bf16[32,16,128]{2,1,0:T(8,128)(2,1)} %shard_map.46), calls=%async_computation | async-start | bytes 262144 | tf_op jit(solution)/shard_map/all_to_all | solution.py:345
  14.6 5.4 %shard_map.47 = (bf16[1024,256]{1,0:T(8,128)(2,1)S(1)}, bf16[256,1024]{1,0:T(8,128)(2,1)S(1)}, bf16[1024,256]{1,0:T(8,128)(2,1)S(1)}, bf16[256,1024]{1,0:T(8,128...) custom-call(s32[1]{0:T(128)} %bitcast.1.core_ref, bf16[1024,1024]{1,0:T(8,128)(2,1)} %tok_ref, ...), custom_call_target="tpu_custom_call" | custom-call | flops 2147483648 | bytes 8388608 | tf_op jit(solution)/shard_map/pallas_call | solution.py:363
  20.0 0.0 copy-start.3
  20.0 4.3 %all-to-all-done.land_ref.own_ref = bf16[32,16,128]{2,1,0:T(8,128)(2,1)S(1)} async-done(((bf16[32,16,128]{2,1,0:T(8,128)(2,1)}), bf16[32,16,128]{2,1,0:T(8,128)(2,1)S(1)}, u32[]{:S(2)}, u32[]{:S(2)}) %all-to-all-start) | async-done | bytes 131104 | tf_op jit(solution)/shard_map/all_to_all | solution.py:345
  24.3 2.3 %shard_map.48 = bf16[32,16,128]{2,1,0:T(8,128)(2,1)} custom-call(bf16[32,16,128]{2,1,0:T(8,128)(2,1)S(1)} %all-to-all-done.land_ref.own_ref, bf16[1024,256]{1,0:T(8,128)(2,1)S(1)} %get-tuple-element.42.k_ref, bf16[256,1024]{1,0:T(8,128)(2,1)S(1)} %get-tuple-element.43.vt_ref, bf16[1024,256]{1,0:T(8,128)(2,1)S(1)} %get-tuple-element.44.k2_ref, ...), custom_call_target="tpu_custom_call" | custom-call | flops 1073741824 | bytes 4194304 | tf_op jit(solution)/shard_map/pallas_call | solution.py:380
  26.6 5.5 %all-to-all-start.1 = ((bf16[32,16,128]{2,1,0:T(8,128)(2,1)}), bf16[32,16,128]{2,1,0:T(8,128)(2,1)S(1)}, u32[]{:S(2)}, u32[]{:S(2)}) async-start(bf16[32,16,128]{2,1,0:T(8,128)(2,1)} %shard_map.48), calls=%async_computation.1 | async-start | bytes 262144 | tf_op jit(solution)/shard_map/all_to_all | solution.py:345
  32.2 0.0 copy-start
  32.2 5.1 %shard_map.49 = (bf16[256,256]{1,0:T(8,128)(2,1)S(1)}, bf16[2,256,256]{2,1,0:T(8,128)(2,1)S(1)}) custom-call(s32[1]{0:T(128)} %bitcast.1.core_ref, s32[1]{0:T(128)} %bitcast.2.head_ref, bf16[32,16,128]{2,1,0:T(8,128)(2,1)S(1)} %all-to-all-done.land_ref.own_ref, bf16[32,16,128]{2,1,0:T(8,128)(2,1)S(1)} %collective-permute-done.1.other_ref), custom_call_target="tpu_custom_call" | custom-call | flops 2415919104 | bytes 524288 | tf_op jit(solution)/shard_map/pallas_call | solution.py:392
  37.3 4.6 %all-to-all-done.1.parts_ref = bf16[32,16,128]{2,1,0:T(8,128)(2,1)S(1)} async-done(((bf16[32,16,128]{2,1,0:T(8,128)(2,1)}), bf16[32,16,128]{2,1,0:T(8,128)(2,1)S(1)}, u32[]{:S(2)}, u32[]{:S(2)}) %all-to-all-start.1) | async-done | bytes 131104 | tf_op jit(solution)/shard_map/all_to_all | solution.py:345
  41.9 0.1 shard_map.50.own_ref
  42.0 0.1 collective-permute-start.2
  42.1 1.2 %collective-permute-done.2.other_ref = f32[8,128]{1,0:T(8,128)S(1)} collective-permute-done((f32[8,128]{1,0:T(8,128)S(1)}, f32[8,128]{1,0:T(8,128)S(1)}, u32[]{:S(2)}, u32[]{:S(2)}) %collective-permute-start.2) | collective-permute-done | bytes 4128 | tf_op jit(solution)/shard_map/ppermute | solution.py:405
  43.3 0.8 %shard_map.51 = bf16[32,16,128]{2,1,0:T(8,128)(2,1)} custom-call(s32[1]{0:T(128)} %bitcast.1.core_ref, f32[8,128]{1,0:T(8,128)S(1)} %shard_map.50.own_ref, f32[8,128]{1,0:T(8,128)S(1)} %collective-permute-done.2.other_ref, bf16[2,256,256]{2,1,0:T(8,128)(2,1)S(1)} %get-tuple-element.49.w_ref), custom_call_target="tpu_custom_call" | custom-call | flops 3145728 | bytes 524288 | tf_op jit(solution)/shard_map/pallas_call | solution.py:406
  44.1 5.2 %all-to-all-start.2 = ((bf16[32,16,128]{2,1,0:T(8,128)(2,1)}), bf16[32,16,128]{2,1,0:T(8,128)(2,1)S(1)}, u32[]{:S(2)}, u32[]{:S(2)}) async-start(bf16[32,16,128]{2,1,0:T(8,128)(2,1)} %shard_map.51), calls=%async_computation.2 | async-start | bytes 262144 | tf_op jit(solution)/shard_map/all_to_all | solution.py:345
  49.3 4.0 %collective-permute-start.3 = (bf16[16,256]{1,0:T(8,128)(2,1)S(1)}, bf16[16,256]{1,0:T(8,128)(2,1)S(1)}, u32[]{:S(2)}, u32[]{:S(2)}) collective-permute-start(bf16[16,256]{1,0:T(8,128)(2,1)S(1)} %get-tuple-element.51), channel_id=1, source_target_pairs={{4,8},{12,16},{20,24},{28,32},{36,40},{44,48},{52,56},{60,64},{68,... | collective-permute-start | bytes 24584 | tf_op jit(solution)/shard_map/ppermute | solution.py:422
  53.3 0.0 copy-start.1
  53.3 1.4 %copy-done.1 = bf16[3,1024,256]{2,1,0:T(8,128)(2,1)S(1)} copy-done((bf16[3,1024,256]{2,1,0:T(8,128)(2,1)S(1)}, bf16[3,1024,256]{2,1,0:T(8,128)(2,1)}, u32[]{:S(2)}) %copy-start.1) | copy-done | bytes 1572888
  54.7 0.7 shard_map.52.q_ref
  55.4 0.0 copy-start.4
  55.5 0.0 copy-start.5
  55.5 1.7 %shard_map.53.kf_ref = bf16[4,256,1024]{2,1,0:T(8,128)(2,1)S(1)} custom-call(bf16[256,256]{1,0:T(8,128)(2,1)S(1)} %get-tuple-element.52.lk_ref, bf16[1024,256]{1,0:T(8,128)(2,1)S(1)} %shard_map.52.q_ref), custom_call_target="tpu_custom_call" | custom-call | flops 536870912 | bytes 3145728 | tf_op jit(solution)/shard_map/pallas_call | solution.py:423
  57.2 1.1 %shard_map.54.conv_ref = f32[256,1024]{1,0:T(8,128)S(1)} custom-call(s32[1]{0:T(128)} %bitcast.1.core_ref, bf16[256,1024]{1,0:T(8,128)(2,1)S(1)} %copy-done.4, bf16[16,256]{1,0:T(8,128)(2,1)S(1)} %get-tuple-element.56.near_ref, bf16[16,256]{1,0:T(8,128)(2,1)S(1)} %collective-permute-done.3.far_ref, f32[4,33]{1,0:T(4,128)S(1)} %copy-done.5), custom_call_target="tpu_custom_call" | custom-call | flops 402653184 | bytes 2097152 | tf_op jit(solution)/shard_map/pallas_call | solution.py:432
  58.3 0.6 all-to-all-done.2.mid_ref
  58.9 0.6 shard_map.55
  59.5 1.7 %collective-permute-start.4 = (bf16[256,256]{1,0:T(8,128)(2,1)S(1)}, bf16[256,256]{1,0:T(8,128)(2,1)S(1)}, u32[]{:S(2)}, u32[]{:S(2)}) collective-permute-start(bf16[256,256]{1,0:T(8,128)(2,1)S(1)} %get-tuple-element.62), channel_id=1, source_target_pairs={{0,1},{1,2},{2,3},{3,0},{4,5},{5,6},{6,7},{7,4},{8,9},{9,10},{10,1... | collective-permute-start | bytes 393224 | tf_op jit(solution)/shard_map/ppermute | solution.py:451
  61.1 2.9 %collective-permute-start.5 = (bf16[256,256]{1,0:T(8,128)(2,1)S(1)}, bf16[256,256]{1,0:T(8,128)(2,1)S(1)}, u32[]{:S(2)}, u32[]{:S(2)}) collective-permute-start(bf16[256,256]{1,0:T(8,128)(2,1)S(1)} %get-tuple-element.63), channel_id=1, source_target_pairs={{0,2},{1,3},{2,0},{3,1},{4,6},{5,7},{6,4},{7,5},{8,10},{9,11},{10,... | collective-permute-start | bytes 393224 | tf_op jit(solution)/shard_map/ppermute | solution.py:451
  64.0 1.3 %collective-permute-start.6 = (bf16[256,256]{1,0:T(8,128)(2,1)S(1)}, bf16[256,256]{1,0:T(8,128)(2,1)S(1)}, u32[]{:S(2)}, u32[]{:S(2)}) collective-permute-start(bf16[256,256]{1,0:T(8,128)(2,1)S(1)} %get-tuple-element.64), channel_id=1, source_target_pairs={{0,3},{1,0},{2,1},{3,2},{4,7},{5,4},{6,5},{7,6},{8,11},{9,8},{10,9... | collective-permute-start | bytes 393224 | tf_op jit(solution)/shard_map/ppermute | solution.py:451
  65.4 1.4 %collective-permute-done.4.refs_1_ = bf16[256,256]{1,0:T(8,128)(2,1)S(1)} collective-permute-done((bf16[256,256]{1,0:T(8,128)(2,1)S(1)}, bf16[256,256]{1,0:T(8,128)(2,1)S(1)}, u32[]{:S(2)}, u32[]{:S(2)}) %collective-permute-start.4) | collective-permute-done | bytes 131104 | tf_op jit(solution)/shard_map/ppermute | solution.py:451
  66.8 2.6 %collective-permute-done.5.refs_2_ = bf16[256,256]{1,0:T(8,128)(2,1)S(1)} collective-permute-done((bf16[256,256]{1,0:T(8,128)(2,1)S(1)}, bf16[256,256]{1,0:T(8,128)(2,1)S(1)}, u32[]{:S(2)}, u32[]{:S(2)}) %collective-permute-start.5) | collective-permute-done | bytes 131104 | tf_op jit(solution)/shard_map/ppermute | solution.py:451
  69.4 0.0 collective-permute-done.6.refs_3_
  69.4 1.5 %shard_map.56 = bf16[256,1024]{1,0:T(8,128)(2,1)} custom-call(s32[1]{0:T(128)} %bitcast.group_ref, bf16[1024,1024]{1,0:T(8,128)(2,1)S(1)} %copy-done.2, bf16[256,256]{1,0:T(8,128)(2,1)S(1)} %get-tuple-element.61.refs_0_, bf16[256,256]{1,0:T(8,128)(2,1)S(1)} %collective-permute-done.4.refs_1_, bf16[256,256]{1,0:T(8,128)(2,1)S(1)} %collective-permute-done.5.refs_2_, ...), custom_call_target="tpu_custom_call" | custom-call | flops 536870912 | bytes 3145728 | tf_op jit(solution)/shard_map/pallas_call | solution.py:452
  (11 shorter events, 0.0 us)
Async XLA Ops:
  0.0 14.6 %collective-permute-start = (bf16[1024,1024]{1,0:T(8,128)(2,1)}, bf16[1024,1024]{1,0:T(8,128)(2,1)}, u32[]{:S(2)}, u32[]{:S(2)}) collective-permute-start(bf16[1024,1024]{1,0:T(8,128)(2,1)} %tok_ref), channel_id=1, source_target_pairs={{0,4},{4,0},{8,12},{12,8},{16,20},{20,16},{24,28},{28,24},{32,36},... | collective-permute-start | bytes 6291464 | tf_op jit(solution)/shard_map/ppermute | solution.py:347
  2.9 21.4 %all-to-all-start = ((bf16[32,16,128]{2,1,0:T(8,128)(2,1)}), bf16[32,16,128]{2,1,0:T(8,128)(2,1)S(1)}, u32[]{:S(2)}, u32[]{:S(2)}) async-start(bf16[32,16,128]{2,1,0:T(8,128)(2,1)} %shard_map.46), calls=%async_computation | async-start | bytes 262144 | tf_op jit(solution)/shard_map/all_to_all | solution.py:345
  20.0 6.6 %copy-start.3 = (bf16[256,1024]{1,0:T(8,128)(2,1)}, bf16[256,1024]{1,0:T(8,128)(2,1)S(1)}, u32[]{:S(2)}) copy-start(bf16[256,1024]{1,0:T(8,128)(2,1)S(1)} %get-tuple-element.43.vt_ref) | copy-start | bytes 1572868
  26.6 5.5 %collective-permute-start.1 = (bf16[32,16,128]{2,1,0:T(8,128)(2,1)S(1)}, bf16[32,16,128]{2,1,0:T(8,128)(2,1)S(1)}, u32[]{:S(2)}, u32[]{:S(2)}) collective-permute-start(bf16[32,16,128]{2,1,0:T(8,128)(2,1)S(1)} %all-to-all-done.land_ref.own_ref), channel_id=1, source_target_pairs={{0,4},{4,0},{8,12},{12,8},{16,20},{20,16},{24,28},{28,24},{32,36},... | collective-permute-start | bytes 393224 | tf_op jit(solution)/shard_map/ppermute | solution.py:391
  26.6 15.3 %all-to-all-start.1 = ((bf16[32,16,128]{2,1,0:T(8,128)(2,1)}), bf16[32,16,128]{2,1,0:T(8,128)(2,1)S(1)}, u32[]{:S(2)}, u32[]{:S(2)}) async-start(bf16[32,16,128]{2,1,0:T(8,128)(2,1)} %shard_map.48), calls=%async_computation.1 | async-start | bytes 262144 | tf_op jit(solution)/shard_map/all_to_all | solution.py:345
  32.2 21.2 %copy-start = (bf16[1024,1024]{1,0:T(8,128)(2,1)S(1)}, bf16[1024,1024]{1,0:T(8,128)(2,1)}, u32[]{:S(2)}) copy-start(bf16[1024,1024]{1,0:T(8,128)(2,1)} %tok_ref) | copy-start | bytes 6291460
  42.0 1.3 %collective-permute-start.2 = (f32[8,128]{1,0:T(8,128)S(1)}, f32[8,128]{1,0:T(8,128)S(1)}, u32[]{:S(2)}, u32[]{:S(2)}) collective-permute-start(f32[8,128]{1,0:T(8,128)S(1)} %shard_map.50.own_ref), channel_id=1, source_target_pairs={{0,4},{4,0},{8,12},{12,8},{16,20},{20,16},{24,28},{28,24},{32,36},... | collective-permute-start | bytes 12296 | tf_op jit(solution)/shard_map/ppermute | solution.py:405
  44.1 14.8 %all-to-all-start.2 = ((bf16[32,16,128]{2,1,0:T(8,128)(2,1)}), bf16[32,16,128]{2,1,0:T(8,128)(2,1)S(1)}, u32[]{:S(2)}, u32[]{:S(2)}) async-start(bf16[32,16,128]{2,1,0:T(8,128)(2,1)} %shard_map.51), calls=%async_computation.2 | async-start | bytes 262144 | tf_op jit(solution)/shard_map/all_to_all | solution.py:345
  49.3 7.8 %collective-permute-start.3 = (bf16[16,256]{1,0:T(8,128)(2,1)S(1)}, bf16[16,256]{1,0:T(8,128)(2,1)S(1)}, u32[]{:S(2)}, u32[]{:S(2)}) collective-permute-start(bf16[16,256]{1,0:T(8,128)(2,1)S(1)} %get-tuple-element.51), channel_id=1, source_target_pairs={{4,8},{12,16},{20,24},{28,32},{36,40},{44,48},{52,56},{60,64},{68,... | collective-permute-start | bytes 24584 | tf_op jit(solution)/shard_map/ppermute | solution.py:422
  53.3 1.4 %copy-start.1 = (bf16[3,1024,256]{2,1,0:T(8,128)(2,1)S(1)}, bf16[3,1024,256]{2,1,0:T(8,128)(2,1)}, u32[]{:S(2)}) copy-start(bf16[3,1024,256]{2,1,0:T(8,128)(2,1)} %w_ref.1) | copy-start | bytes 4718596
  55.4 1.7 %copy-start.4 = (bf16[256,1024]{1,0:T(8,128)(2,1)S(1)}, bf16[256,1024]{1,0:T(8,128)(2,1)}, u32[]{:S(2)}) copy-start(bf16[256,1024]{1,0:T(8,128)(2,1)} %copy-done.3) | copy-start | bytes 1572868
  55.5 1.7 %copy-start.5 = (f32[4,33]{1,0:T(4,128)S(1)}, f32[4,33]{1,0:T(4,128)}, u32[]{:S(2)}) copy-start(f32[4,33]{1,0:T(4,128)} %cw_ref.1) | copy-start | bytes 1588
  58.9 10.5 %copy-start.2 = (bf16[1024,1024]{1,0:T(8,128)(2,1)S(1)}, bf16[1024,1024]{1,0:T(8,128)(2,1)}, u32[]{:S(2)}) copy-start(bf16[1024,1024]{1,0:T(8,128)(2,1)} %w_ref.2) | copy-start | bytes 6291460
  59.5 7.3 %collective-permute-start.4 = (bf16[256,256]{1,0:T(8,128)(2,1)S(1)}, bf16[256,256]{1,0:T(8,128)(2,1)S(1)}, u32[]{:S(2)}, u32[]{:S(2)}) collective-permute-start(bf16[256,256]{1,0:T(8,128)(2,1)S(1)} %get-tuple-element.62), channel_id=1, source_target_pairs={{0,1},{1,2},{2,3},{3,0},{4,5},{5,6},{6,7},{7,4},{8,9},{9,10},{10,1... | collective-permute-start | bytes 393224 | tf_op jit(solution)/shard_map/ppermute | solution.py:451
  61.1 8.2 %collective-permute-start.5 = (bf16[256,256]{1,0:T(8,128)(2,1)S(1)}, bf16[256,256]{1,0:T(8,128)(2,1)S(1)}, u32[]{:S(2)}, u32[]{:S(2)}) collective-permute-start(bf16[256,256]{1,0:T(8,128)(2,1)S(1)} %get-tuple-element.63), channel_id=1, source_target_pairs={{0,2},{1,3},{2,0},{3,1},{4,6},{5,7},{6,4},{7,5},{8,10},{9,11},{10,... | collective-permute-start | bytes 393224 | tf_op jit(solution)/shard_map/ppermute | solution.py:451
  64.0 5.4 %collective-permute-start.6 = (bf16[256,256]{1,0:T(8,128)(2,1)S(1)}, bf16[256,256]{1,0:T(8,128)(2,1)S(1)}, u32[]{:S(2)}, u32[]{:S(2)}) collective-permute-start(bf16[256,256]{1,0:T(8,128)(2,1)S(1)} %get-tuple-element.64), channel_id=1, source_target_pairs={{0,3},{1,0},{2,1},{3,2},{4,7},{5,4},{6,5},{7,6},{8,11},{9,8},{10,9... | collective-permute-start | bytes 393224 | tf_op jit(solution)/shard_map/ppermute | solution.py:451

commit v6 on v5

--- a/solution.py
+++ b/solution.py
@@ -246,8 +246,8 @@
     parts = parts_ref[...].astype(f32)
     level = (parts[:, 8] + parts[:, 9]) + parts[:, 10]
     weight = jnp.exp(level - jnp.max(level, axis=0, keepdims=True))
-    weight = weight / jnp.sum(weight, axis=0, keepdims=True)
-    out_ref[...] = jnp.sum(parts[:, 0:8] * weight[:, None, :], axis=0)
+    total = jnp.sum(weight, axis=0, keepdims=True)
+    out_ref[...] = jnp.sum(parts[:, 0:8] * weight[:, None, :], axis=0) / total
 
 
 def middle_kernel(core_ref, own_ref, other_ref, w_ref, out_ref):

time: 71.4 us -> 71.4 us (level)
  no operation moved by 1% of the time
where the time goes in v6:
time: 71.4 us; the launch traced here: 71 us
  starting transfers between devices  32.3 us (45%)
  Pallas kernels  22.3 us (31%)
  waiting for transfers between devices  14.6 us (20%)
  local copies, waits for them, and re-layouts  1.43 us (2%)
    all_to_all x3, starting transfers between devices, exchange(): lax.all_to_all(x, 'ctx', 0, 0, tiled=True, axis_index_groups=same_core)  22.4 us
    all_to_all x3, waiting for transfers between devices, exchange(): lax.all_to_all(x, 'ctx', 0, 0, tiled=True, axis_index_groups=same_core)  9.44 us
    ppermute x3, starting transfers between devices, body(): arrived.append(lax.ppermute(head_out[step], 'head', ring))  5.9 us
    pallas_call x1, Pallas kernels, body(): call(project_kernel, [shaped((ROWS, WIDTH), bf16), shaped((WIDTH, ROWS),...  5.42 us
    pallas_call x1, Pallas kernels, body(): call(pinv_kernel, [shaped((M, WIDTH), bf16), shaped((2, M, M), bf16)], [p...  5.15 us
    ppermute x3, waiting for transfers between devices, body(): arrived.append(lax.ppermute(head_out[step], 'head', ring))  4.02 us
    ppermute x1, starting transfers between devices, body(): far = lax.ppermute(far, 'ctx', onward)  3.97 us
    pallas_call x1, Pallas kernels, body(): call(landmarks_kernel, shaped((CHIPS, 16, 128), bf16), [pltpu.VMEM((ROWS,...  2.89 us
  transfers between devices with their start and end apart: 10, of which 6 were waited for; matrix products, arithmetic and copies ran while one was open for 0% of the time, Pallas kernels for 24%

profile of v6, /device:TPU:2, one launch (start us, length us, event | category | flops | bytes accessed | tf_op | source)
XLA Modules:
  0.0 71.0 jit_solution(16871698661536300085)
XLA Ops:
  0.0 2.9 %shard_map.46 = bf16[32,16,128]{2,1,0:T(8,128)(2,1)} custom-call(bf16[1024,1024]{1,0:T(8,128)(2,1)} %tok_ref, bf16[3,1024,256]{2,1,0:T(8,128)(2,1)} %w_ref.1), custom_call_target="tpu_custom_call" | custom-call | flops 16777216 | bytes 3145728 | tf_op jit(solution)/shard_map/pallas_call | solution.py:348
  2.9 11.6 %all-to-all-start = ((bf16[32,16,128]{2,1,0:T(8,128)(2,1)}), bf16[32,16,128]{2,1,0:T(8,128)(2,1)S(1)}, u32[]{:S(2)}, u32[]{:S(2)}) async-start(bf16[32,16,128]{2,1,0:T(8,128)(2,1)} %shard_map.46), calls=%async_computation | async-start | bytes 262144 | tf_op jit(solution)/shard_map/all_to_all | solution.py:345
  14.6 5.4 %shard_map.47 = (bf16[1024,256]{1,0:T(8,128)(2,1)S(1)}, bf16[256,1024]{1,0:T(8,128)(2,1)S(1)}, bf16[1024,256]{1,0:T(8,128)(2,1)S(1)}, bf16[256,1024]{1,0:T(8,128...) custom-call(s32[1]{0:T(128)} %bitcast.1.core_ref, bf16[1024,1024]{1,0:T(8,128)(2,1)} %tok_ref, ...), custom_call_target="tpu_custom_call" | custom-call | flops 2147483648 | bytes 8388608 | tf_op jit(solution)/shard_map/pallas_call | solution.py:363
  20.0 0.0 copy-start.3
  20.0 4.3 %all-to-all-done.land_ref.own_ref = bf16[32,16,128]{2,1,0:T(8,128)(2,1)S(1)} async-done(((bf16[32,16,128]{2,1,0:T(8,128)(2,1)}), bf16[32,16,128]{2,1,0:T(8,128)(2,1)S(1)}, u32[]{:S(2)}, u32[]{:S(2)}) %all-to-all-start) | async-done | bytes 131104 | tf_op jit(solution)/shard_map/all_to_all | solution.py:345
  24.3 2.3 %shard_map.48 = bf16[32,16,128]{2,1,0:T(8,128)(2,1)} custom-call(bf16[32,16,128]{2,1,0:T(8,128)(2,1)S(1)} %all-to-all-done.land_ref.own_ref, bf16[1024,256]{1,0:T(8,128)(2,1)S(1)} %get-tuple-element.42.k_ref, bf16[256,1024]{1,0:T(8,128)(2,1)S(1)} %get-tuple-element.43.vt_ref, bf16[1024,256]{1,0:T(8,128)(2,1)S(1)} %get-tuple-element.44.k2_ref, ...), custom_call_target="tpu_custom_call" | custom-call | flops 1073741824 | bytes 4194304 | tf_op jit(solution)/shard_map/pallas_call | solution.py:380
  26.6 5.5 %all-to-all-start.1 = ((bf16[32,16,128]{2,1,0:T(8,128)(2,1)}), bf16[32,16,128]{2,1,0:T(8,128)(2,1)S(1)}, u32[]{:S(2)}, u32[]{:S(2)}) async-start(bf16[32,16,128]{2,1,0:T(8,128)(2,1)} %shard_map.48), calls=%async_computation.1 | async-start | bytes 262144 | tf_op jit(solution)/shard_map/all_to_all | solution.py:345
  32.2 0.0 copy-start
  32.2 5.1 %shard_map.49 = (bf16[256,256]{1,0:T(8,128)(2,1)S(1)}, bf16[2,256,256]{2,1,0:T(8,128)(2,1)S(1)}) custom-call(s32[1]{0:T(128)} %bitcast.1.core_ref, s32[1]{0:T(128)} %bitcast.2.head_ref, bf16[32,16,128]{2,1,0:T(8,128)(2,1)S(1)} %all-to-all-done.land_ref.own_ref, bf16[32,16,128]{2,1,0:T(8,128)(2,1)S(1)} %collective-permute-done.1.other_ref), custom_call_target="tpu_custom_call" | custom-call | flops 2415919104 | bytes 524288 | tf_op jit(solution)/shard_map/pallas_call | solution.py:392
  37.3 4.6 %all-to-all-done.1.parts_ref = bf16[32,16,128]{2,1,0:T(8,128)(2,1)S(1)} async-done(((bf16[32,16,128]{2,1,0:T(8,128)(2,1)}), bf16[32,16,128]{2,1,0:T(8,128)(2,1)S(1)}, u32[]{:S(2)}, u32[]{:S(2)}) %all-to-all-start.1) | async-done | bytes 131104 | tf_op jit(solution)/shard_map/all_to_all | solution.py:345
  41.9 0.1 shard_map.50.own_ref
  42.0 0.1 collective-permute-start.2
  42.1 1.2 %collective-permute-done.2.other_ref = f32[8,128]{1,0:T(8,128)S(1)} collective-permute-done((f32[8,128]{1,0:T(8,128)S(1)}, f32[8,128]{1,0:T(8,128)S(1)}, u32[]{:S(2)}, u32[]{:S(2)}) %collective-permute-start.2) | collective-permute-done | bytes 4128 | tf_op jit(solution)/shard_map/ppermute | solution.py:405
  43.2 0.8 %shard_map.51 = bf16[32,16,128]{2,1,0:T(8,128)(2,1)} custom-call(s32[1]{0:T(128)} %bitcast.1.core_ref, f32[8,128]{1,0:T(8,128)S(1)} %shard_map.50.own_ref, f32[8,128]{1,0:T(8,128)S(1)} %collective-permute-done.2.other_ref, bf16[2,256,256]{2,1,0:T(8,128)(2,1)S(1)} %get-tuple-element.49.w_ref), custom_call_target="tpu_custom_call" | custom-call | flops 3145728 | bytes 524288 | tf_op jit(solution)/shard_map/pallas_call | solution.py:406
  44.1 5.2 %all-to-all-start.2 = ((bf16[32,16,128]{2,1,0:T(8,128)(2,1)}), bf16[32,16,128]{2,1,0:T(8,128)(2,1)S(1)}, u32[]{:S(2)}, u32[]{:S(2)}) async-start(bf16[32,16,128]{2,1,0:T(8,128)(2,1)} %shard_map.51), calls=%async_computation.2 | async-start | bytes 262144 | tf_op jit(solution)/shard_map/all_to_all | solution.py:345
  49.3 4.0 %collective-permute-start.3 = (bf16[16,256]{1,0:T(8,128)(2,1)S(1)}, bf16[16,256]{1,0:T(8,128)(2,1)S(1)}, u32[]{:S(2)}, u32[]{:S(2)}) collective-permute-start(bf16[16,256]{1,0:T(8,128)(2,1)S(1)} %get-tuple-element.51), channel_id=1, source_target_pairs={{4,8},{12,16},{20,24},{28,32},{36,40},{44,48},{52,56},{60,64},{68,... | collective-permute-start | bytes 24584 | tf_op jit(solution)/shard_map/ppermute | solution.py:422
  53.3 0.0 copy-start.1
  53.3 1.4 %copy-done.1 = bf16[3,1024,256]{2,1,0:T(8,128)(2,1)S(1)} copy-done((bf16[3,1024,256]{2,1,0:T(8,128)(2,1)S(1)}, bf16[3,1024,256]{2,1,0:T(8,128)(2,1)}, u32[]{:S(2)}) %copy-start.1) | copy-done | bytes 1572888
  54.7 0.7 shard_map.52.q_ref
  55.4 0.0 copy-start.4
  55.4 0.0 copy-start.5
  55.4 1.7 %shard_map.53.kf_ref = bf16[4,256,1024]{2,1,0:T(8,128)(2,1)S(1)} custom-call(bf16[256,256]{1,0:T(8,128)(2,1)S(1)} %get-tuple-element.52.lk_ref, bf16[1024,256]{1,0:T(8,128)(2,1)S(1)} %shard_map.52.q_ref), custom_call_target="tpu_custom_call" | custom-call | flops 536870912 | bytes 3145728 | tf_op jit(solution)/shard_map/pallas_call | solution.py:423
  57.2 1.1 %shard_map.54.conv_ref = f32[256,1024]{1,0:T(8,128)S(1)} custom-call(s32[1]{0:T(128)} %bitcast.1.core_ref, bf16[256,1024]{1,0:T(8,128)(2,1)S(1)} %copy-done.4, bf16[16,256]{1,0:T(8,128)(2,1)S(1)} %get-tuple-element.56.near_ref, bf16[16,256]{1,0:T(8,128)(2,1)S(1)} %collective-permute-done.3.far_ref, f32[4,33]{1,0:T(4,128)S(1)} %copy-done.5), custom_call_target="tpu_custom_call" | custom-call | flops 402653184 | bytes 2097152 | tf_op jit(solution)/shard_map/pallas_call | solution.py:432
  58.3 0.6 all-to-all-done.2.mid_ref
  58.8 0.6 shard_map.55
  59.5 1.7 %collective-permute-start.4 = (bf16[256,256]{1,0:T(8,128)(2,1)S(1)}, bf16[256,256]{1,0:T(8,128)(2,1)S(1)}, u32[]{:S(2)}, u32[]{:S(2)}) collective-permute-start(bf16[256,256]{1,0:T(8,128)(2,1)S(1)} %get-tuple-element.62), channel_id=1, source_target_pairs={{0,1},{1,2},{2,3},{3,0},{4,5},{5,6},{6,7},{7,4},{8,9},{9,10},{10,1... | collective-permute-start | bytes 393224 | tf_op jit(solution)/shard_map/ppermute | solution.py:451
  61.1 2.9 %collective-permute-start.5 = (bf16[256,256]{1,0:T(8,128)(2,1)S(1)}, bf16[256,256]{1,0:T(8,128)(2,1)S(1)}, u32[]{:S(2)}, u32[]{:S(2)}) collective-permute-start(bf16[256,256]{1,0:T(8,128)(2,1)S(1)} %get-tuple-element.63), channel_id=1, source_target_pairs={{0,2},{1,3},{2,0},{3,1},{4,6},{5,7},{6,4},{7,5},{8,10},{9,11},{10,... | collective-permute-start | bytes 393224 | tf_op jit(solution)/shard_map/ppermute | solution.py:451
  64.0 1.3 %collective-permute-start.6 = (bf16[256,256]{1,0:T(8,128)(2,1)S(1)}, bf16[256,256]{1,0:T(8,128)(2,1)S(1)}, u32[]{:S(2)}, u32[]{:S(2)}) collective-permute-start(bf16[256,256]{1,0:T(8,128)(2,1)S(1)} %get-tuple-element.64), channel_id=1, source_target_pairs={{0,3},{1,0},{2,1},{3,2},{4,7},{5,4},{6,5},{7,6},{8,11},{9,8},{10,9... | collective-permute-start | bytes 393224 | tf_op jit(solution)/shard_map/ppermute | solution.py:451
  65.4 1.4 %collective-permute-done.4.refs_1_ = bf16[256,256]{1,0:T(8,128)(2,1)S(1)} collective-permute-done((bf16[256,256]{1,0:T(8,128)(2,1)S(1)}, bf16[256,256]{1,0:T(8,128)(2,1)S(1)}, u32[]{:S(2)}, u32[]{:S(2)}) %collective-permute-start.4) | collective-permute-done | bytes 131104 | tf_op jit(solution)/shard_map/ppermute | solution.py:451
  66.8 2.5 %collective-permute-done.5.refs_2_ = bf16[256,256]{1,0:T(8,128)(2,1)S(1)} collective-permute-done((bf16[256,256]{1,0:T(8,128)(2,1)S(1)}, bf16[256,256]{1,0:T(8,128)(2,1)S(1)}, u32[]{:S(2)}, u32[]{:S(2)}) %collective-permute-start.5) | collective-permute-done | bytes 131104 | tf_op jit(solution)/shard_map/ppermute | solution.py:451
  69.3 0.0 collective-permute-done.6.refs_3_
  69.4 1.5 %shard_map.56 = bf16[256,1024]{1,0:T(8,128)(2,1)} custom-call(s32[1]{0:T(128)} %bitcast.group_ref, bf16[1024,1024]{1,0:T(8,128)(2,1)S(1)} %copy-done.2, bf16[256,256]{1,0:T(8,128)(2,1)S(1)} %get-tuple-element.61.refs_0_, bf16[256,256]{1,0:T(8,128)(2,1)S(1)} %collective-permute-done.4.refs_1_, bf16[256,256]{1,0:T(8,128)(2,1)S(1)} %collective-permute-done.5.refs_2_, ...), custom_call_target="tpu_custom_call" | custom-call | flops 536870912 | bytes 3145728 | tf_op jit(solution)/shard_map/pallas_call | solution.py:452
  (11 shorter events, 0.0 us)
Async XLA Ops:
  0.0 14.6 %collective-permute-start = (bf16[1024,1024]{1,0:T(8,128)(2,1)}, bf16[1024,1024]{1,0:T(8,128)(2,1)}, u32[]{:S(2)}, u32[]{:S(2)}) collective-permute-start(bf16[1024,1024]{1,0:T(8,128)(2,1)} %tok_ref), channel_id=1, source_target_pairs={{0,4},{4,0},{8,12},{12,8},{16,20},{20,16},{24,28},{28,24},{32,36},... | collective-permute-start | bytes 6291464 | tf_op jit(solution)/shard_map/ppermute | solution.py:347
  2.9 21.4 %all-to-all-start = ((bf16[32,16,128]{2,1,0:T(8,128)(2,1)}), bf16[32,16,128]{2,1,0:T(8,128)(2,1)S(1)}, u32[]{:S(2)}, u32[]{:S(2)}) async-start(bf16[32,16,128]{2,1,0:T(8,128)(2,1)} %shard_map.46), calls=%async_computation | async-start | bytes 262144 | tf_op jit(solution)/shard_map/all_to_all | solution.py:345
  20.0 6.6 %copy-start.3 = (bf16[256,1024]{1,0:T(8,128)(2,1)}, bf16[256,1024]{1,0:T(8,128)(2,1)S(1)}, u32[]{:S(2)}) copy-start(bf16[256,1024]{1,0:T(8,128)(2,1)S(1)} %get-tuple-element.43.vt_ref) | copy-start | bytes 1572868
  26.6 5.5 %collective-permute-start.1 = (bf16[32,16,128]{2,1,0:T(8,128)(2,1)S(1)}, bf16[32,16,128]{2,1,0:T(8,128)(2,1)S(1)}, u32[]{:S(2)}, u32[]{:S(2)}) collective-permute-start(bf16[32,16,128]{2,1,0:T(8,128)(2,1)S(1)} %all-to-all-done.land_ref.own_ref), channel_id=1, source_target_pairs={{0,4},{4,0},{8,12},{12,8},{16,20},{20,16},{24,28},{28,24},{32,36},... | collective-permute-start | bytes 393224 | tf_op jit(solution)/shard_map/ppermute | solution.py:391
  26.6 15.3 %all-to-all-start.1 = ((bf16[32,16,128]{2,1,0:T(8,128)(2,1)}), bf16[32,16,128]{2,1,0:T(8,128)(2,1)S(1)}, u32[]{:S(2)}, u32[]{:S(2)}) async-start(bf16[32,16,128]{2,1,0:T(8,128)(2,1)} %shard_map.48), calls=%async_computation.1 | async-start | bytes 262144 | tf_op jit(solution)/shard_map/all_to_all | solution.py:345
  32.2 21.1 %copy-start = (bf16[1024,1024]{1,0:T(8,128)(2,1)S(1)}, bf16[1024,1024]{1,0:T(8,128)(2,1)}, u32[]{:S(2)}) copy-start(bf16[1024,1024]{1,0:T(8,128)(2,1)} %tok_ref) | copy-start | bytes 6291460
  42.0 1.2 %collective-permute-start.2 = (f32[8,128]{1,0:T(8,128)S(1)}, f32[8,128]{1,0:T(8,128)S(1)}, u32[]{:S(2)}, u32[]{:S(2)}) collective-permute-start(f32[8,128]{1,0:T(8,128)S(1)} %shard_map.50.own_ref), channel_id=1, source_target_pairs={{0,4},{4,0},{8,12},{12,8},{16,20},{20,16},{24,28},{28,24},{32,36},... | collective-permute-start | bytes 12296 | tf_op jit(solution)/shard_map/ppermute | solution.py:405
  44.1 14.8 %all-to-all-start.2 = ((bf16[32,16,128]{2,1,0:T(8,128)(2,1)}), bf16[32,16,128]{2,1,0:T(8,128)(2,1)S(1)}, u32[]{:S(2)}, u32[]{:S(2)}) async-start(bf16[32,16,128]{2,1,0:T(8,128)(2,1)} %shard_map.51), calls=%async_computation.2 | async-start | bytes 262144 | tf_op jit(solution)/shard_map/all_to_all | solution.py:345
  49.3 7.8 %collective-permute-start.3 = (bf16[16,256]{1,0:T(8,128)(2,1)S(1)}, bf16[16,256]{1,0:T(8,128)(2,1)S(1)}, u32[]{:S(2)}, u32[]{:S(2)}) collective-permute-start(bf16[16,256]{1,0:T(8,128)(2,1)S(1)} %get-tuple-element.51), channel_id=1, source_target_pairs={{4,8},{12,16},{20,24},{28,32},{36,40},{44,48},{52,56},{60,64},{68,... | collective-permute-start | bytes 24584 | tf_op jit(solution)/shard_map/ppermute | solution.py:422
  53.3 1.4 %copy-start.1 = (bf16[3,1024,256]{2,1,0:T(8,128)(2,1)S(1)}, bf16[3,1024,256]{2,1,0:T(8,128)(2,1)}, u32[]{:S(2)}) copy-start(bf16[3,1024,256]{2,1,0:T(8,128)(2,1)} %w_ref.1) | copy-start | bytes 4718596
  55.4 1.7 %copy-start.4 = (bf16[256,1024]{1,0:T(8,128)(2,1)S(1)}, bf16[256,1024]{1,0:T(8,128)(2,1)}, u32[]{:S(2)}) copy-start(bf16[256,1024]{1,0:T(8,128)(2,1)} %copy-done.3) | copy-start | bytes 1572868
  55.4 1.7 %copy-start.5 = (f32[4,33]{1,0:T(4,128)S(1)}, f32[4,33]{1,0:T(4,128)}, u32[]{:S(2)}) copy-start(f32[4,33]{1,0:T(4,128)} %cw_ref.1) | copy-start | bytes 1588
  58.8 10.5 %copy-start.2 = (bf16[1024,1024]{1,0:T(8,128)(2,1)S(1)}, bf16[1024,1024]{1,0:T(8,128)(2,1)}, u32[]{:S(2)}) copy-start(bf16[1024,1024]{1,0:T(8,128)(2,1)} %w_ref.2) | copy-start | bytes 6291460
  59.5 7.3 %collective-permute-start.4 = (bf16[256,256]{1,0:T(8,128)(2,1)S(1)}, bf16[256,256]{1,0:T(8,128)(2,1)S(1)}, u32[]{:S(2)}, u32[]{:S(2)}) collective-permute-start(bf16[256,256]{1,0:T(8,128)(2,1)S(1)} %get-tuple-element.62), channel_id=1, source_target_pairs={{0,1},{1,2},{2,3},{3,0},{4,5},{5,6},{6,7},{7,4},{8,9},{9,10},{10,1... | collective-permute-start | bytes 393224 | tf_op jit(solution)/shard_map/ppermute | solution.py:451
  61.1 8.2 %collective-permute-start.5 = (bf16[256,256]{1,0:T(8,128)(2,1)S(1)}, bf16[256,256]{1,0:T(8,128)(2,1)S(1)}, u32[]{:S(2)}, u32[]{:S(2)}) collective-permute-start(bf16[256,256]{1,0:T(8,128)(2,1)S(1)} %get-tuple-element.63), channel_id=1, source_target_pairs={{0,2},{1,3},{2,0},{3,1},{4,6},{5,7},{6,4},{7,5},{8,10},{9,11},{10,... | collective-permute-start | bytes 393224 | tf_op jit(solution)/shard_map/ppermute | solution.py:451
  64.0 5.4 %collective-permute-start.6 = (bf16[256,256]{1,0:T(8,128)(2,1)S(1)}, bf16[256,256]{1,0:T(8,128)(2,1)S(1)}, u32[]{:S(2)}, u32[]{:S(2)}) collective-permute-start(bf16[256,256]{1,0:T(8,128)(2,1)S(1)} %get-tuple-element.64), channel_id=1, source_target_pairs={{0,3},{1,0},{2,1},{3,2},{4,7},{5,4},{6,5},{7,6},{8,11},{9,8},{10,9... | collective-permute-start | bytes 393224 | tf_op jit(solution)/shard_map/ppermute | solution.py:451
